TPU v7x, 32 devices: a whole 2x2x4 slice. The times are simulated.
32 devices in a mesh: dp: 8 (over y, x, core), hist: 4 (over z).
Axes of the slice: x: 2, y: 2, z: 4, core: 2. Of those that a mesh axis runs over, the one named last changes fastest.
Arguments:
- history: bfloat16 [16, 24, 256, 2048], P('hist', 'dp'), may hold values from -6 to 6
- history_layer_index: int32 [16], replicated, may hold values from 0 to 15, each once
- lengths: int32 [24], P('dp'), may hold values from 32 to 256, as said below
- norm_gains: bfloat16 [5, 2048], P(None, 'dp'), may hold values from 0.099609375 to 1.8984375
- mix_in: bfloat16 [2048, 64], P('dp'), may hold values from -0.125 to 0.125
- mix_out: bfloat16 [64, 64], P('dp'), may hold values from -0.25 to 0.25
- w_attn: bfloat16 [3, 2048, 2048], P(None, 'dp'), may hold values from -0.125 to 0.125
- w_out: bfloat16 [2048, 2048], P('dp'), may hold values from -1 to 1
- w_up: bfloat16 [2048, 8192], P('dp'), may hold values from -0.125 to 0.125
- w_down: bfloat16 [8192, 2048], P('dp'), may hold values from -0.0625 to 0.0625
- cotangent: bfloat16 [24, 256, 2048], P('dp', 'hist'), may hold values from -6 to 6
Outputs:
- block_out: bfloat16 [24, 256, 2048], P('dp', 'hist')
- history_grad: bfloat16 [16, 24, 256, 2048], P('hist', 'dp')
- norm_gains_grad: float32 [5, 2048], P(None, 'dp')
- mix_in_grad: float32 [2048, 64], P('dp')
- mix_out_grad: float32 [64, 64], P('dp')
- w_attn_grad: float32 [3, 2048, 2048], P(None, 'dp')
- w_out_grad: float32 [2048, 2048], P('dp')
- w_up_grad: float32 [2048, 8192], P('dp')
- w_down_grad: float32 [8192, 2048], P('dp')
Inputs may be any that keep to these rules, and one draw needn't show every extreme that they name: Slot s holds the output of layer history_layer_index[s]; each layer once. `lengths`: positions at or past a sequence's length are padding; some sequence has the full 256 tokens and some has 32.
All inputs are finite; a program needn't handle non-finite values.
Results may differ from a plain program's by a relative error of at most 0.018.
Values may be sent and summed in bfloat16 or wider, within the bound.
A program may use at most 704 MiB of HBM per device.

v0:
```python
import math

import jax
import jax.numpy as jnp
from jax import lax
from jax.sharding import PartitionSpec as P

MODEL_WIDTH = 2048
HEADS = 16
HEAD_DIM = 128
FF = 8192
STREAM_COUNT = 4


epsilon = 1e-06
masked_out = -1e30
highest = lax.Precision.HIGHEST
contract_rows = (((0,), (0,)), ((), ()))
contract_cols = (((1,), (1,)), ((), ()))


def broadcast(value, axis, source):
    kept = jnp.where(lax.axis_index(axis) == source, value, 0).astype(value.dtype)
    return lax.psum(kept, axis)


def matmul(left_side, right_side):
    return jnp.dot(left_side, right_side, preferred_element_type=jnp.float32)


def precise(left_side, right_side):
    return jnp.dot(left_side, right_side, precision=highest, preferred_element_type=jnp.float32)


def gelu_slope(values):
    return 0.5 * (1.0 + lax.erf(values * (1.0 / math.sqrt(2.0)))) + values * jnp.exp(
        -0.5 * values * values
    ) * (1.0 / math.sqrt(2.0 * math.pi))


def rms_scale(values, gain_row):
    inverse = lax.rsqrt(jnp.mean(values * values, axis=-1, keepdims=True) + epsilon)
    return (values * inverse * gain_row, inverse)


def rms_back(values, inverse, gain_row, grad_in):
    scaled = grad_in * gain_row
    gain_grad = jnp.sum(grad_in * values * inverse, axis=0)
    inner_mean = jnp.mean(scaled * values, axis=-1, keepdims=True)
    return (inverse * scaled - values * (inverse * inverse * inverse) * inner_mean, gain_grad)


def rotate(values, positions, turn_sign):
    half_dim = values.shape[-1] // 2
    frequency = jnp.exp(
        jnp.arange(half_dim, dtype=jnp.float32) * (-2.0 * math.log(10000.0) / values.shape[-1])
    )
    angles = positions.astype(jnp.float32)[:, None] * frequency[None, :]
    cosine = jnp.cos(angles)[:, None, :]
    sine_part = jnp.sin(angles)[:, None, :] * turn_sign
    lower_half = values[..., :half_dim]
    upper_half = values[..., half_dim:]
    return jnp.concatenate(
        [
            lower_half * cosine - upper_half * sine_part,
            upper_half * cosine + lower_half * sine_part,
        ],
        axis=-1,
    )


def first_rows(weights, lefts):

    def add_piece(totals, pieces, start_at):
        return tuple(
            (matmul(left_side, piece_rows) for left_side, piece_rows in zip(lefts, pieces))
        )

    initial = tuple(
        (jnp.zeros((lefts[0].shape[0], weight.shape[1]), jnp.float32) for weight in weights)
    )
    return add_piece(
        initial,
        (
            lax.all_gather(weights[0], "dp", axis=0, tiled=True),
            lax.all_gather(weights[1], "dp", axis=0, tiled=True),
            lax.all_gather(weights[2], "dp", axis=0, tiled=True),
            lax.all_gather(weights[3], "dp", axis=0, tiled=True),
        ),
        jnp.int32(0),
    )


def second_rows(w_out, down_folded, attended_low, hidden, ratio):

    def add_piece(total_sum, pieces, start_at):
        count = pieces[0].shape[0]
        down_rows = pieces[1].reshape(count * ratio, pieces[1].shape[1] // ratio)
        return matmul(attended_low, pieces[0]) + matmul(hidden, down_rows)

    initial = jnp.zeros((attended_low.shape[0], w_out.shape[1]), jnp.float32)
    return add_piece(
        initial,
        (
            lax.all_gather(w_out, "dp", axis=0, tiled=True),
            lax.all_gather(down_folded, "dp", axis=0, tiled=True),
        ),
        jnp.int32(0),
    )


def back_first(w_out, down_folded, grad_low, ratio):

    def add_piece(totals, pieces, start_at):
        count = pieces[0].shape[0]
        out_part = lax.dot_general(
            grad_low, pieces[0], contract_cols, preferred_element_type=jnp.float32
        )
        down_rows = pieces[1].reshape(count * ratio, pieces[1].shape[1] // ratio)
        down_part = lax.dot_general(
            grad_low, down_rows, contract_cols, preferred_element_type=jnp.float32
        )
        return (out_part, down_part)

    features = w_out.shape[1]
    initial = (
        jnp.zeros((grad_low.shape[0], features), jnp.float32),
        jnp.zeros((grad_low.shape[0], features * ratio), jnp.float32),
    )
    return add_piece(
        initial,
        (
            lax.all_gather(w_out, "dp", axis=0, tiled=True),
            lax.all_gather(down_folded, "dp", axis=0, tiled=True),
        ),
        jnp.int32(0),
    )


def back_second(weights, rights):

    def add_piece(totals, pieces, start_at):
        return tuple(
            (
                lax.dot_general(
                    right_side, piece_rows, contract_cols, preferred_element_type=jnp.float32
                )
                for right_side, piece_rows in zip(rights, pieces)
            )
        )

    features = weights[1].shape[1]
    initial = tuple((jnp.zeros((rights[0].shape[0], features), jnp.float32) for weight in weights))
    return add_piece(
        initial,
        (
            lax.all_gather(weights[0], "dp", axis=0, tiled=True),
            lax.all_gather(weights[1], "dp", axis=0, tiled=True),
            lax.all_gather(weights[2], "dp", axis=0, tiled=True),
            lax.all_gather(weights[3], "dp", axis=0, tiled=True),
        ),
        jnp.int32(0),
    )


def mix_forward(values_low, gain_row, mix_in_all, mixer_output_wide):
    values = values_low.astype(jnp.float32)
    scaled, inverse = rms_scale(values, gain_row)
    normed_mix = scaled.astype(jnp.bfloat16)
    mixer_preactivation = matmul(normed_mix, mix_in_all)
    mix_act = jax.nn.gelu(mixer_preactivation, approximate=False)
    return (
        precise(mix_act, mixer_output_wide),
        (values, inverse, normed_mix, mixer_preactivation, mix_act),
    )


def mix_backward(kept_mix, act_grad, gain_row, mix_in_all):
    values, inverse, normed_mix, mixer_preactivation, mix_act = kept_mix
    pre_grad = act_grad * gelu_slope(mixer_preactivation)
    in_grad = precise(normed_mix.astype(jnp.float32).T, pre_grad)
    normed_grad = precise(pre_grad, mix_in_all.astype(jnp.float32).T)
    latest_grad, gain_grad = rms_back(values, inverse, gain_row, normed_grad)
    return (latest_grad, gain_grad, in_grad)


def shards(
    history,
    history_layer_index,
    lengths,
    norm_gains,
    mix_in,
    mix_out,
    w_attn,
    w_out,
    w_up,
    w_down,
    cotangent,
):
    local_slots, micro_count, sequence_length, features = history.shape
    hist_count = lax.axis_size("hist")
    dp_count = lax.axis_size("dp")
    hist_place = lax.axis_index("hist")
    slot_count = local_slots * hist_count
    ratio = FF // MODEL_WIDTH
    gains_all, mix_in_all, mix_out_all = (
        lax.all_gather(norm_gains, "dp", axis=1, tiled=True),
        lax.all_gather(mix_in, "dp", axis=0, tiled=True),
        lax.all_gather(mix_out, "dp", axis=0, tiled=True),
    )
    gains_all = gains_all.astype(jnp.float32)
    mixer_output_wide = mix_out_all.astype(jnp.float32)
    mix_width = mixer_output_wide.shape[0]
    layer_lookup = (
        history_layer_index[:, None] == jnp.arange(slot_count, dtype=jnp.int32)[None, :]
    ).astype(jnp.float32)
    newest_output = jnp.sum(
        jnp.arange(slot_count, dtype=jnp.int32)
        * (history_layer_index == slot_count - 1).astype(jnp.int32)
    )
    down_folded = w_down.reshape(w_down.shape[0] // ratio, ratio * w_down.shape[1])
    quarter = cotangent.shape[1]
    own_rows = micro_count * quarter
    positions = hist_place * quarter + jnp.arange(quarter, dtype=jnp.int32)
    valid_rows = (positions[None, :] < lengths[:, None]).astype(jnp.float32).reshape(own_rows, 1)
    root = newest_output // local_slots
    latest_local = lax.dynamic_index_in_dim(history, newest_output % local_slots, 0, keepdims=False)
    latest_rows = broadcast(latest_local, "hist", root)
    dynamic_weights, kept_mix = mix_forward(
        latest_rows.reshape(micro_count * sequence_length, features),
        gains_all[0],
        mix_in_all,
        mixer_output_wide,
    )
    dynamic_weights = dynamic_weights.reshape(
        micro_count, sequence_length, STREAM_COUNT, slot_count
    )
    own_table = lax.dynamic_slice_in_dim(layer_lookup, hist_place * local_slots, local_slots, 0)
    depth_combination_factors = jnp.einsum(
        "mtcj,sj->scmt", dynamic_weights, own_table, precision=highest
    )
    partial_sums = jnp.zeros((STREAM_COUNT, micro_count, sequence_length, features), jnp.float32)
    for depth_position_number in range(local_slots):
        partial_sums = (
            partial_sums
            + depth_combination_factors[depth_position_number][..., None]
            * history[depth_position_number].astype(jnp.float32)[None]
        )
    blended_residual_inputs = lax.psum_scatter(
        partial_sums, "hist", scatter_dimension=2, tiled=True
    )
    stream_rows = blended_residual_inputs.reshape(STREAM_COUNT, own_rows, features)
    normed = []
    inverses = []
    for stream_idx in range(STREAM_COUNT):
        scaled, inverse = rms_scale(stream_rows[stream_idx], gains_all[stream_idx + 1])
        normed.append(scaled.astype(jnp.bfloat16))
        inverses.append(inverse)
    head_shape = (micro_count, quarter, HEADS, HEAD_DIM)
    query_pre, key_pre, value_pre, up_pre = first_rows(
        (w_attn[0], w_attn[1], w_attn[2], w_up), (normed[0], normed[1], normed[2], normed[3])
    )
    attention_asker_vectors = rotate(query_pre.reshape(head_shape), positions, 1.0).astype(
        jnp.bfloat16
    )
    keys_rot = rotate(key_pre.reshape(head_shape), positions, 1.0).astype(jnp.bfloat16)
    values_low = value_pre.astype(jnp.bfloat16)
    keys_all, values_all = (
        lax.all_gather(
            keys_rot.reshape(micro_count, quarter, features), "hist", axis=1, tiled=True
        ),
        lax.all_gather(
            values_low.reshape(micro_count, quarter, features), "hist", axis=1, tiled=True
        ),
    )
    key_heads = keys_all.reshape(micro_count, sequence_length, HEADS, HEAD_DIM)
    value_wide = values_all.reshape(micro_count, sequence_length, HEADS, HEAD_DIM).astype(
        jnp.float32
    )
    score_scale = 1.0 / math.sqrt(HEAD_DIM)
    scores = (
        jnp.einsum(
            "mqhd,mkhd->mhqk",
            attention_asker_vectors,
            key_heads,
            preferred_element_type=jnp.float32,
        )
        * score_scale
    )
    key_positions = jnp.arange(sequence_length, dtype=jnp.int32)
    allowed = (key_positions[None, None, :] <= positions[None, :, None]) & (
        key_positions[None, None, :] < lengths[:, None, None]
    )
    scores = jnp.where(allowed[:, None], scores, masked_out)
    row_top = jnp.max(scores, axis=-1, keepdims=True)
    raised = jnp.exp(scores - row_top)
    soft_weights = raised / jnp.sum(raised, axis=-1, keepdims=True)
    attended = jnp.einsum("mhqk,mkhd->mqhd", soft_weights, value_wide, precision=highest)
    attended_low = attended.reshape(own_rows, features).astype(jnp.bfloat16)
    hidden = jax.nn.gelu(up_pre, approximate=False).astype(jnp.bfloat16)
    branch = second_rows(w_out, down_folded, attended_low, hidden, ratio)
    block_out = (
        ((stream_rows[3] + branch) * valid_rows)
        .astype(jnp.bfloat16)
        .reshape(micro_count, quarter, features)
    )
    grad_rows = cotangent.reshape(own_rows, features).astype(jnp.float32) * valid_rows
    grad_low = grad_rows.astype(jnp.bfloat16)
    attended_back, hidden_grad = back_first(w_out, down_folded, grad_low, ratio)
    up_grad = (hidden_grad * gelu_slope(up_pre)).astype(jnp.bfloat16)
    attended_grad = attended_back.astype(jnp.bfloat16)
    attended_wide = attended_grad.astype(jnp.float32).reshape(head_shape)
    prob_grad = jnp.einsum("mqhd,mkhd->mhqk", attended_wide, value_wide, precision=highest)
    inner_rows = jnp.sum(attended_wide * attended, axis=-1)
    logit_derivative = (
        soft_weights * (prob_grad - jnp.transpose(inner_rows, (0, 2, 1))[..., None]) * score_scale
    )
    query_grad = jnp.einsum(
        "mhqk,mkhd->mqhd", logit_derivative, key_heads.astype(jnp.float32), precision=highest
    )
    key_grad_all = jnp.einsum(
        "mhqk,mqhd->mkhd",
        logit_derivative,
        attention_asker_vectors.astype(jnp.float32),
        precision=highest,
    )
    value_grad_all = jnp.einsum("mhqk,mqhd->mkhd", soft_weights, attended_wide, precision=highest)
    key_grad, value_grad = (
        lax.psum_scatter(
            key_grad_all.reshape(micro_count, sequence_length, features).astype(jnp.bfloat16),
            "hist",
            scatter_dimension=1,
            tiled=True,
        ).astype(jnp.float32),
        lax.psum_scatter(
            value_grad_all.reshape(micro_count, sequence_length, features).astype(jnp.bfloat16),
            "hist",
            scatter_dimension=1,
            tiled=True,
        ).astype(jnp.float32),
    )
    projection_grads = [
        rotate(query_grad, positions, -1.0).reshape(own_rows, features).astype(jnp.bfloat16),
        rotate(key_grad.reshape(head_shape), positions, -1.0)
        .reshape(own_rows, features)
        .astype(jnp.bfloat16),
        value_grad.reshape(own_rows, features).astype(jnp.bfloat16),
    ]
    resid_normed_grad, query_normed_grad, key_normed_grad, value_normed_grad = back_second(
        (w_up, w_attn[0], w_attn[1], w_attn[2]),
        (up_grad, projection_grads[0], projection_grads[1], projection_grads[2]),
    )
    normed_grads = [query_normed_grad, key_normed_grad, value_normed_grad]
    stream_grads = []
    gain_grads = []
    for stream_idx in range(3):
        stream_grad, gain_grad = rms_back(
            stream_rows[stream_idx],
            inverses[stream_idx],
            gains_all[stream_idx + 1],
            normed_grads[stream_idx],
        )
        stream_grads.append(stream_grad)
        gain_grads.append(gain_grad)
    resid_grad, skip_scaling_derivative = rms_back(
        stream_rows[3], inverses[3], gains_all[4], resid_normed_grad
    )
    stream_grads.append(resid_grad + grad_rows)
    gain_grads.append(skip_scaling_derivative)
    stream_grads_all = jnp.stack(stream_grads).reshape(STREAM_COUNT, micro_count, quarter, features)
    full_grads = lax.all_gather(
        stream_grads_all.astype(jnp.bfloat16), "hist", axis=2, tiled=True
    ).astype(stream_grads_all.dtype)
    slot_grads = []
    dyn_grad = jnp.zeros((micro_count, sequence_length, STREAM_COUNT, slot_count), jnp.float32)
    for depth_position_number in range(local_slots):
        rows_now = history[depth_position_number].astype(jnp.float32)
        slot_grads.append(
            jnp.sum(
                depth_combination_factors[depth_position_number][..., None] * full_grads, axis=0
            )
        )
        inner_now = jnp.sum(full_grads * rows_now[None], axis=-1)
        dyn_grad = dyn_grad + jnp.einsum("cmt,j->mtcj", inner_now, own_table[depth_position_number])
    dyn_grad = dyn_grad.reshape(micro_count * sequence_length, STREAM_COUNT * slot_count)
    act_part = precise(dyn_grad, mixer_output_wide.T)
    mix_out_grad = precise(kept_mix[4].T, dyn_grad)
    act_grad = lax.psum(act_part.astype(jnp.bfloat16), "hist").astype(jnp.float32)
    on_root = (hist_place == root).astype(jnp.float32)
    latest_grad, gain_zero, mix_in_grad = mix_backward(kept_mix, act_grad, gains_all[0], mix_in_all)
    gain_zero = gain_zero * on_root
    mix_in_grad = mix_in_grad * on_root
    latest_grad = latest_grad.reshape(micro_count, sequence_length, features)
    marked = []
    for depth_position_number in range(local_slots):
        is_latest = (hist_place * local_slots + depth_position_number == newest_output).astype(
            jnp.float32
        )
        marked.append(slot_grads[depth_position_number] + latest_grad * is_latest)
    history_grad = jnp.stack(marked).astype(jnp.bfloat16)
    gains_grad_full = jnp.stack(
        [gain_zero, gain_grads[0], gain_grads[1], gain_grads[2], gain_grads[3]]
    )
    share_rows = w_out.shape[0]
    per_device = mix_width // dp_count
    mix_out_padded = jnp.pad(
        mix_out_grad.reshape(dp_count, per_device, mix_width),
        ((0, 0), (0, share_rows - per_device), (0, 0)),
    ).reshape(dp_count * share_rows, mix_width)
    small_wide = jnp.concatenate([mix_in_grad, gains_grad_full.T, mix_out_padded], axis=1)
    attn_lefts = (normed[0], normed[1], normed[2], attended_low)
    attn_rights = (projection_grads[0], projection_grads[1], projection_grads[2], grad_low)
    attn_share = lax.psum_scatter(
        jnp.concatenate(
            [
                lax.dot_general(
                    left_side, right_side, contract_rows, preferred_element_type=jnp.float32
                )
                for left_side, right_side in zip(attn_lefts, attn_rights)
            ],
            axis=1,
        ).astype(jnp.bfloat16),
        "dp",
        scatter_dimension=0,
        tiled=True,
    )
    up_term = lax.dot_general(normed[3], up_grad, contract_rows, preferred_element_type=jnp.float32)
    down_term = lax.dot_general(
        hidden, grad_low, contract_rows, preferred_element_type=jnp.float32
    ).reshape(share_rows * lax.axis_size("dp"), ratio * features)
    ffn_share = lax.psum_scatter(
        jnp.concatenate([up_term, down_term, small_wide], axis=1).astype(jnp.bfloat16),
        "dp",
        scatter_dimension=0,
        tiled=True,
    )
    attn_total, ffn_total = (
        lax.psum(attn_share, "hist").astype(jnp.float32),
        lax.psum(ffn_share, "hist").astype(jnp.float32),
    )
    ff_width = ratio * features
    w_attn_grad = jnp.stack(
        [
            attn_total[:, 0:features],
            attn_total[:, features : 2 * features],
            attn_total[:, 2 * features : 3 * features],
        ]
    )
    w_out_grad = attn_total[:, 3 * features : 4 * features]
    w_up_grad = ffn_total[:, 0:ff_width]
    w_down_grad = ffn_total[:, ff_width : 2 * ff_width].reshape(share_rows * ratio, features)
    mix_in_share = ffn_total[:, 2 * ff_width : 2 * ff_width + mix_width]
    gains_share = ffn_total[:, 2 * ff_width + mix_width : 2 * ff_width + mix_width + 5].T
    mix_out_share = ffn_total[0:per_device, 2 * ff_width + mix_width + 5 :]
    return (
        block_out,
        history_grad,
        gains_share,
        mix_in_share,
        mix_out_share,
        w_attn_grad,
        w_out_grad,
        w_up_grad,
        w_down_grad,
    )


def solution(mesh):
    placed = (
        P("hist", "dp", None, None),
        P(),
        P("dp"),
        P(None, "dp"),
        P("dp", None),
        P("dp", None),
        P(None, "dp", None),
        P("dp", None),
        P("dp", None),
        P("dp", None),
        P("dp", "hist", None),
    )
    return jax.shard_map(
        shards,
        mesh=mesh,
        in_specs=placed,
        out_specs=(
            P("dp", "hist", None),
            P("hist", "dp", None, None),
            P(None, "dp"),
            P("dp", None),
            P("dp", None),
            P(None, "dp", None),
            P("dp", None),
            P("dp", None),
            P("dp", None),
        ),
        check_vma=False,
    )
```

profile of v0, /device:TPU:0, one launch (start us, length us, event | category | flops | bytes accessed | tf_op | source)
XLA Modules:
  0.0 2687.3 jit_solution(343068552630693090)
XLA Ops:
  11.6 14.8 bitcast_convert_fusion.3
  30.8 10.3 all_gather.44
  41.1 9.2 all_gather.42
  50.3 9.6 all_gather.43
  60.0 90.4 %all-reduce.6.cloned.1.call-done = bf16[3,256,2048]{2,1,0:T(8,128)(2,1)} async-done(((bf16[3,256,2048]{2,1,0:T(8,128)(2,1)}), bf16[3,256,2048]{2,1,0:T(8,128)(2,1)}) %all-reduce.6.cloned.1.call-update) | async-done | bytes 3145744 | tf_op jit(solution)/shard_map/psum | solution.py:24
  159.2 21.5 multiply_add_fusion
  182.4 12.4 copy.102
  194.9 12.2 copy.103
  207.1 387.2 %reduce-scatter.6.cloned.1.call-done = f32[4,3,64,2048]{3,2,1,0:T(8,128)} async-done(((f32[4,3,256,2048]{3,2,1,0:T(8,128)}), f32[4,3,64,2048]{3,2,1,0:T(8,128)}) %reduce-scatter.6.cloned.1.call-update) | async-done | bytes 6291472 | tf_op jit(solution)/shard_map/reduce_scatter | solution.py:249
  635.2 45.3 %all-gather.15.cloned.1.call-done = bf16[3,256,2048]{2,1,0:T(8,128)(2,1)} async-done(((bf16[3,64,2048]{2,1,0:T(8,128)(2,1)}), bf16[3,256,2048]{2,1,0:T(8,128)(2,1)}) %all-gather.15.cloned.1.call-update) | async-done | bytes 3145744 | tf_op jit(solution)/shard_map/all_gather | solution.py:269
  689.2 153.4 %all-gather.21.cloned.1.call-done = bf16[2048,8192]{1,0:T(8,128)(2,1)} async-done(((bf16[256,8192]{1,0:T(8,128)(2,1)}), bf16[2048,8192]{1,0:T(8,128)(2,1)}) %all-gather.21.cloned.1.call-update) | async-done | bytes 33554448 | tf_op jit(solution)/shard_map/all_gather | solution.py:106
  842.6 55.7 %reshape.639 = bf16[8192,2048]{1,0:T(8,128)(2,1)} reshape(bf16[2048,8192]{1,0:T(8,128)(2,1)} %all-gather.21.cloned.1.call-done) | data formatting | bytes 67108864 | tf_op jit(solution)/shard_map/reshape | solution.py:98
  898.3 107.0 %all-gather.19.cloned.1.call-done = bf16[2048,8192]{1,0:T(8,128)(2,1)} async-done(((bf16[256,8192]{1,0:T(8,128)(2,1)}), bf16[2048,8192]{1,0:T(8,128)(2,1)}) %all-gather.19.cloned.1.call-update) | async-done | bytes 33554448 | tf_op jit(solution)/shard_map/all_gather | solution.py:88
  1005.3 26.1 fusion.19
  1031.4 21.2 fusion.8
  1052.6 23.3 multiply_reduce_fusion
  1096.7 46.9 %all-gather.13.cloned.1.call-done = bf16[3,256,2048]{2,1,0:T(8,128)(2,1)} async-done(((bf16[3,64,2048]{2,1,0:T(8,128)(2,1)}), bf16[3,256,2048]{2,1,0:T(8,128)(2,1)}) %all-gather.13.cloned.1.call-update) | async-done | bytes 3145744 | tf_op jit(solution)/shard_map/all_gather | solution.py:272
  1184.7 54.7 %reduce-scatter.8.cloned.1.call-done = bf16[3,64,2048]{2,1,0:T(8,128)(2,1)} async-done(((bf16[3,256,2048]{2,1,0:T(8,128)(2,1)}), bf16[3,64,2048]{2,1,0:T(8,128)(2,1)}) %reduce-scatter.8.cloned.1.call-update) | async-done | bytes 786448 | tf_op jit(solution)/shard_map/reduce_scatter | solution.py:329
  1283.8 193.0 %all-gather.23.cloned.1.call-done = bf16[4,3,256,2048]{3,2,1,0:T(8,128)(2,1)} async-done(((bf16[4,3,64,2048]{3,2,1,0:T(8,128)(2,1)}), bf16[4,3,256,2048]{3,2,1,0:T(8,128)(2,1)}) %all-gather.23.cloned.1.call-update) | async-done | bytes 12582928 | tf_op jit(solution)/shard_map/all_gather | solution.py:371
  1476.8 31.2 %fusion = (f32[3,256,2048]{2,1,0:T(8,128)}, f32[4,3,256]{2,1,0:T(4,128)S(1)}, f32[4,3,256]{2,1,0:T(4,128)S(1)}, f32[4,3,256]{2,1,0:T(4,128)S(1)}, f32[4,3,256]{2...) fusion(bf16[4,3,256,2048]{3,2,1,0:T(8,128)(2,1)} %all-gather.23.cloned.1.call-done, ...), kind=kLoop, calls=%fused_computation.11 | loop fusion | flops 100651008 | bytes 63012864 | tf_op jit(solution)/shard_map/reduce_sum | solution.py:379
  1509.9 24.3 pad_maximum_fusion
  1536.1 21.4 convolution_convert_fusion.1
  1557.5 57.2 %reshape.650 = bf16[2048,8192]{1,0:T(8,128)(2,1)} reshape(bf16[8192,2048]{1,0:T(8,128)(2,1)} %convolution_convert_fusion.1) | data formatting | bytes 67108864 | tf_op jit(solution)/shard_map/reshape | solution.py:430
  1614.8 15.4 convolution_convert_fusion
  1638.9 8.7 fusion.35
  1648.0 155.2 %concatenate.28 = bf16[2048,16517]{1,0:T(8,128)(2,1)} concatenate(bf16[2048,8192]{1,0:T(8,128)(2,1)} %convolution_convert_fusion, bf16[2048,8192]{1,0:T(8,128)(2,1)} %reshape.650, bf16[2048,64]{1,0:T(8,128)(2,1)S(1)} %copy.121, bf16[2048,5]{1,0:T(8,128)(2,1)S(1)} %bitcast.394, bf16[2048,64]{1,0:T(8,128)(2,1)S(1)} %bitcast.393), dimensions={1} | concatenate | bytes 135307264 | tf_op jit(solution)/shard_map/concatenate | solution.py:432
  1803.3 387.8 %reduce-scatter.12.cloned.1.call-done = bf16[256,16517]{1,0:T(8,128)(2,1)} async-done(((bf16[2048,16517]{1,0:T(8,128)(2,1)}), bf16[256,16517]{1,0:T(8,128)(2,1)}) %reduce-scatter.12.cloned.1.call-update) | async-done | bytes 8456720 | tf_op jit(solution)/shard_map/reduce_scatter | solution.py:431
  2193.8 15.5 fusion.348
  2254.7 367.7 %all-reduce.10.cloned.1.call-done = (bf16[256,16517]{1,0:T(8,128)(2,1)}, bf16[256,8192]{0,1:T(8,128)(2,1)}) async-done(((bf16[256,16517]{1,0:T(8,128)(2,1)}, bf16[256,8192]{0,1:T(8,128)(2,1)}), (bf16[256,16517]{1,0:T(8,128)(2,1)}, bf16[256,8192]{0,1:T(8,128)(2,1)})) %all-reduce.10.cloned.1.call-update) | async-done | bytes 12651024 | tf_op jit(solution)/shard_map/psum | solution.py:439
  2622.4 10.6 convert_element_type.274
  2640.6 11.8 fusion.342
  2669.8 9.8 reshape.652
  (345 shorter events, 254.6 us)
Async XLA Ops:
  8.0 142.3 %all-reduce.6.cloned.1.call-start = ((), (), s32[]{:S(2)}) async-start(), calls=%async_computation.5 | async-start | bytes 6291456 | tf_op jit(solution)/shard_map/psum | solution.py:24
  26.5 155.9 %all-gather.27.cloned.1.call-start = ((), (), s32[]{:S(2)}) async-start(), calls=%async_computation.19 | async-start | bytes 9437184 | tf_op jit(solution)/shard_map/all_gather | solution.py:85
  30.0 164.8 %all-gather.29.cloned.1.call-start = ((), (), s32[]{:S(2)}) async-start(), calls=%async_computation.20 | async-start | bytes 9437184 | tf_op jit(solution)/shard_map/all_gather | solution.py:86
  30.6 563.6 %reduce-scatter.6.cloned.1.call-start = ((), (), s32[]{:S(2)}) async-start(), calls=%async_computation.6 | async-start | bytes 31457280 | tf_op jit(solution)/shard_map/reduce_scatter | solution.py:249
  30.8 127.4 %copy-start.80 = (s32[4]{0:T(128)}, s32[4]{0:T(128)S(1)}, u32[]{:S(2)}) copy-start(s32[4]{0:T(128)S(1)} %dynamic-slice) | copy-start | bytes 52
  41.1 115.6 %copy-start.64 = (bf16[64,64]{1,0:T(8,128)(2,1)}, bf16[64,64]{1,0:T(8,128)(2,1)S(1)}, u32[]{:S(2)}) copy-start(bf16[64,64]{1,0:T(8,128)(2,1)S(1)} %all_gather.44) | copy-start | bytes 24580
  59.9 94.1 %copy-start.44 = (bf16[2048,64]{0,1:T(8,128)(2,1)}, bf16[2048,64]{0,1:T(8,128)(2,1)S(1)}, u32[]{:S(2)}) copy-start(bf16[2048,64]{0,1:T(8,128)(2,1)S(1)} %all_gather.43) | copy-start | bytes 786436
  60.0 94.0 %copy-start.62 = (f32[1,2048]{1,0:T(1,128)}, f32[1,2048]{1,0:T(1,128)S(1)}, u32[]{:S(2)}) copy-start(f32[1,2048]{1,0:T(1,128)S(1)} %get-tuple-element.119) | copy-start | bytes 24580
  60.0 537.8 %copy-start.56 = (f32[1,2048]{1,0:T(1,128)}, f32[1,2048]{1,0:T(1,128)S(1)}, u32[]{:S(2)}) copy-start(f32[1,2048]{1,0:T(1,128)S(1)} %get-tuple-element.115) | copy-start | bytes 24580
  60.0 537.8 %copy-start.58 = (f32[1,2048]{1,0:T(1,128)}, f32[1,2048]{1,0:T(1,128)S(1)}, u32[]{:S(2)}) copy-start(f32[1,2048]{1,0:T(1,128)S(1)} %get-tuple-element.116) | copy-start | bytes 24580
  180.7 447.9 %all-gather.25.cloned.1.call-start = ((), (), s32[]{:S(2)}) async-start(), calls=%async_computation.18 | async-start | bytes 9437184 | tf_op jit(solution)/shard_map/all_gather | solution.py:87
  181.3 499.3 %all-gather.15.cloned.1.call-start = ((), (), s32[]{:S(2)}) async-start(), calls=%async_computation.8 | async-start | bytes 3932160 | tf_op jit(solution)/shard_map/all_gather | solution.py:269
  182.4 429.3 %copy-start.46 = (f32[64,64]{1,0:T(8,128)}, f32[64,64]{1,0:T(8,128)S(1)}, u32[]{:S(2)}) copy-start(f32[64,64]{1,0:T(8,128)S(1)} %get-tuple-element.122) | copy-start | bytes 49156
  615.3 227.3 %all-gather.21.cloned.1.call-start = ((), (), s32[]{:S(2)}) async-start(), calls=%async_computation.11 | async-start | bytes 37748736 | tf_op jit(solution)/shard_map/all_gather | solution.py:106
  623.3 382.0 %all-gather.19.cloned.1.call-start = ((), (), s32[]{:S(2)}) async-start(), calls=%async_computation.10 | async-start | bytes 37748736 | tf_op jit(solution)/shard_map/all_gather | solution.py:88
  624.0 455.7 %all-gather.17.cloned.1.call-start = ((), (), s32[]{:S(2)}) async-start(), calls=%async_computation.9 | async-start | bytes 9437184 | tf_op jit(solution)/shard_map/all_gather | solution.py:105
  624.6 519.1 %all-gather.13.cloned.1.call-start = ((), (), s32[]{:S(2)}) async-start(), calls=%async_computation.7 | async-start | bytes 3932160 | tf_op jit(solution)/shard_map/all_gather | solution.py:272
  624.8 451.0 %copy-start.75 = (f32[192]{0:T(256)}, f32[192]{0:T(256)S(1)}, u32[]{:S(2)}) copy-start(f32[192]{0:T(256)S(1)} %reshape.658) | copy-start | bytes 2308
  634.8 542.1 %reduce-scatter.10.cloned.1.call-start = ((), (), s32[]{:S(2)}) async-start(), calls=%async_computation.13 | async-start | bytes 3932160 | tf_op jit(solution)/shard_map/reduce_scatter | solution.py:335
  1096.7 142.7 %reduce-scatter.8.cloned.1.call-start = ((), (), s32[]{:S(2)}) async-start(), calls=%async_computation.12 | async-start | bytes 3932160 | tf_op jit(solution)/shard_map/reduce_scatter | solution.py:329
  1168.7 308.0 %all-gather.23.cloned.1.call-start = ((), (), s32[]{:S(2)}) async-start(), calls=%async_computation.14 | async-start | bytes 15728640 | tf_op jit(solution)/shard_map/all_gather | solution.py:371
  1258.4 375.8 %all-reduce.8.cloned.1.call-start = ((), (), s32[]{:S(2)}) async-start(), calls=%async_computation.15 | async-start | bytes 196608 | tf_op jit(solution)/shard_map/psum | solution.py:388
  1278.0 198.7 %copy-start.49 = (f32[4,3,256]{2,1,0:T(4,128)S(1)}, f32[4,3,256]{2,1,0:T(4,128)}, u32[]{:S(2)}) copy-start(f32[4,3,256]{2,1,0:T(4,128)} %copy-done.48) | copy-start | bytes 36868
  1278.0 198.7 %copy-start.51 = (f32[4,3,256]{2,1,0:T(4,128)S(1)}, f32[4,3,256]{2,1,0:T(4,128)}, u32[]{:S(2)}) copy-start(f32[4,3,256]{2,1,0:T(4,128)} %copy-done.50) | copy-start | bytes 36868
  1278.0 198.7 %copy-start.53 = (f32[4,3,256]{2,1,0:T(4,128)S(1)}, f32[4,3,256]{2,1,0:T(4,128)}, u32[]{:S(2)}) copy-start(f32[4,3,256]{2,1,0:T(4,128)} %copy-done.52) | copy-start | bytes 36868
  1278.0 198.7 %copy-start.55 = (f32[4,3,256]{2,1,0:T(4,128)S(1)}, f32[4,3,256]{2,1,0:T(4,128)}, u32[]{:S(2)}) copy-start(f32[4,3,256]{2,1,0:T(4,128)} %copy-done.54) | copy-start | bytes 36868
  1283.8 225.2 %copy-start.65 = (bf16[64,64]{1,0:T(8,128)(2,1)S(1)}, bf16[64,64]{1,0:T(8,128)(2,1)}, u32[]{:S(2)}) copy-start(bf16[64,64]{1,0:T(8,128)(2,1)} %copy-done.64) | copy-start | bytes 24580
  1509.8 293.5 %reduce-scatter.14.cloned.1.call-start = ((), (), s32[]{:S(2)}) async-start(), calls=%async_computation.17 | async-start | bytes 37748736 | tf_op jit(solution)/shard_map/reduce_scatter | solution.py:413
  1534.2 656.9 %reduce-scatter.12.cloned.1.call-start = ((), (), s32[]{:S(2)}) async-start(), calls=%async_computation.16 | async-start | bytes 76677120 | tf_op jit(solution)/shard_map/reduce_scatter | solution.py:431
  1557.5 57.3 %copy-start.78 = (bf16[2048]{0:T(1024)(128)(2,1)S(1)}, bf16[2048]{0:T(1024)(128)(2,1)}, u32[]{:S(2)}) copy-start(bf16[2048]{0:T(1024)(128)(2,1)} %get-tuple-element.59) | copy-start | bytes 12292
  1557.5 57.3 %copy-start.33 = (bf16[192,8192]{1,0:T(8,128)(2,1)S(1)}, bf16[192,8192]{1,0:T(8,128)(2,1)}, u32[]{:S(2)}) copy-start(bf16[192,8192]{1,0:T(8,128)(2,1)} %fusion.8) | copy-start | bytes 9437188
  1803.2 819.1 %all-reduce.10.cloned.1.call-start = ((), (), s32[]{:S(2)}) async-start(), calls=%async_computation.21 | async-start | bytes 25427968 | tf_op jit(solution)/shard_map/psum | solution.py:439
  (75 other events, 424.3 us)
Sparse Core Ops, SparseCore 0:
  26.5 123.7 all-reduce.5
  180.8 413.3 reduce-scatter.5
  1096.8 80.0 reduce-scatter.9
  1179.2 60.1 reduce-scatter.7
  1258.5 218.2 all-gather.22
  1510.0 32.4 all-reduce.7
  2191.3 431.0 all-reduce.9
Sparse Core Ops, SparseCore 1:
  30.1 57.7 all-gather.26
  90.3 54.2 all-gather.28
  183.8 53.2 all-gather.24
  615.4 65.1 all-gather.14
  683.2 159.3 all-gather.20
  844.6 160.6 all-gather.18
  1007.2 54.2 all-gather.16
  1063.0 80.6 all-gather.12
  1534.3 203.1 reduce-scatter.13
  1803.3 387.8 reduce-scatter.11
where the time goes:
time: 2700 us; the launch traced here: 2690 us
  waiting for transfers between devices  1840 us (68%)
  local copies, waits for them, and re-layouts  387 us (14%)
  matrix products  231 us (9%)
  other arithmetic  181 us (7%)
  blocking collectives  29.1 us (1%)
    reduce_scatter x1, waiting for transfers between devices, shards(): lax.psum_scatter(jnp.concatenate([up_term, down_term, small_wide], axis=1...  388 us
    reduce_scatter x1, waiting for transfers between devices, shards(): lax.psum_scatter(partial_sums, 'hist', scatter_dimension=2, tiled=True)  387 us
    psum x1, waiting for transfers between devices, shards(): lax.psum(ffn_share, 'hist').astype(jnp.float32)  368 us
    all_gather x1, waiting for transfers between devices, shards(): lax.all_gather(stream_grads_all.astype(jnp.bfloat16), 'hist', axis=2, til...  193 us
    concatenate x1, local copies, waits for them, and re-layouts, shards(): jnp.concatenate([up_term, down_term, small_wide], axis=1)  155 us
    all_gather x1, waiting for transfers between devices, second_rows(): lax.all_gather(down_folded, 'dp', axis=0, tiled=True)  153 us
    all_gather x1, waiting for transfers between devices, first_rows(): lax.all_gather(weights[3], 'dp', axis=0, tiled=True)  107 us
    psum x1, waiting for transfers between devices, broadcast(): return lax.psum(kept, axis)  90.4 us
  transfers between devices with their start and end apart: 17, of which 11 were waited for; matrix products, arithmetic and copies ran while one was open for 24% of the time, Pallas kernels for 0%

commit v1 on v0

--- a/solution.py
+++ b/solution.py
@@ -1,8 +1,11 @@
+import functools
 import math
 
 import jax
 import jax.numpy as jnp
 from jax import lax
+from jax.experimental import pallas as pl
+from jax.experimental.pallas import tpu as pltpu
 from jax.sharding import PartitionSpec as P
 
 MODEL_WIDTH = 2048
@@ -465,6 +468,683 @@
     )
 
 
+DEVICE_MESH = pl.DeviceIdType.MESH
+CORE, ACROSS_X, ACROSS_Y = 1, 2, 4
+
+
+def partner(column, mask):
+    moved = column
+    for bit in (1, 2, 4):
+        if mask & bit:
+            on = lax.rem(lax.div(moved, bit), 2)
+            moved = moved + bit - 2 * bit * on
+    return moved
+
+
+def greet(column, masks):
+    barrier = pltpu.get_barrier_semaphore()
+    for mask in masks:
+        pl.semaphore_signal(
+            barrier, inc=1, device_id={"dp": partner(column, mask)}, device_id_type=DEVICE_MESH
+        )
+    pl.semaphore_wait(barrier, len(masks))
+
+
+def push(source, target, send_sem, recv_sem, place):
+    copy = pltpu.make_async_remote_copy(
+        src_ref=source,
+        dst_ref=target,
+        send_sem=send_sem,
+        recv_sem=recv_sem,
+        device_id={"dp": place},
+        device_id_type=DEVICE_MESH,
+    )
+    copy.start()
+    return copy
+
+
+def gather_kernel(own_ref, all_ref, send_sem, recv_sem, local_sem):
+    column = lax.axis_index("dp")
+    rows = own_ref.shape[0]
+    half = rows // 2
+    greet(column, (CORE, ACROSS_X, ACROSS_Y))
+    across = partner(column, ACROSS_X)
+    along = partner(column, ACROSS_Y)
+    beside = partner(column, CORE)
+    corner = partner(column, ACROSS_X + ACROSS_Y)
+
+    def place(owner, part):
+        start = owner * rows + (half if part == 1 else 0)
+        count = rows if part is None else half
+        return all_ref.at[pl.ds(pl.multiple_of(start, 16), count)]
+
+    def own(part):
+        return own_ref.at[pl.ds(half if part == 1 else 0, rows if part is None else half)]
+
+    local = pltpu.make_async_copy(own_ref, place(column, None), local_sem)
+    local.start()
+
+    def send(index, source, owner, part, to):
+        return push(source, place(owner, part), send_sem.at[index], recv_sem.at[index], to)
+
+    x_second = send(0, own(1), column, 1, across)
+    y_first = send(1, own(0), column, 0, along)
+    x_first = send(2, own(0), column, 0, across)
+    y_second = send(3, own(1), column, 1, along)
+    sibling = send(4, own(None), column, None, beside)
+    y_first.wait_recv()
+    x_corner = send(5, place(along, 0), along, 0, across)
+    x_second.wait_recv()
+    y_corner = send(6, place(across, 1), across, 1, along)
+    x_first.wait_recv()
+    sibling_x = send(7, place(across, None), across, None, beside)
+    y_second.wait_recv()
+    sibling_y = send(8, place(along, None), along, None, beside)
+    x_corner.wait_recv()
+    sibling_first = send(9, place(corner, 0), corner, 0, beside)
+    y_corner.wait_recv()
+    sibling_second = send(10, place(corner, 1), corner, 1, beside)
+    for copy in (sibling, sibling_x, sibling_y, sibling_first, sibling_second):
+        copy.wait_recv()
+    for copy in (x_second, y_first, x_first, y_second, sibling, x_corner, y_corner):
+        copy.wait_send()
+    for copy in (sibling_x, sibling_y, sibling_first, sibling_second):
+        copy.wait_send()
+    local.wait()
+
+
+def plane_gather(own):
+    rows, features = own.shape
+    return pl.pallas_call(
+        gather_kernel,
+        out_shape=jax.ShapeDtypeStruct((8 * rows, features), own.dtype),
+        in_specs=[pl.BlockSpec(memory_space=pl.ANY)],
+        out_specs=pl.BlockSpec(memory_space=pl.ANY),
+        scratch_shapes=[
+            pltpu.SemaphoreType.DMA((11,)),
+            pltpu.SemaphoreType.DMA((11,)),
+            pltpu.SemaphoreType.DMA,
+        ],
+        compiler_params=pltpu.CompilerParams(collective_id=1, has_side_effects=True),
+        cost_estimate=pl.CostEstimate(
+            flops=0, bytes_accessed=64 * 8 * rows * features, transcendentals=0
+        ),
+    )(own)
+
+
+def scatter_kernel(*refs, pairs, dims):
+    inputs = refs[: 2 * pairs]
+    out_ref, out_buf, side, chip, from_x, from_y, last, send_sem, recv_sem = refs[2 * pairs :]
+    column = lax.axis_index("dp")
+    rows, features = out_ref.shape
+    half = rows // 2
+    tile = 512
+    across = partner(column, ACROSS_X)
+    along = partner(column, ACROSS_Y)
+    beside = partner(column, CORE)
+    blocks = (6, 2, 4, 0)
+
+    def product(owner, target):
+        left_rows = pl.ds(pl.multiple_of(owner * rows, 16), rows)
+
+        def one_tile(t, carry):
+            lanes = pl.ds(pl.multiple_of(t * tile, tile), tile)
+            total = None
+            for p in range(pairs):
+                left = inputs[2 * p][left_rows, :]
+                if dims[p] == 1:
+                    term = lax.dot_general(
+                        left,
+                        inputs[2 * p + 1][lanes, :],
+                        contract_cols,
+                        preferred_element_type=jnp.float32,
+                    )
+                else:
+                    term = jnp.dot(
+                        left, inputs[2 * p + 1][:, lanes], preferred_element_type=jnp.float32
+                    )
+                total = term if total is None else total + term
+            target[:, lanes] = total.astype(jnp.bfloat16)
+            return carry
+
+        lax.fori_loop(0, features // tile, one_tile, 0)
+
+    def added(target, other):
+        target[...] = (
+            target[...].astype(jnp.float32) + other[...].astype(jnp.float32)
+        ).astype(jnp.bfloat16)
+
+    def sibling_copy(i):
+        return pltpu.make_async_remote_copy(
+            src_ref=out_buf.at[i],
+            dst_ref=side.at[i],
+            send_sem=send_sem.at[i],
+            recv_sem=recv_sem.at[i],
+            device_id={"dp": beside},
+            device_id_type=DEVICE_MESH,
+        )
+
+    first, second = pl.ds(0, half), pl.ds(half, half)
+    product(partner(column, 6 + CORE), out_buf.at[0])
+    greet(column, (CORE, ACROSS_X, ACROSS_Y))
+    siblings = []
+    sends = []
+    for i, mask in enumerate(blocks):
+        if i > 0:
+            product(partner(column, mask + CORE), out_buf.at[i])
+        copy = sibling_copy(i)
+        copy.start()
+        siblings.append(copy)
+        product(partner(column, mask), chip.at[i])
+        copy.wait_recv()
+        added(chip.at[i], side.at[i])
+        if mask == 6:
+            sends.append(
+                push(chip.at[0, first], from_x.at[0], send_sem.at[4], recv_sem.at[4], across)
+            )
+            sends.append(
+                push(chip.at[0, second], from_y.at[0], send_sem.at[5], recv_sem.at[5], along)
+            )
+        if mask == 2:
+            sends.append(
+                push(chip.at[1, first], from_x.at[1], send_sem.at[6], recv_sem.at[6], across)
+            )
+        if mask == 4:
+            sends.append(
+                push(chip.at[2, second], from_y.at[1], send_sem.at[7], recv_sem.at[7], along)
+            )
+    sends[0].wait_recv()
+    added(chip.at[2, first], from_x.at[0])
+    sends.append(push(chip.at[2, first], last.at[0], send_sem.at[8], recv_sem.at[8], along))
+    sends[1].wait_recv()
+    added(chip.at[1, second], from_y.at[0])
+    sends.append(push(chip.at[1, second], last.at[1], send_sem.at[9], recv_sem.at[9], across))
+    sends[2].wait_recv()
+    added(chip.at[3, first], from_x.at[1])
+    sends[3].wait_recv()
+    added(chip.at[3, second], from_y.at[1])
+    sends[4].wait_recv()
+    added(chip.at[3, first], last.at[0])
+    sends[5].wait_recv()
+    added(chip.at[3, second], last.at[1])
+    out_ref[...] = chip[3]
+    for copy in siblings + sends:
+        copy.wait_send()
+
+
+def plane_scatter(terms, collective):
+    total, features = terms[0][0].shape[0], 0
+    rows = total // 8
+    operands, dims, flops = [], [], 0
+    for left, right, dim in terms:
+        operands += [left, right]
+        dims.append(dim)
+        features = right.shape[0] if dim == 1 else right.shape[1]
+        flops += 2 * total * left.shape[1] * features
+    block = (rows, features)
+    return pl.pallas_call(
+        functools.partial(scatter_kernel, pairs=len(terms), dims=tuple(dims)),
+        out_shape=jax.ShapeDtypeStruct(block, jnp.bfloat16),
+        in_specs=[pl.BlockSpec(memory_space=pltpu.VMEM)] * len(operands),
+        out_specs=pl.BlockSpec(memory_space=pltpu.VMEM),
+        scratch_shapes=[
+            pltpu.VMEM((4,) + block, jnp.bfloat16),
+            pltpu.VMEM((4,) + block, jnp.bfloat16),
+            pltpu.VMEM((4,) + block, jnp.bfloat16),
+            pltpu.VMEM((2, rows // 2, features), jnp.bfloat16),
+            pltpu.VMEM((2, rows // 2, features), jnp.bfloat16),
+            pltpu.VMEM((2, rows // 2, features), jnp.bfloat16),
+            pltpu.SemaphoreType.DMA((10,)),
+            pltpu.SemaphoreType.DMA((10,)),
+        ],
+        compiler_params=pltpu.CompilerParams(
+            collective_id=collective, has_side_effects=True, vmem_limit_bytes=48 * 1024 * 1024
+        ),
+        cost_estimate=pl.CostEstimate(
+            flops=flops, bytes_accessed=64 * total * features, transcendentals=0
+        ),
+    )(*operands)
+
+
+def rotary_table(row_positions, head_dim):
+    half_dim = head_dim // 2
+    frequency = jnp.exp(
+        jnp.arange(half_dim, dtype=jnp.float32) * (-2.0 * math.log(10000.0) / head_dim)
+    )
+    angles = row_positions.astype(jnp.float32)[:, None] * frequency[None, :]
+    cosine = jnp.cos(angles)
+    sine_part = jnp.sin(angles)
+    return (
+        jnp.concatenate([cosine, cosine], axis=-1),
+        jnp.concatenate([-sine_part, sine_part], axis=-1),
+    )
+
+
+def attention_kernel(
+    length_ref,
+    plane_ref,
+    cos_ref,
+    sin_ref,
+    q_ref,
+    k_ref,
+    v_ref,
+    kv_before_ref,
+    out_grad_ref,
+    att_ref,
+    q_grad_ref,
+    kv_grad_ref,
+    kv_before_grad_ref,
+    *,
+    heads,
+    micro_count,
+    sequence_length,
+):
+    column = pl.program_id(0)
+    plane = plane_ref[0]
+    rows = q_ref.shape[0]
+    scale = 1.0 / math.sqrt(HEAD_DIM)
+    row = plane * rows + lax.broadcasted_iota(jnp.int32, (rows, 1), 0)
+    start = jnp.zeros((rows, 1), jnp.int32)
+    limit = jnp.zeros((rows, 1), jnp.int32)
+    for m in range(micro_count):
+        here = (row >= m * sequence_length) & (row < (m + 1) * sequence_length)
+        start = jnp.where(here, m * sequence_length, start)
+        limit = jnp.where(here, m * sequence_length + length_ref[column * micro_count + m], limit)
+    limit = jnp.minimum(limit, row + 1)
+    key_row = (plane - 1) * rows + lax.broadcasted_iota(jnp.int32, (1, 2 * rows), 1)
+    allowed = (key_row >= start) & (key_row < limit)
+    cosine = cos_ref[...]
+    sine_part = sin_ref[...]
+    width = heads * HEAD_DIM
+    for head in range(heads):
+        lanes = slice(head * HEAD_DIM, (head + 1) * HEAD_DIM)
+        value_lanes = slice(width + head * HEAD_DIM, width + (head + 1) * HEAD_DIM)
+        query = q_ref[:, lanes]
+        keys = jnp.concatenate([kv_before_ref[:, lanes], k_ref[:, lanes]], axis=0)
+        values = jnp.concatenate([kv_before_ref[:, value_lanes], v_ref[:, lanes]], axis=0)
+        out_grad = out_grad_ref[:, lanes]
+        scores = (
+            lax.dot_general(query, keys, contract_cols, preferred_element_type=jnp.float32) * scale
+        )
+        scores = jnp.where(allowed, scores, masked_out)
+        raised = jnp.exp(scores - jnp.max(scores, axis=-1, keepdims=True))
+        weights = raised / jnp.sum(raised, axis=-1, keepdims=True)
+        weights_low = weights.astype(jnp.bfloat16)
+        att_ref[:, lanes] = matmul(weights_low, values).astype(jnp.bfloat16)
+        weight_grad = lax.dot_general(
+            out_grad, values, contract_cols, preferred_element_type=jnp.float32
+        )
+        inner = jnp.sum(weights * weight_grad, axis=-1, keepdims=True)
+        score_grad = (weights * (weight_grad - inner) * scale).astype(jnp.bfloat16)
+        query_grad = matmul(score_grad, keys)
+        swapped = jnp.concatenate(
+            [query_grad[:, HEAD_DIM // 2 :], query_grad[:, : HEAD_DIM // 2]], axis=1
+        )
+        q_grad_ref[:, lanes] = (query_grad * cosine - swapped * sine_part).astype(jnp.bfloat16)
+        key_grad = lax.dot_general(
+            score_grad, query, contract_rows, preferred_element_type=jnp.float32
+        )
+        value_grad = lax.dot_general(
+            weights_low, out_grad, contract_rows, preferred_element_type=jnp.float32
+        )
+        kv_before_grad_ref[:, lanes] = key_grad[:rows].astype(jnp.bfloat16)
+        kv_before_grad_ref[:, value_lanes] = value_grad[:rows].astype(jnp.bfloat16)
+        kv_grad_ref[:, lanes] = key_grad[rows:]
+        kv_grad_ref[:, value_lanes] = value_grad[rows:]
+
+
+def attention(
+    lengths_all, plane, cosine, sine_part, q, k, v, kv_before, out_grad, rows, micro_count, length
+):
+    total, width = q.shape
+    heads = width // HEAD_DIM
+    block = lambda columns: pl.BlockSpec((rows, columns), lambda m: (m, 0))
+    whole = pl.BlockSpec(memory_space=pltpu.SMEM)
+    table = pl.BlockSpec((rows, HEAD_DIM), lambda m: (0, 0))
+    return pl.pallas_call(
+        functools.partial(
+            attention_kernel, heads=heads, micro_count=micro_count, sequence_length=length
+        ),
+        grid=(total // rows,),
+        in_specs=[whole, whole, table, table]
+        + [block(width)] * 3
+        + [block(2 * width), block(width)],
+        out_specs=[block(width), block(width), block(2 * width), block(2 * width)],
+        out_shape=[
+            jax.ShapeDtypeStruct((total, width), jnp.bfloat16),
+            jax.ShapeDtypeStruct((total, width), jnp.bfloat16),
+            jax.ShapeDtypeStruct((total, 2 * width), jnp.float32),
+            jax.ShapeDtypeStruct((total, 2 * width), jnp.bfloat16),
+        ],
+        compiler_params=pltpu.CompilerParams(vmem_limit_bytes=32 * 1024 * 1024),
+        cost_estimate=pl.CostEstimate(
+            flops=28 * total * rows * width, bytes_accessed=24 * total * width, transcendentals=0
+        ),
+    )(lengths_all, plane, cosine, sine_part, q, k, v, kv_before, out_grad)
+
+
+def turned(values, cosine, sine_part, rows, sign):
+    total, width = values.shape
+    heads = values.reshape(total // rows, rows, width // HEAD_DIM, HEAD_DIM)
+    swapped = jnp.concatenate(
+        [heads[..., HEAD_DIM // 2 :], heads[..., : HEAD_DIM // 2]], axis=-1
+    )
+    return (
+        heads * cosine[None, :, None, :] + sign * swapped * sine_part[None, :, None, :]
+    ).reshape(total, width)
+
+
+def shards_split(
+    history,
+    history_layer_index,
+    lengths,
+    norm_gains,
+    mix_in,
+    mix_out,
+    w_attn,
+    w_out,
+    w_up,
+    w_down,
+    cotangent,
+):
+    local_slots, micro_count, sequence_length, features = history.shape
+    planes = lax.axis_size("hist")
+    columns = lax.axis_size("dp")
+    plane = lax.axis_index("hist")
+    slot_count = local_slots * planes
+    all_rows = micro_count * sequence_length
+    rows = all_rows // planes
+    share = features // columns
+    mix_width = mix_in.shape[1]
+    ff_share = w_down.shape[0]
+    low = lambda values: values.astype(jnp.bfloat16)
+
+    top = jnp.concatenate(
+        [mix_in, norm_gains.T, jnp.zeros((share, 128 - mix_width - 5), jnp.bfloat16)], axis=1
+    )
+    mix_rows = mix_out.shape[0]
+    bottom = jnp.zeros((16, 128), jnp.bfloat16)
+    bottom = bottom.at[:mix_rows, :mix_width].set(mix_out)
+    bottom = bottom.at[0, mix_width : mix_width + micro_count].set(low(lengths))
+    packed = lax.all_gather(jnp.concatenate([top, bottom], axis=0), "dp", axis=0, tiled=False)
+    mix_in_all = packed[:, :share, :mix_width].reshape(features, mix_width)
+    gains_all = (
+        packed[:, :share, mix_width : mix_width + 5].reshape(features, 5).astype(jnp.float32).T
+    )
+    mixer_output_wide = (
+        packed[:, share : share + mix_rows, :mix_width]
+        .reshape(mix_width, mix_width)
+        .astype(jnp.float32)
+    )
+    lengths_all = (
+        packed[:, share, mix_width : mix_width + micro_count].reshape(-1).astype(jnp.int32)
+    )
+
+    up_columns = lax.all_to_all(
+        w_up.reshape(share, columns, ff_share), "dp", split_axis=1, concat_axis=0, tiled=True
+    ).reshape(features, ff_share)
+    attn_columns = lax.all_to_all(
+        w_attn.reshape(3, share, columns, share).transpose(1, 2, 0, 3),
+        "dp",
+        split_axis=1,
+        concat_axis=0,
+        tiled=True,
+    ).reshape(features, 3, share)
+
+    chunk = sequence_length // planes
+    inverse_step = pow(micro_count, -1, planes)
+    received = []
+    for i in range(micro_count):
+        target = lax.rem((plane - i + planes * micro_count) * inverse_step, planes)
+        which = lax.div(target * micro_count + i, planes)
+        piece = lax.dynamic_index_in_dim(cotangent, which, 0, keepdims=False)
+        pairs = [(t, ((t - i) * inverse_step) % planes) for t in range(planes)]
+        received.append(lax.ppermute(piece, "hist", pairs))
+    my_row = plane * rows + jnp.arange(rows, dtype=jnp.int32)
+    my_position = lax.rem(my_row, sequence_length)
+    my_sequence = lax.div(my_row, sequence_length)
+    my_length = jnp.sum(
+        jnp.where(
+            my_sequence[:, None] == jnp.arange(micro_count, dtype=jnp.int32)[None, :],
+            lengths[None, :],
+            0,
+        ),
+        axis=1,
+    )
+    valid_rows = (my_position < my_length).astype(jnp.float32)[:, None]
+    grad_rows = jnp.concatenate(received, axis=0).astype(jnp.float32) * valid_rows
+    grad_all = plane_gather(low(grad_rows))
+
+    layer_lookup = (
+        history_layer_index[:, None] == jnp.arange(slot_count, dtype=jnp.int32)[None, :]
+    ).astype(jnp.float32)
+    newest_output = jnp.sum(
+        jnp.arange(slot_count, dtype=jnp.int32)
+        * (history_layer_index == slot_count - 1).astype(jnp.int32)
+    )
+    root = newest_output // local_slots
+    on_root = (plane == root).astype(jnp.float32)
+    latest_local = lax.dynamic_index_in_dim(history, newest_output % local_slots, 0, keepdims=False)
+    dyn_local, kept_mix = mix_forward(
+        latest_local.reshape(all_rows, features), gains_all[0], mix_in_all, mixer_output_wide
+    )
+    dyn_every = lax.all_gather(dyn_local, "hist", axis=0, tiled=False)
+    dyn = lax.dynamic_index_in_dim(dyn_every, root, 0, keepdims=False)
+    own_table = lax.dynamic_slice_in_dim(layer_lookup, plane * local_slots, local_slots, 0)
+    factors = jnp.einsum(
+        "tcj,sj->sct",
+        dyn.reshape(all_rows, STREAM_COUNT, slot_count),
+        own_table,
+        precision=highest,
+    )
+    flat_history = history.reshape(local_slots, all_rows, features)
+
+    def mixed(stream):
+        total = jnp.zeros((all_rows, features), jnp.float32)
+        for slot in range(local_slots):
+            total = total + factors[slot, stream][:, None] * flat_history[slot].astype(jnp.float32)
+        return lax.psum_scatter(low(total), "hist", scatter_dimension=0, tiled=True).astype(
+            jnp.float32
+        )
+
+    stream_rows = [None] * STREAM_COUNT
+    inverses = [None] * STREAM_COUNT
+    normed = [None] * STREAM_COUNT
+    for stream in (3, 0, 1, 2):
+        stream_rows[stream] = mixed(stream)
+        scaled, inverses[stream] = rms_scale(stream_rows[stream], gains_all[stream + 1])
+        normed[stream] = plane_gather(low(scaled))
+
+    up_pre = matmul(normed[3], up_columns)
+    hidden = low(jax.nn.gelu(up_pre, approximate=False))
+    hidden_grad = lax.dot_general(
+        grad_all, w_down, contract_cols, preferred_element_type=jnp.float32
+    )
+    up_grad = low(hidden_grad * gelu_slope(up_pre))
+    normed_grads = [None] * STREAM_COUNT
+    normed_grads[3] = plane_scatter([(up_grad, up_columns, 1)], 2)
+    down_term = low(
+        lax.dot_general(hidden, grad_all, contract_rows, preferred_element_type=jnp.float32)
+    )
+    up_term = low(
+        lax.dot_general(normed[3], up_grad, contract_rows, preferred_element_type=jnp.float32)
+    )
+
+    cosine, sine_part = rotary_table(my_position, HEAD_DIM)
+    q = low(turned(matmul(normed[0], attn_columns[:, 0]), cosine, sine_part, rows, 1.0))
+    k = low(turned(matmul(normed[1], attn_columns[:, 1]), cosine, sine_part, rows, 1.0))
+    v = low(matmul(normed[2], attn_columns[:, 2]))
+    onward = [(p, p + 1) for p in range(planes - 1)]
+    back = [(p + 1, p) for p in range(planes - 1)]
+    kv_before = lax.ppermute(jnp.concatenate([k, v], axis=1), "hist", onward)
+    att_grad = low(
+        lax.dot_general(grad_all, w_out, contract_cols, preferred_element_type=jnp.float32)
+    )
+    att, q_grad, kv_grad, kv_before_grad = attention(
+        lengths_all,
+        plane.reshape(1),
+        cosine,
+        sine_part,
+        q,
+        k,
+        v,
+        kv_before,
+        att_grad,
+        rows,
+        micro_count,
+        sequence_length,
+    )
+    kv_grad = kv_grad + lax.ppermute(kv_before_grad, "hist", back).astype(jnp.float32)
+    k_grad = low(turned(kv_grad[:, :share], cosine, sine_part, rows, -1.0))
+    v_grad = low(kv_grad[:, share:])
+    branch = plane_scatter([(att, w_out, 0), (hidden, w_down, 0)], 3)
+    block_rows = low((stream_rows[3] + branch.astype(jnp.float32)) * valid_rows)
+    block_out = jnp.zeros((micro_count, chunk, features), jnp.bfloat16)
+    for i in range(micro_count):
+        pairs = [(p, (micro_count * p + i) % planes) for p in range(planes)]
+        piece = lax.ppermute(block_rows[i * chunk : (i + 1) * chunk], "hist", pairs)
+        source = lax.rem((plane - i + planes * micro_count) * inverse_step, planes)
+        which = lax.div(source * micro_count + i, planes)
+        block_out = lax.dynamic_update_index_in_dim(block_out, piece, which, 0)
+    out_term = low(
+        lax.dot_general(att, grad_all, contract_rows, preferred_element_type=jnp.float32)
+    )
+    projection_grads = (q_grad, k_grad, v_grad)
+    attn_terms = []
+    for stream in range(3):
+        normed_grads[stream] = plane_scatter(
+            [(projection_grads[stream], attn_columns[:, stream], 1)], 4
+        )
+        attn_terms.append(
+            low(
+                lax.dot_general(
+                    normed[stream],
+                    projection_grads[stream],
+                    contract_rows,
+                    preferred_element_type=jnp.float32,
+                )
+            )
+        )
+
+    full_grads = [None] * STREAM_COUNT
+    gain_grads = [None] * STREAM_COUNT
+    for stream in (3, 0, 1, 2):
+        stream_grad, gain_grads[stream] = rms_back(
+            stream_rows[stream],
+            inverses[stream],
+            gains_all[stream + 1],
+            normed_grads[stream].astype(jnp.float32),
+        )
+        if stream == 3:
+            stream_grad = stream_grad + grad_rows
+        full_grads[stream] = lax.all_gather(low(stream_grad), "hist", axis=0, tiled=True).astype(
+            jnp.float32
+        )
+    inner = jnp.stack(
+        [
+            jnp.stack(
+                [
+                    jnp.sum(full_grads[stream] * flat_history[slot].astype(jnp.float32), axis=-1)
+                    for slot in range(local_slots)
+                ],
+                axis=-1,
+            )
+            for stream in range(STREAM_COUNT)
+        ],
+        axis=1,
+    )
+    dyn_part = jnp.einsum("tcs,sj->tcj", inner, own_table, precision=highest)
+    dyn_grad = jnp.sum(
+        lax.all_gather(
+            dyn_part.reshape(all_rows, STREAM_COUNT * slot_count), "hist", axis=0, tiled=False
+        ),
+        axis=0,
+    )
+    act_grad = precise(dyn_grad, mixer_output_wide.T)
+    mix_out_grad = precise(kept_mix[4].T, dyn_grad) * on_root
+    latest_grad, gain_zero, mix_in_grad = mix_backward(kept_mix, act_grad, gains_all[0], mix_in_all)
+    slot_grads = []
+    for slot in range(local_slots):
+        is_latest = (plane * local_slots + slot == newest_output).astype(jnp.float32)
+        slot_grad = latest_grad * is_latest
+        for stream in range(STREAM_COUNT):
+            slot_grad = slot_grad + factors[slot, stream][:, None] * full_grads[stream]
+        slot_grads.append(low(slot_grad))
+    history_grad = jnp.stack(slot_grads).reshape(history.shape)
+
+    def scattered(term):
+        return lax.psum_scatter(term, "hist", scatter_dimension=0, tiled=True)
+
+    def gathered(term, axis):
+        return lax.all_gather(term, "hist", axis=axis, tiled=True).astype(jnp.float32)
+
+    part = share // planes
+    w_down_grad = gathered(scattered(down_term), 0)
+    w_out_grad = gathered(scattered(out_term), 0)
+
+    def by_plane(term):
+        return (
+            term.reshape(columns, planes, part, term.shape[1])
+            .transpose(1, 0, 2, 3)
+            .reshape(features, term.shape[1])
+        )
+
+    up_own = scattered(by_plane(up_term)).reshape(columns, part, ff_share)
+    up_own = lax.all_to_all(up_own, "dp", split_axis=0, concat_axis=0, tiled=True)
+    w_up_grad = gathered(up_own.transpose(1, 0, 2).reshape(part, columns * ff_share), 0)
+    attn_own = scattered(by_plane(jnp.concatenate(attn_terms, axis=1))).reshape(
+        columns, part, 3 * share
+    )
+    attn_own = lax.all_to_all(attn_own, "dp", split_axis=0, concat_axis=0, tiled=True)
+    attn_own = attn_own.reshape(columns, part, 3, share).transpose(2, 1, 0, 3)
+    w_attn_grad = gathered(attn_own.reshape(3, part, features), 1)
+
+    small_top = jnp.concatenate(
+        [
+            mix_in_grad * on_root,
+            jnp.stack([gain_zero * on_root] + gain_grads).T,
+            jnp.zeros((features, 128 - mix_width - 5), jnp.float32),
+        ],
+        axis=1,
+    ).reshape(columns, share, 128)
+    small_bottom = jnp.pad(
+        mix_out_grad.reshape(columns, mix_rows, mix_width),
+        ((0, 0), (0, 16 - mix_rows), (0, 128 - mix_width)),
+    )
+    small = low(jnp.concatenate([small_top, small_bottom], axis=1))
+    small = lax.psum_scatter(small, "dp", scatter_dimension=0, tiled=False)
+    small = lax.psum(small, "hist").astype(jnp.float32)
+    return (
+        block_out,
+        history_grad,
+        small[:share, mix_width : mix_width + 5].T,
+        small[:share, :mix_width],
+        small[share : share + mix_rows, :mix_width],
+        w_attn_grad,
+        w_out_grad,
+        w_up_grad,
+        w_down_grad,
+    )
+
+
+def splits_by_heads(mesh, micro_count, sequence_length):
+    columns, planes = mesh.shape["dp"], mesh.shape["hist"]
+    all_rows = micro_count * sequence_length
+    rows = all_rows // planes
+    return (
+        columns == 8
+        and HEADS % columns == 0
+        and all_rows % planes == 0
+        and sequence_length % planes == 0
+        and rows % 64 == 0
+        and math.gcd(micro_count, planes) == 1
+        and all(
+            (p * rows) // sequence_length * sequence_length >= (p - 1) * rows
+            for p in range(planes)
+        )
+    )
+
+
 def solution(mesh):
     placed = (
         P("hist", "dp", None, None),
@@ -479,8 +1159,14 @@
         P("dp", None),
         P("dp", "hist", None),
     )
+    def plan(*arrays):
+        micro_count = arrays[2].shape[0]
+        if splits_by_heads(mesh, micro_count, arrays[0].shape[2]):
+            return shards_split(*arrays)
+        return shards(*arrays)
+
     return jax.shard_map(
-        shards,
+        plan,
         mesh=mesh,
         in_specs=placed,
         out_specs=(

time: 2700 us -> 1450 us (0.54)
  waiting for transfers between devices: 1840 us -> 607 us
  Pallas kernels: 0 us -> 373 us
  local copies, waits for them, and re-layouts: 387 us -> 82.1 us
  matrix products: 231 us -> 103 us
  blocking collectives: 29.1 us -> 73.9 us
  other arithmetic: 181 us -> 140 us
  starting transfers between devices: 1.34 us -> 34.2 us
    reduce_scatter x5 -> x9, waiting for transfers between devices: 831 us -> 195 us  [the longest x4 193 us: scattered(): return lax.psum_scatter(term, 'hist', scatter_dimension=0, tiled=True)]
    psum x3 -> x1, waiting for transfers between devices: 458 us -> 5.17 us  [shards_split(): small = lax.psum(small, 'hist').astype(jnp.float32)]
    pallas_call x0 -> x11, Pallas kernels: none -> 373 us  [the longest x5 190 us: plane_gather(): pl.pallas_call(gather_kernel, out_shape=jax.ShapeDtypeStruct((8 * rows, f...]
    all_gather x9 -> x8, waiting for transfers between devices: 546 us -> 289 us  [the longest x4 212 us: gathered(): lax.all_gather(term, 'hist', axis=axis, tiled=True).astype(jnp.float32)]
    concatenate x1 -> x2, local copies, waits for them, and re-layouts: 155 us -> 2.87 us  [the longest x1 2.79 us: shards_split(): jnp.concatenate(attn_terms, axis=1)]
    reshape x6 -> x7, local copies, waits for them, and re-layouts: 132 us -> 13.5 us  [the longest x1 4.83 us: shards_split(): w_up.reshape(share, columns, ff_share)]
    ppermute x0 -> x8, waiting for transfers between devices: none -> 112 us  [the longest x1 87.6 us: shards_split(): lax.ppermute(kv_before_grad, 'hist', back).astype(jnp.float32)]
    dot_general x19 -> x10, matrix products: 155 us -> 56 us  [the longest x1 12.7 us: shards_split(): lax.dot_general(grad_all, w_down, contract_cols, preferred_element_type=j...]
  transfers between devices with their start and end apart: 17 -> 29, of which waited for: 11 -> 17; matrix products, arithmetic and copies ran while one was open for 24% -> 18% of each run, Pallas kernels for 0% -> 23%
where the time goes in v1:
time: 1450 us; the launch traced here: 1440 us
  waiting for transfers between devices  607 us (42%)
  Pallas kernels  373 us (26%)
  other arithmetic  140 us (10%)
  matrix products  103 us (7%)
  local copies, waits for them, and re-layouts  82.1 us (6%)
  blocking collectives  73.9 us (5%)
  starting transfers between devices  34.2 us (2%)
  between operations  21.6 us (1%)
    all_gather x4, waiting for transfers between devices, gathered(): lax.all_gather(term, 'hist', axis=axis, tiled=True).astype(jnp.float32)  212 us
    reduce_scatter x4, waiting for transfers between devices, scattered(): return lax.psum_scatter(term, 'hist', scatter_dimension=0, tiled=True)  193 us
    pallas_call x5, Pallas kernels, plane_gather(): pl.pallas_call(gather_kernel, out_shape=jax.ShapeDtypeStruct((8 * rows, f...  190 us
    pallas_call x5, Pallas kernels, plane_scatter(): pl.pallas_call(functools.partial(scatter_kernel, pairs=len(terms), dims=t...  168 us
    ppermute x1, waiting for transfers between devices, shards_split(): lax.ppermute(kv_before_grad, 'hist', back).astype(jnp.float32)  87.6 us
    all_gather x4, waiting for transfers between devices, shards_split(): lax.all_gather(low(stream_grad), 'hist', axis=0, tiled=True)  76.7 us
    convert_element_type x16, other arithmetic, shards_split(): low = lambda values: values.astype(jnp.bfloat16)  58.7 us
    dot_general x5, matrix products, matmul(): return jnp.dot(left_side, right_side, preferred_element_type=jnp.float32)  35.5 us
  transfers between devices with their start and end apart: 29, of which 17 were waited for; matrix products, arithmetic and copies ran while one was open for 18% of the time, Pallas kernels for 23%

profile of v1, /device:TPU:0, one launch (start us, length us, event | category | flops | bytes accessed | tf_op | source)
XLA Modules:
  0.0 1435.3 jit_solution(17879541146834555518)
XLA Ops:
  19.2 11.4 all-gather
  54.7 20.2 %all-gather.1 = f32[3072,64]{0,1:T(8,128)} all-gather(f32[768,64]{0,1:T(8,128)S(1)} %fusion.154), channel_id=3, replica_groups=mesh['dp'=8,'hist'=4] {'hist'}, dimensions={0}, use_global_device_ids=true | all-gather | bytes 983040 | tf_op jit(solution)/shard_map/all_gather | solution.py:931
  79.3 10.7 fusion.44
  141.2 31.7 %shard_map.181 = bf16[1536,2048]{1,0:T(8,128)(2,1)} custom-call(bf16[192,2048]{1,0:T(8,128)(2,1)} %fusion.127.own_ref), custom_call_target="tpu_custom_call" | custom-call | bytes 201326592 | tf_op jit(solution)/shard_map/pallas_call | solution.py:558
  194.3 64.7 %shard_map.180 = bf16[1536,2048]{1,0:T(8,128)(2,1)} custom-call(bf16[192,2048]{1,0:T(8,128)(2,1)} %fusion.108.own_ref), custom_call_target="tpu_custom_call" | custom-call | bytes 201326592 | tf_op jit(solution)/shard_map/pallas_call | solution.py:558
  262.7 31.0 %shard_map.178 = bf16[1536,2048]{1,0:T(8,128)(2,1)} custom-call(bf16[192,2048]{1,0:T(8,128)(2,1)} %fusion.94.own_ref), custom_call_target="tpu_custom_call" | custom-call | bytes 201326592 | tf_op jit(solution)/shard_map/pallas_call | solution.py:558
  297.6 31.1 %shard_map.179 = bf16[1536,2048]{1,0:T(8,128)(2,1)} custom-call(bf16[192,2048]{1,0:T(8,128)(2,1)} %fusion.101.own_ref), custom_call_target="tpu_custom_call" | custom-call | bytes 201326592 | tf_op jit(solution)/shard_map/pallas_call | solution.py:558
  351.8 31.2 %shard_map.183 = bf16[1536,2048]{1,0:T(8,128)(2,1)} custom-call(bf16[192,2048]{1,0:T(8,128)(2,1)} %fusion.115.own_ref), custom_call_target="tpu_custom_call" | custom-call | bytes 201326592 | tf_op jit(solution)/shard_map/pallas_call | solution.py:558
  383.1 24.3 %fusion.2 = (bf16[1536,1024]{1,0:T(8,128)(2,1)}, f32[1536,1024]{1,0:T(8,128)}) fusion(bf16[1536,2048]{1,0:T(8,128)(2,1)} %shard_map.183, bf16[2048,1024]{1,0:T(8,128)(2,1)} %bitcast.51.refs_1_), kind=kOutput, calls=%fused_computation.53 | convolution fusion | flops 6544687104 | bytes 19922944 | tf_op jit(solution)/shard_map/dot_general | solution.py:31
  408.4 15.1 %shard_map.182 = (bf16[1536,256]{1,0:T(8,128)(2,1)S(1)}, bf16[1536,256]{1,0:T(8,128)(2,1)S(1)}, f32[1536,512]{1,0:T(8,128)S(1)}, bf16[1536,512]{1,0:T(8,128)(2,1)S(1)}) custom-call(s32[24]{0:T(128)S(1)} %reshape.395.length_ref, s32[1]{0:T(128)} %bitcast.17.plane_ref, f32[192,128]{1,0:T(8,128)S(1)} %pad_maximum_fusion.4.cos_ref, ...), custom_call_target="tpu_custom_call" | custom-call | flops 2113929216 | bytes 9437184 | tf_op jit(solution)/shard_map/pallas_call | solution.py:804
  426.3 32.1 %shard_map.185 = bf16[192,2048]{1,0:T(8,128)(2,1)S(1)} custom-call(bf16[1536,256]{1,0:T(8,128)(2,1)S(1)} %get-tuple-element.38.refs_0_, bf16[2048,256]{1,0:T(8,128)(2,1)S(1)} %get-tuple-element.152.refs_1_), custom_call_target="tpu_custom_call" | custom-call | flops 1610612736 | bytes 201326592 | tf_op jit(solution)/shard_map/pallas_call | solution.py:685
  460.4 12.7 fusion.8.refs_0_
  473.2 36.6 %shard_map.188 = bf16[192,2048]{1,0:T(8,128)(2,1)S(1)} custom-call(bf16[1536,1024]{1,0:T(8,128)(2,1)S(1)} %fusion.8.refs_0_, bf16[2048,1024]{1,0:T(8,128)(2,1)} %bitcast.51.refs_1_), custom_call_target="tpu_custom_call" | custom-call | flops 6442450944 | bytes 201326592 | tf_op jit(solution)/shard_map/pallas_call | solution.py:685
  510.3 35.1 %shard_map.184 = bf16[192,2048]{1,0:T(8,128)(2,1)S(1)} custom-call(bf16[1536,256]{1,0:T(8,128)(2,1)S(1)} %get-tuple-element.37.refs_0_, bf16[256,2048]{1,0:T(8,128)(2,1)S(1)} %copy-done.10, bf16[1536,1024]{1,0:T(8,128)(2,1)S(1)} %copy-done.14, bf16[1024,2048]{1,0:T(8,128)(2,1)} %refs_3_.1), custom_call_target="tpu_custom_call" | custom-call | flops 8053063680 | bytes 201326592 | tf_op jit(solution)/shard_map/pallas_call | solution.py:685
  550.1 87.6 %collective-permute-done.7 = bf16[1536,512]{1,0:T(8,128)(2,1)S(1)} collective-permute-done((bf16[1536,512]{1,0:T(8,128)(2,1)}, bf16[1536,512]{1,0:T(8,128)(2,1)S(1)}, u32[]{:S(2)}, u32[]{:S(2)}) %collective-permute-start.7) | collective-permute-done | bytes 1572896 | tf_op jit(solution)/shard_map/ppermute | solution.py:997
  638.4 31.6 %shard_map.187 = bf16[192,2048]{1,0:T(8,128)(2,1)S(1)} custom-call(bf16[1536,256]{1,0:T(8,128)(2,1)S(1)} %slice.358.refs_0_, bf16[2048,256]{1,0:T(8,128)(2,1)S(1)} %copy-done.5), custom_call_target="tpu_custom_call" | custom-call | flops 1610612736 | bytes 201326592 | tf_op jit(solution)/shard_map/pallas_call | solution.py:685
  680.2 32.4 %shard_map.186 = bf16[192,2048]{1,0:T(8,128)(2,1)S(1)} custom-call(bf16[1536,256]{1,0:T(8,128)(2,1)S(1)} %fusion.122.refs_0_, bf16[2048,256]{1,0:T(8,128)(2,1)S(1)} %copy-done.4), custom_call_target="tpu_custom_call" | custom-call | flops 1610612736 | bytes 201326592 | tf_op jit(solution)/shard_map/pallas_call | solution.py:685
  721.1 12.4 all-gather.15.cloned.1.call-done
  733.5 64.3 %all-gather.13.cloned.1.call-done = bf16[768,2048]{1,0:T(8,128)(2,1)} async-done(((bf16[192,2048]{1,0:T(8,128)(2,1)}), bf16[768,2048]{1,0:T(8,128)(2,1)}) %all-gather.13.cloned.1.call-update) | async-done | bytes 3145744 | tf_op jit(solution)/shard_map/all_gather | solution.py:1040
  797.8 13.9 fusion.45
  812.3 26.0 %all_gather.47 = f32[4,768,64]{1,2,0:T(8,128)S(1)} all-gather(f32[1,768,64]{1,2,0:T(8,128)S(1)} %bitcast.288), channel_id=1, replica_groups=mesh['dp'=8,'hist'=4] {'hist'}, dimensions={0}, use_global_device_ids=true | all-gather | bytes 983040 | tf_op jit(solution)/shard_map/all_gather | solution.py:1058
  847.4 11.6 fusion.68
  862.4 11.2 convolution_convert_fusion
  893.0 8.9 convolution_convert_fusion.1
  905.8 68.9 %reduce-scatter.26.cloned.1.call-done = bf16[256,2048]{1,0:T(8,128)(2,1)} async-done(((bf16[1024,2048]{1,0:T(8,128)(2,1)}), bf16[256,2048]{1,0:T(8,128)(2,1)}) %reduce-scatter.26.cloned.1.call-update) | async-done | bytes 1048592 | tf_op jit(solution)/shard_map/reduce_scatter | solution.py:1076
  974.7 63.0 %reduce-scatter.20.cloned.1.call-done = bf16[512,768]{1,0:T(8,128)(2,1)} async-done(((bf16[2048,768]{1,0:T(8,128)(2,1)}), bf16[512,768]{1,0:T(8,128)(2,1)}) %reduce-scatter.20.cloned.1.call-update) | async-done | bytes 786448 | tf_op jit(solution)/shard_map/reduce_scatter | solution.py:1076
  1037.8 16.2 %all_to_all.40 = bf16[8,64,768]{2,1,0:T(8,128)(2,1)S(1)} all-to-all(bf16[8,64,768]{2,1,0:T(8,128)(2,1)} %bitcast.286), channel_id=1, replica_groups=mesh['dp'=8,'hist'=4] {'dp'}, dimensions={0} | all-to-all | bytes 1572864 | tf_op jit(solution)/shard_map/all_to_all | solution.py:1098
  1056.2 61.3 %reduce-scatter.24.cloned.1.call-done = bf16[512,1024]{1,0:T(8,128)(2,1)} async-done(((bf16[2048,1024]{1,0:T(8,128)(2,1)}), bf16[512,1024]{1,0:T(8,128)(2,1)}) %reduce-scatter.24.cloned.1.call-update) | async-done | bytes 1048592 | tf_op jit(solution)/shard_map/reduce_scatter | solution.py:1076
  1162.2 9.7 fusion.13
  1198.8 77.8 %all-gather.25.cloned.1.call-done = bf16[1024,2048]{1,0:T(8,128)(2,1)} async-done(((bf16[256,2048]{1,0:T(8,128)(2,1)}), bf16[1024,2048]{1,0:T(8,128)(2,1)}) %all-gather.25.cloned.1.call-update) | async-done | bytes 4194320 | tf_op jit(solution)/shard_map/all_gather | solution.py:1079
  1283.2 56.9 %all-gather.19.cloned.1.call-done = bf16[3,256,2048]{2,1,0:T(8,128)(2,1)} async-done(((bf16[3,64,2048]{2,1,0:T(8,128)(2,1)}), bf16[3,256,2048]{2,1,0:T(8,128)(2,1)}) %all-gather.19.cloned.1.call-update) | async-done | bytes 3145744 | tf_op jit(solution)/shard_map/all_gather | solution.py:1079
  1345.5 76.1 %all-gather.23.cloned.1.call-done = bf16[256,8192]{1,0:T(8,128)(2,1)} async-done(((bf16[64,8192]{1,0:T(8,128)(2,1)}), bf16[256,8192]{1,0:T(8,128)(2,1)}) %all-gather.23.cloned.1.call-update) | async-done | bytes 4194320 | tf_op jit(solution)/shard_map/all_gather | solution.py:1079
  (408 shorter events, 296.0 us)
Async XLA Ops:
  7.2 183.5 %reduce-scatter.16.cloned.1.call-start = ((), (), s32[]{:S(2)}) async-start(), calls=%async_computation.16 | async-start | bytes 3932160 | tf_op jit(solution)/shard_map/reduce_scatter | solution.py:946
  90.1 168.9 %reduce-scatter.12.cloned.1.call-start = ((), (), s32[]{:S(2)}) async-start(), calls=%async_computation.14 | async-start | bytes 3932160 | tf_op jit(solution)/shard_map/reduce_scatter | solution.py:946
  90.9 202.9 %reduce-scatter.14.cloned.1.call-start = ((), (), s32[]{:S(2)}) async-start(), calls=%async_computation.15 | async-start | bytes 3932160 | tf_op jit(solution)/shard_map/reduce_scatter | solution.py:946
  101.0 77.5 %all-to-all-start = ((bf16[256,8,3,256]{3,0,2,1:T(8,128)(2,1)}), bf16[256,8,3,256]{3,0,2,1:T(8,128)(2,1)}, u32[]{:S(2)}, u32[]{:S(2)}) async-start(bf16[256,8,3,256]{3,0,2,1:T(8,128)(2,1)} %copy.112), calls=%async_computation.2 | async-start | bytes 6291456 | tf_op jit(solution)/shard_map/all_to_all | solution.py:886
  105.4 242.7 %reduce-scatter.10.cloned.1.call-start = ((), (), s32[]{:S(2)}) async-start(), calls=%async_computation.13 | async-start | bytes 3932160 | tf_op jit(solution)/shard_map/reduce_scatter | solution.py:946
  107.5 20.3 %collective-permute-start.1 = (bf16[64,2048]{1,0:T(8,128)(2,1)}, bf16[64,2048]{1,0:T(8,128)(2,1)S(1)}, u32[]{:S(2)}, u32[]{:S(2)}) collective-permute-start(bf16[64,2048]{1,0:T(8,128)(2,1)} %get-tuple-element.164), channel_id=1, source_target_pairs={{0,0},{1,3},{2,2},{3,1},{4,4},{5,7},{6,6},{7,5},{8,8},{9,11},{10,1... | collective-permute-start | bytes 786440 | tf_op jit(solution)/shard_map/ppermute | solution.py:902
  109.1 24.7 %collective-permute-start.2 = (bf16[64,2048]{1,0:T(8,128)(2,1)}, bf16[64,2048]{1,0:T(8,128)(2,1)}, u32[]{:S(2)}, u32[]{:S(2)}) collective-permute-start(bf16[64,2048]{1,0:T(8,128)(2,1)} %get-tuple-element.166), channel_id=1, source_target_pairs={{0,1},{1,0},{2,3},{3,2},{4,5},{5,4},{6,7},{7,6},{8,9},{9,8},{10,11... | collective-permute-start | bytes 786440 | tf_op jit(solution)/shard_map/ppermute | solution.py:902
  112.3 26.7 %collective-permute-start.3 = (bf16[64,2048]{1,0:T(8,128)(2,1)}, bf16[64,2048]{1,0:T(8,128)(2,1)}, u32[]{:S(2)}, u32[]{:S(2)}) collective-permute-start(bf16[64,2048]{1,0:T(8,128)(2,1)} %get-tuple-element.165), channel_id=1, source_target_pairs={{0,2},{1,1},{2,0},{3,3},{4,6},{5,5},{6,4},{7,7},{8,10},{9,9},{10,8... | collective-permute-start | bytes 786440 | tf_op jit(solution)/shard_map/ppermute | solution.py:902
  178.4 204.6 %all-to-all-start.1 = ((bf16[256,8,1024]{2,0,1:T(8,128)(2,1)}), bf16[256,8,1024]{2,0,1:T(8,128)(2,1)}, u32[]{:S(2)}, u32[]{:S(2)}) async-start(bf16[256,8,1024]{2,0,1:T(8,128)(2,1)} %bitcast.251), calls=%async_computation.5 | async-start | bytes 8388608 | tf_op jit(solution)/shard_map/all_to_all | solution.py:883
  183.0 538.0 %all-gather.11.cloned.1.call-start = ((), (), s32[]{:S(2)}) async-start(), calls=%async_computation.17 | async-start | bytes 3932160 | tf_op jit(solution)/shard_map/all_gather | solution.py:1040
  343.6 64.7 %collective-permute-start = (bf16[1536,512]{1,0:T(8,128)(2,1)}, bf16[1536,512]{1,0:T(8,128)(2,1)}, u32[]{:S(2)}, u32[]{:S(2)}) collective-permute-start(bf16[1536,512]{1,0:T(8,128)(2,1)} %pad_maximum_fusion.2), channel_id=1, source_target_pairs={{0,1},{1,2},{2,3},{4,5},{5,6},{6,7},{8,9},{9,10},{10,11},{12,13},{... | collective-permute-start | bytes 4718600 | tf_op jit(solution)/shard_map/ppermute | solution.py:979
  460.4 260.7 %all-gather.17.cloned.1.call-start = ((), (), s32[]{:S(2)}) async-start(), calls=%async_computation.20 | async-start | bytes 3932160 | tf_op jit(solution)/shard_map/all_gather | solution.py:1040
  548.6 184.8 %all-gather.15.cloned.1.call-start = ((), (), s32[]{:S(2)}) async-start(), calls=%async_computation.19 | async-start | bytes 3932160 | tf_op jit(solution)/shard_map/all_gather | solution.py:1040
  548.7 89.0 %collective-permute-start.7 = (bf16[1536,512]{1,0:T(8,128)(2,1)}, bf16[1536,512]{1,0:T(8,128)(2,1)S(1)}, u32[]{:S(2)}, u32[]{:S(2)}) collective-permute-start(bf16[1536,512]{1,0:T(8,128)(2,1)} %copy-done.8), channel_id=1, source_target_pairs={{1,0},{2,1},{3,2},{5,4},{6,5},{7,6},{9,8},{10,9},{11,10},{13,12},{... | collective-permute-start | bytes 4718600 | tf_op jit(solution)/shard_map/ppermute | solution.py:997
  671.9 125.9 %all-gather.13.cloned.1.call-start = ((), (), s32[]{:S(2)}) async-start(), calls=%async_computation.18 | async-start | bytes 3932160 | tf_op jit(solution)/shard_map/all_gather | solution.py:1040
  714.5 190.2 %reduce-scatter.22.cloned.1.call-start = ((), (), s32[]{:S(2)}) async-start(), calls=%async_computation.25 | async-start | bytes 1310720 | tf_op jit(solution)/shard_map/reduce_scatter | solution.py:1076
  720.9 184.3 %reduce-scatter.18.cloned.1.call-start = ((), (), s32[]{:S(2)}) async-start(), calls=%async_computation.21 | async-start | bytes 626688 | tf_op jit(solution)/shard_map/reduce_scatter | solution.py:1115
  721.0 117.4 %copy-start.81 = (f32[768,64]{0,1:T(8,128)S(1)}, f32[768,64]{0,1:T(8,128)}, u32[]{:S(2)}) copy-start(f32[768,64]{0,1:T(8,128)} %get-tuple-element.188) | copy-start | bytes 589828
  721.0 118.4 %copy-start.40 = (bf16[8,256,64]{2,1,0:T(8,128)(2,1)S(1)}, bf16[8,256,64]{2,1,0:T(8,128)(2,1)}, u32[]{:S(2)}) copy-start(bf16[8,256,64]{2,1,0:T(8,128)(2,1)} %slice.287) | copy-start | bytes 786436
  721.0 118.4 %copy-start.42 = (f32[1,2048]{1,0:T(1,128)S(1)}, f32[1,2048]{1,0:T(1,128)}, u32[]{:S(2)}) copy-start(f32[1,2048]{1,0:T(1,128)} %copy-done.41) | copy-start | bytes 24580
  862.4 112.3 %reduce-scatter.26.cloned.1.call-start = ((), (), s32[]{:S(2)}) async-start(), calls=%async_computation.29 | async-start | bytes 5242880 | tf_op jit(solution)/shard_map/reduce_scatter | solution.py:1076
  873.7 164.1 %reduce-scatter.20.cloned.1.call-start = ((), (), s32[]{:S(2)}) async-start(), calls=%async_computation.23 | async-start | bytes 3932160 | tf_op jit(solution)/shard_map/reduce_scatter | solution.py:1076
  893.0 224.6 %reduce-scatter.24.cloned.1.call-start = ((), (), s32[]{:S(2)}) async-start(), calls=%async_computation.27 | async-start | bytes 5242880 | tf_op jit(solution)/shard_map/reduce_scatter | solution.py:1076
  904.5 254.6 %all-gather.21.cloned.1.call-start = ((), (), s32[]{:S(2)}) async-start(), calls=%async_computation.26 | async-start | bytes 1310720 | tf_op jit(solution)/shard_map/all_gather | solution.py:1079
  905.1 289.2 %all-reduce.4.cloned.1.call-start = ((), (), s32[]{:S(2)}) async-start(), calls=%async_computation.22 | async-start | bytes 139264 | tf_op jit(solution)/shard_map/psum | solution.py:1116
  905.7 370.9 %all-gather.25.cloned.1.call-start = ((), (), s32[]{:S(2)}) async-start(), calls=%async_computation.30 | async-start | bytes 5242880 | tf_op jit(solution)/shard_map/all_gather | solution.py:1079
  974.7 365.4 %all-gather.19.cloned.1.call-start = ((), (), s32[]{:S(2)}) async-start(), calls=%async_computation.24 | async-start | bytes 3932160 | tf_op jit(solution)/shard_map/all_gather | solution.py:1079
  1117.5 19.7 %all-to-all-start.3 = ((bf16[8,64,1024]{2,1,0:T(8,128)(2,1)}), bf16[8,64,1024]{2,1,0:T(8,128)(2,1)}, u32[]{:S(2)}, u32[]{:S(2)}) async-start(bf16[8,64,1024]{2,1,0:T(8,128)(2,1)} %bitcast.283), calls=%async_computation.11 | async-start | bytes 2097152 | tf_op jit(solution)/shard_map/all_to_all | solution.py:1093
  1121.8 299.9 %all-gather.23.cloned.1.call-start = ((), (), s32[]{:S(2)}) async-start(), calls=%async_computation.28 | async-start | bytes 5242880 | tf_op jit(solution)/shard_map/all_gather | solution.py:1079
  1123.8 15.7 %collective-permute-start.4 = (bf16[64,2048]{1,0:T(8,128)(2,1)}, bf16[64,2048]{1,0:T(8,128)(2,1)S(1)}, u32[]{:S(2)}, u32[]{:S(2)}) collective-permute-start(bf16[64,2048]{1,0:T(8,128)(2,1)} %get-tuple-element.163), channel_id=1, source_target_pairs={{0,0},{1,3},{2,2},{3,1},{4,4},{5,7},{6,6},{7,5},{8,8},{9,11},{10,1... | collective-permute-start | bytes 786440 | tf_op jit(solution)/shard_map/ppermute | solution.py:1005
  1127.3 22.2 %collective-permute-start.5 = (bf16[64,2048]{1,0:T(8,128)(2,1)}, bf16[64,2048]{1,0:T(8,128)(2,1)}, u32[]{:S(2)}, u32[]{:S(2)}) collective-permute-start(bf16[64,2048]{1,0:T(8,128)(2,1)} %get-tuple-element.162), channel_id=1, source_target_pairs={{0,1},{1,0},{2,3},{3,2},{4,5},{5,4},{6,7},{7,6},{8,9},{9,8},{10,11... | collective-permute-start | bytes 786440 | tf_op jit(solution)/shard_map/ppermute | solution.py:1005
  1130.8 25.2 %collective-permute-start.6 = (bf16[64,2048]{1,0:T(8,128)(2,1)}, bf16[64,2048]{1,0:T(8,128)(2,1)}, u32[]{:S(2)}, u32[]{:S(2)}) collective-permute-start(bf16[64,2048]{1,0:T(8,128)(2,1)} %get-tuple-element.161), channel_id=1, source_target_pairs={{0,2},{1,1},{2,0},{3,3},{4,6},{5,5},{6,4},{7,7},{8,10},{9,9},{10,8... | collective-permute-start | bytes 786440 | tf_op jit(solution)/shard_map/ppermute | solution.py:1005
  (86 other events, 2205.7 us)
Sparse Core Ops, SparseCore 0:
  90.2 70.1 reduce-scatter.15
  162.8 60.2 reduce-scatter.11
  225.4 60.2 reduce-scatter.13
  287.8 60.2 reduce-scatter.9
  460.5 62.9 all-gather.10
  548.8 87.4 all-gather.16
  672.0 61.4 all-gather.14
  735.6 62.1 all-gather.12
  800.6 33.5 reduce-scatter.21
  862.5 32.4 reduce-scatter.17
  897.9 76.7 reduce-scatter.25
  976.9 60.7 reduce-scatter.19
  1040.7 76.7 reduce-scatter.23
  1119.0 40.1 all-gather.20
  1161.3 32.9 all-reduce.3
  1195.8 80.7 all-gather.24
  1278.1 61.9 all-gather.18
  1342.2 79.4 all-gather.22

commit v2 on v0

--- a/solution.py
+++ b/solution.py
@@ -1,8 +1,11 @@
+import functools
 import math
 
 import jax
 import jax.numpy as jnp
 from jax import lax
+from jax.experimental import pallas as pl
+from jax.experimental.pallas import tpu as pltpu
 from jax.sharding import PartitionSpec as P
 
 MODEL_WIDTH = 2048
@@ -465,6 +468,1841 @@
     )
 
 
+DEVICE_MESH = pl.DeviceIdType.MESH
+CORE, ACROSS_X, ACROSS_Y = 1, 2, 4
+
+
+def partner(column, mask):
+    moved = column
+    for bit in (1, 2, 4):
+        if mask & bit:
+            on = lax.rem(lax.div(moved, bit), 2)
+            moved = moved + bit - 2 * bit * on
+    return moved
+
+
+def greet(column, masks):
+    barrier = pltpu.get_barrier_semaphore()
+    for mask in masks:
+        pl.semaphore_signal(
+            barrier, inc=1, device_id={"dp": partner(column, mask)}, device_id_type=DEVICE_MESH
+        )
+    pl.semaphore_wait(barrier, len(masks))
+
+
+def push(source, target, send_sem, recv_sem, place):
+    copy = pltpu.make_async_remote_copy(
+        src_ref=source,
+        dst_ref=target,
+        send_sem=send_sem,
+        recv_sem=recv_sem,
+        device_id={"dp": place},
+        device_id_type=DEVICE_MESH,
+    )
+    copy.start()
+    return copy
+
+
+def z_place(plane):
+    return {"hist": plane}
+
+
+class PlaneGatherSteps:
+
+    def __init__(self, column, own, whole, send_sem, recv_sem, local_sem):
+        self.column, self.own, self.whole = column, own, whole
+        self.send_sem, self.recv_sem, self.local_sem = send_sem, recv_sem, local_sem
+        self.rows = own.shape[0]
+        self.half = self.rows // 2
+        self.across = partner(column, ACROSS_X)
+        self.along = partner(column, ACROSS_Y)
+        self.beside = partner(column, CORE)
+        self.corner = partner(column, ACROSS_X + ACROSS_Y)
+        self.copies = []
+
+    def place(self, owner, part):
+        start = owner * self.rows + (self.half if part == 1 else 0)
+        count = self.rows if part is None else self.half
+        return self.whole.at[pl.ds(pl.multiple_of(start, 16), count)]
+
+    def mine(self, part):
+        start = self.half if part == 1 else 0
+        return self.own.at[pl.ds(start, self.rows if part is None else self.half)]
+
+    def send(self, source, owner, part, to):
+        index = len(self.copies)
+        copy = push(
+            source, self.place(owner, part), self.send_sem.at[index], self.recv_sem.at[index], to
+        )
+        self.copies.append(copy)
+
+    def begin(self):
+        me = self.column
+        self.local = pltpu.make_async_copy(self.mine(None), self.place(me, None), self.local_sem)
+        self.local.start()
+        self.send(self.mine(1), me, 1, self.across)
+        self.send(self.mine(0), me, 0, self.along)
+        self.send(self.mine(0), me, 0, self.across)
+        self.send(self.mine(1), me, 1, self.along)
+        self.send(self.mine(None), me, None, self.beside)
+
+    def corners(self):
+        self.copies[1].wait_recv()
+        self.send(self.place(self.along, 0), self.along, 0, self.across)
+        self.copies[0].wait_recv()
+        self.send(self.place(self.across, 1), self.across, 1, self.along)
+
+    def siblings(self):
+        self.copies[2].wait_recv()
+        self.send(self.place(self.across, None), self.across, None, self.beside)
+        self.copies[3].wait_recv()
+        self.send(self.place(self.along, None), self.along, None, self.beside)
+
+    def rest(self):
+        self.copies[5].wait_recv()
+        self.send(self.place(self.corner, 0), self.corner, 0, self.beside)
+        self.copies[6].wait_recv()
+        self.send(self.place(self.corner, 1), self.corner, 1, self.beside)
+
+    def finish(self):
+        for index in (4, 7, 8, 9, 10):
+            self.copies[index].wait_recv()
+        for copy in self.copies:
+            copy.wait_send()
+        self.local.wait()
+
+
+class PlaneScatterSteps:
+    def __init__(self, column, product, refs, send_sem, recv_sem):
+        self.column, self.product = column, product
+        self.out_buf, self.side, self.chip, self.from_x, self.from_y, self.last = refs
+        self.send_sem, self.recv_sem = send_sem, recv_sem
+        rows = self.chip.shape[1]
+        self.first, self.second = pl.ds(0, rows // 2), pl.ds(rows // 2, rows // 2)
+        self.across = partner(column, ACROSS_X)
+        self.along = partner(column, ACROSS_Y)
+        self.beside = partner(column, CORE)
+        self.pair, self.sends = [], []
+
+    def block(self, i):
+        mask = (6, 2, 4, 0)[i]
+        self.product(partner(self.column, mask + CORE), self.out_buf.at[i])
+        self.pair.append(
+            push(
+                self.out_buf.at[i],
+                self.side.at[i],
+                self.send_sem.at[i],
+                self.recv_sem.at[i],
+                self.beside,
+            )
+        )
+        self.product(partner(self.column, mask), self.chip.at[i])
+        self.pair[i].wait_recv()
+        add_into(self.chip.at[i], self.side.at[i])
+        if i == 0:
+            self.send(self.chip.at[0, self.first], self.from_x.at[0], self.across)
+            self.send(self.chip.at[0, self.second], self.from_y.at[0], self.along)
+        if i == 1:
+            self.send(self.chip.at[1, self.first], self.from_x.at[1], self.across)
+        if i == 2:
+            self.send(self.chip.at[2, self.second], self.from_y.at[1], self.along)
+
+    def send(self, source, target, to):
+        index = 4 + len(self.sends)
+        self.sends.append(
+            push(source, target, self.send_sem.at[index], self.recv_sem.at[index], to)
+        )
+
+    def turn(self):
+        self.sends[0].wait_recv()
+        add_into(self.chip.at[2, self.first], self.from_x.at[0])
+        self.send(self.chip.at[2, self.first], self.last.at[0], self.along)
+        self.sends[1].wait_recv()
+        add_into(self.chip.at[1, self.second], self.from_y.at[0])
+        self.send(self.chip.at[1, self.second], self.last.at[1], self.across)
+
+    def finish(self, out_ref):
+        self.sends[2].wait_recv()
+        add_into(self.chip.at[3, self.first], self.from_x.at[1])
+        self.sends[3].wait_recv()
+        add_into(self.chip.at[3, self.second], self.from_y.at[1])
+        self.sends[4].wait_recv()
+        add_into(self.chip.at[3, self.first], self.last.at[0])
+        self.sends[5].wait_recv()
+        add_into(self.chip.at[3, self.second], self.last.at[1])
+        out_ref[...] = self.chip[3]
+        for copy in self.pair + self.sends:
+            copy.wait_send()
+
+
+def add_into(target, other):
+    rows = target.shape[0]
+    step = 32 if rows % 32 == 0 else 16
+
+    def some_rows(r, carry):
+        piece = pl.ds(pl.multiple_of(r * step, step), step)
+        target[piece, :] = (
+            target[piece, :].astype(jnp.float32) + other[piece, :].astype(jnp.float32)
+        ).astype(jnp.bfloat16)
+        return carry
+
+    lax.fori_loop(0, rows // step, some_rows, 0)
+
+
+class LineSums:
+
+    def __init__(self, plane, parts, arrived, own, last, held, send_sem, recv_sem, load_sem):
+        self.plane, self.parts, self.arrived = plane, parts, arrived
+        self.own, self.last, self.held = own, last, held
+        self.send_sem, self.recv_sem, self.load_sem = send_sem, recv_sem, load_sem
+        self.rows = own.shape[0]
+
+    def part(self, way, item, b):
+        place = b if way == 0 else 3 - b
+        return self.parts.at[pl.ds((item * 4 + place) * self.rows, self.rows)]
+
+    def message(self, way, turn, a, source):
+        to = a + 1 if way == 0 else 2 - a
+        return pltpu.make_async_remote_copy(
+            src_ref=source,
+            dst_ref=self.arrived.at[way * 12 + turn],
+            send_sem=self.send_sem.at[way * 12 + turn],
+            recv_sem=self.recv_sem.at[way * 12 + turn],
+            device_id=z_place(to),
+            device_id_type=DEVICE_MESH,
+        )
+
+    def origin(self, way, turn):
+        item, t = divmod(turn, 3)
+        return self.message(way, turn, 0, self.part(way, item, 3 - t))
+
+    def slot(self, way, a, turn):
+        item, t = divmod(turn, 3)
+        return way * 2 + (item * (3 - a) + t) % 2
+
+    def relay(self, way, turn, a):
+        return self.message(way, turn, a, self.held.at[self.slot(way, a, turn)])
+
+    def start(self):
+        for place in (0, 3):
+
+            @pl.when(self.plane == place)
+            def _():
+                way = 0 if place == 0 else 1
+                self.origin(way, 0).start()
+                self.origin(way, 1).start()
+
+    def load(self, source, target, index):
+        return pltpu.make_async_copy(source, target, self.load_sem.at[index])
+
+    def service(self, sigma):
+        for place in range(4):
+
+            @pl.when(self.plane == place)
+            def _():
+                for way in (0, 1):
+                    a = place if way == 0 else 3 - place
+                    if a == 0:
+                        if sigma < 12:
+                            self.origin(way, sigma).wait_send()
+                        if sigma + 2 < 12:
+                            self.origin(way, sigma + 2).start()
+                        continue
+                    turn = sigma - a + 1
+                    if turn < 0 or turn >= 12:
+                        continue
+                    item, t = divmod(turn, 3)
+                    b = 3 - t
+                    if b < a:
+                        continue
+                    if b > a:
+                        slot = self.slot(way, a, turn)
+                        sent = [
+                            earlier
+                            for earlier in range(turn)
+                            if 3 - earlier % 3 > a and self.slot(way, a, earlier) == slot
+                        ]
+                        if sent:
+                            self.relay(way, sent[-1], a).wait_send()
+                        target = self.held.at[slot]
+                        mine = self.load(self.part(way, item, b), self.own, 0)
+                        mine.start()
+                        self.relay(way, turn, a).wait_recv()
+                        came = self.load(self.arrived.at[way * 12 + turn], target, 1)
+                        came.start()
+                        mine.wait()
+                        came.wait()
+                        add_into(target, self.own)
+                        self.relay(way, turn, a).start()
+                    else:
+                        self.message(way, turn, a - 1, self.own).wait_recv()
+                        came = self.load(self.arrived.at[way * 12 + turn], self.last.at[way], 1)
+                        came.start()
+                        came.wait()
+                if sigma % 3 == 2:
+                    item = sigma // 3
+                    mine = self.load(self.part(0, item, place), self.own, 0)
+                    mine.start()
+                    mine.wait()
+
+    def drain(self):
+        for place in range(4):
+
+            @pl.when(self.plane == place)
+            def _():
+                for way in (0, 1):
+                    a = place if way == 0 else 3 - place
+                    if a == 0 or a == 3:
+                        continue
+                    for slot in (way * 2, way * 2 + 1):
+                        sent = [
+                            turn
+                            for turn in range(12)
+                            if 3 - turn % 3 > a and self.slot(way, a, turn) == slot
+                        ]
+                        self.relay(way, sent[-1], a).wait_send()
+
+
+def forward_kernel(
+    part_ref,
+    grad_ref,
+    w_up_ref,
+    w_attn_ref,
+    w_down_ref,
+    gain_ref,
+    x_ref,
+    normed_ref,
+    grad_all_ref,
+    hidden_ref,
+    up_term_ref,
+    down_term_ref,
+    back_ref,
+    attn_columns_ref,
+    arrived_ref,
+    normed3,
+    grads,
+    up_columns,
+    up_grad,
+    out_buf,
+    side,
+    chip,
+    from_x,
+    from_y,
+    last,
+    own,
+    ends,
+    held,
+    x_buf,
+    normed_buf,
+    term_buf,
+    gather_send,
+    gather_recv,
+    gather_local,
+    scatter_send,
+    scatter_recv,
+    line_send,
+    line_recv,
+    line_load,
+    swap_send,
+    swap_recv,
+    swap_local,
+    out_sem,
+):
+    column = lax.axis_index("dp")
+    plane = lax.axis_index("hist")
+    rows, features = grad_ref.shape
+    total = 8 * rows
+    share = w_up_ref.shape[0]
+    ff_share = w_down_ref.shape[0]
+    tile = 256
+
+    barrier = pltpu.get_barrier_semaphore()
+    for mask in range(1, 8):
+        pl.semaphore_signal(
+            barrier, inc=1, device_id={"dp": partner(column, mask)}, device_id_type=DEVICE_MESH
+        )
+    for place in range(4):
+
+        @pl.when(plane == place)
+        def _():
+            nearby = [p for p in (place - 1, place + 1) if 0 <= p < 4]
+            for p in nearby:
+                pl.semaphore_signal(
+                    barrier, inc=1, device_id=z_place(p), device_id_type=DEVICE_MESH
+                )
+            pl.semaphore_wait(barrier, 7 + len(nearby))
+
+    line = LineSums(
+        plane, part_ref, arrived_ref, own, ends, held, line_send, line_recv, line_load
+    )
+    line.start()
+    zeros = jnp.zeros((16, features), jnp.bfloat16)
+
+    def clear(r, carry):
+        ends[0, pl.ds(pl.multiple_of(r * 16, 16), 16), :] = zeros
+        ends[1, pl.ds(pl.multiple_of(r * 16, 16), 16), :] = zeros
+        return carry
+
+    lax.fori_loop(0, rows // 16, clear, 0)
+
+    my_rows = pl.ds(pl.multiple_of(column * share, 16), share)
+
+    def up_piece(owner):
+        return w_up_ref.at[:, pl.ds(pl.multiple_of(owner * ff_share, 128), ff_share)]
+
+    up_local = pltpu.make_async_copy(up_piece(column), up_columns.at[my_rows], swap_local.at[0])
+    up_local.start()
+    up_swaps = [
+        push(
+            up_piece(partner(column, mask)),
+            up_columns.at[my_rows],
+            swap_send.at[mask],
+            swap_recv.at[mask],
+            partner(column, mask),
+        )
+        for mask in (6, 7, 2, 3, 4, 5, 1)
+    ]
+
+    def gather(index, own_rows, whole):
+        return PlaneGatherSteps(
+            column,
+            own_rows,
+            whole,
+            gather_send.at[index],
+            gather_recv.at[index],
+            gather_local.at[index],
+        )
+
+    grad_gather = gather(4, grad_ref, grads)
+    grad_gather.begin()
+
+    x_copies = []
+
+    def combine(item):
+        if item >= 2:
+            x_copies[item - 2].wait()
+        x_now = x_buf.at[item % 2]
+
+        def some_rows(r, carry):
+            piece = pl.ds(pl.multiple_of(r * 16, 16), 16)
+            x = (
+                own[piece, :].astype(jnp.float32)
+                + ends[0, piece, :].astype(jnp.float32)
+                + ends[1, piece, :].astype(jnp.float32)
+            )
+            x_now[piece, :] = x
+            inverse = lax.rsqrt(jnp.mean(x * x, axis=-1, keepdims=True) + epsilon)
+            normed_buf[item, piece, :] = (x * inverse * gain_ref[pl.ds(item, 1), :]).astype(
+                jnp.bfloat16
+            )
+            return carry
+
+        lax.fori_loop(0, rows // 16, some_rows, 0)
+        copy = pltpu.make_async_copy(x_now, x_ref.at[item], out_sem.at[item % 2])
+        copy.start()
+        x_copies.append(copy)
+        steps = gather(
+            item, normed_buf.at[item], normed3 if item == 0 else normed_ref.at[item - 1]
+        )
+        steps.begin()
+        return steps
+
+    line.service(0)
+    grad_gather.corners()
+    line.service(1)
+    grad_gather.siblings()
+    line.service(2)
+    gather3 = combine(0)
+    grad_gather.rest()
+    gather3.corners()
+    line.service(3)
+    grad_gather.finish()
+    grads_out = pltpu.make_async_copy(grads, grad_all_ref, out_sem.at[2])
+    grads_out.start()
+    gather3.siblings()
+    gather3.rest()
+    line.service(4)
+    for copy in up_swaps:
+        copy.wait_recv()
+    up_local.wait()
+    gather3.finish()
+
+    def attn_piece(stream, owner):
+        return w_attn_ref.at[stream, :, pl.ds(pl.multiple_of(owner * share, 128), share)]
+
+    def attn_place(stream):
+        return attn_columns_ref.at[stream, my_rows]
+
+    attn_swaps, attn_locals = [], []
+    for stream in range(3):
+        local = pltpu.make_async_copy(
+            attn_piece(stream, column), attn_place(stream), swap_local.at[1 + stream]
+        )
+        local.start()
+        attn_locals.append(local)
+        for mask in (6, 7, 2, 3, 4, 5, 1):
+            attn_swaps.append(
+                push(
+                    attn_piece(stream, partner(column, mask)),
+                    attn_place(stream),
+                    swap_send.at[8 * (stream + 1) + mask],
+                    swap_recv.at[8 * (stream + 1) + mask],
+                    partner(column, mask),
+                )
+            )
+
+    def feed(first_block, count):
+        def one_tile(step, carry):
+            piece = pl.ds(pl.multiple_of((step // (ff_share // tile)) * rows, 16), rows)
+            lanes = pl.ds(pl.multiple_of((step % (ff_share // tile)) * tile, tile), tile)
+            up = jnp.dot(normed3[piece, :], up_columns[:, lanes], preferred_element_type=jnp.float32)
+            spread = 0.5 * (1.0 + lax.erf(up * (1.0 / math.sqrt(2.0))))
+            hidden_ref[piece, lanes] = (up * spread).astype(jnp.bfloat16)
+            slope = spread + up * jnp.exp(-0.5 * up * up) * (1.0 / math.sqrt(2.0 * math.pi))
+            hidden_grad = lax.dot_general(
+                grads[piece, :],
+                w_down_ref[lanes, :],
+                contract_cols,
+                preferred_element_type=jnp.float32,
+            )
+            up_grad[piece, lanes] = (hidden_grad * slope).astype(jnp.bfloat16)
+            return carry
+
+        per_block = ff_share // tile
+        lax.fori_loop(first_block * per_block, (first_block + count) * per_block, one_tile, 0)
+
+    feed(0, 1)
+    line.service(5)
+    gather0 = combine(1)
+    feed(1, 3)
+    gather0.corners()
+    line.service(6)
+    feed(4, 2)
+    gather0.siblings()
+    gather0.rest()
+    line.service(7)
+    feed(6, 2)
+
+    def back_product(owner, target):
+        left_rows = pl.ds(pl.multiple_of(owner * rows, 16), rows)
+
+        def one_tile(t, carry):
+            lanes = pl.ds(pl.multiple_of(t * 2 * tile, 2 * tile), 2 * tile)
+            target[:, lanes] = lax.dot_general(
+                up_grad[left_rows, :],
+                up_columns[lanes, :],
+                contract_cols,
+                preferred_element_type=jnp.float32,
+            ).astype(jnp.bfloat16)
+            return carry
+
+        lax.fori_loop(0, features // (2 * tile), one_tile, 0)
+
+    scatter = PlaneScatterSteps(
+        column,
+        back_product,
+        (out_buf, side, chip, from_x, from_y, last),
+        scatter_send,
+        scatter_recv,
+    )
+    scatter.block(0)
+    line.service(8)
+    gather1 = combine(2)
+    gather0.finish()
+    scatter.block(1)
+    scatter.block(2)
+    scatter.block(3)
+    scatter.turn()
+    gather1.corners()
+    line.service(9)
+    scatter.finish(back_ref)
+
+    term_slots = 2
+    part = share // 4
+
+    def term_copies(kind, slot, index):
+        if kind == 0:
+            return [
+                pltpu.make_async_copy(
+                    term_buf.at[slot, pl.ds(h * part, part), pl.ds(0, ff_share)],
+                    up_term_ref.at[
+                        pl.ds(h * 4 * part + index % 4 * part, part),
+                        pl.ds(index // 4 * ff_share, ff_share),
+                    ],
+                    out_sem.at[3 + 4 * slot + h],
+                )
+                for h in range(4)
+            ]
+        return [
+            pltpu.make_async_copy(
+                term_buf.at[slot], down_term_ref.at[pl.ds(index * tile, tile)], out_sem.at[3 + 4 * slot]
+            )
+        ]
+
+    def terms(kind, first, count):
+        width = ff_share if kind == 0 else features
+        pending = []
+        for index in range(first, first + count):
+            slot = index % term_slots
+            if len(pending) >= term_slots:
+                for copy in pending[-term_slots]:
+                    copy.wait()
+
+            def one_tile(t, carry):
+                lanes = pl.ds(pl.multiple_of(t * 2 * tile, 2 * tile), 2 * tile)
+                if kind == 0:
+                    left, right = normed3[:, index * tile : (index + 1) * tile], up_grad[:, lanes]
+                else:
+                    left, right = hidden_ref[:, index * tile : (index + 1) * tile], grads[:, lanes]
+                term_buf[slot, :, lanes] = lax.dot_general(
+                    left, right, contract_rows, preferred_element_type=jnp.float32
+                ).astype(jnp.bfloat16)
+                return carry
+
+            lax.fori_loop(0, width // (2 * tile), one_tile, 0)
+            copies = term_copies(kind, slot, index)
+            for copy in copies:
+                copy.start()
+            pending.append(copies)
+        for copies in pending[-term_slots:]:
+            for copy in copies:
+                copy.wait()
+
+    terms(1, 0, 2)
+    gather1.siblings()
+    gather1.rest()
+    terms(1, 2, ff_share // tile - 2)
+    line.service(10)
+    terms(0, 0, 4)
+    gather1.finish()
+    line.service(11)
+    gather2 = combine(3)
+    terms(0, 4, features // tile - 4)
+    gather2.corners()
+    gather2.siblings()
+    gather2.rest()
+    line.drain()
+    for copy in attn_swaps:
+        copy.wait_recv()
+    for copy in attn_locals:
+        copy.wait()
+    for copy in up_swaps + attn_swaps:
+        copy.wait_send()
+    grads_out.wait()
+    for copy in x_copies[-2:]:
+        copy.wait()
+    gather2.finish()
+
+
+def forward_and_feed(parts, grad_low, w_up, w_attn, w_down, gains):
+    rows, features = grad_low.shape
+    total = 8 * rows
+    share = w_up.shape[0]
+    ff_share = w_down.shape[0]
+    block = (rows, features)
+    half = (2, rows // 2, features)
+    anywhere = pl.BlockSpec(memory_space=pl.ANY)
+    near = pl.BlockSpec(memory_space=pltpu.VMEM)
+    shape = jax.ShapeDtypeStruct
+    low_type = jnp.bfloat16
+    return pl.pallas_call(
+        forward_kernel,
+        in_specs=[anywhere, near, anywhere, anywhere, near, near],
+        out_specs=[anywhere, anywhere, anywhere, near, anywhere, anywhere, near]
+        + [anywhere, anywhere],
+        out_shape=[
+            shape((4,) + block, jnp.float32),
+            shape((3, total, features), low_type),
+            shape((total, features), low_type),
+            shape((total, ff_share), low_type),
+            shape((features * ff_share // features, features), low_type),
+            shape((ff_share, features), low_type),
+            shape(block, low_type),
+            shape((3, features, share), low_type),
+            shape((24,) + block, low_type),
+        ],
+        scratch_shapes=[
+            pltpu.VMEM((total, features), low_type),
+            pltpu.VMEM((total, features), low_type),
+            pltpu.VMEM((features, ff_share), low_type),
+            pltpu.VMEM((total, ff_share), low_type),
+            pltpu.VMEM((4,) + block, low_type),
+            pltpu.VMEM((4,) + block, low_type),
+            pltpu.VMEM((4,) + block, low_type),
+            pltpu.VMEM(half, low_type),
+            pltpu.VMEM(half, low_type),
+            pltpu.VMEM(half, low_type),
+            pltpu.VMEM(block, low_type),
+            pltpu.VMEM((2,) + block, low_type),
+            pltpu.VMEM((4,) + block, low_type),
+            pltpu.VMEM((2,) + block, jnp.float32),
+            pltpu.VMEM((4,) + block, low_type),
+            pltpu.VMEM((2, 256, features), low_type),
+            pltpu.SemaphoreType.DMA((5, 11)),
+            pltpu.SemaphoreType.DMA((5, 11)),
+            pltpu.SemaphoreType.DMA((5,)),
+            pltpu.SemaphoreType.DMA((10,)),
+            pltpu.SemaphoreType.DMA((10,)),
+            pltpu.SemaphoreType.DMA((24,)),
+            pltpu.SemaphoreType.DMA((24,)),
+            pltpu.SemaphoreType.DMA((2,)),
+            pltpu.SemaphoreType.DMA((32,)),
+            pltpu.SemaphoreType.DMA((32,)),
+            pltpu.SemaphoreType.DMA((4,)),
+            pltpu.SemaphoreType.DMA((11,)),
+        ],
+        compiler_params=pltpu.CompilerParams(
+            collective_id=5, has_side_effects=True, vmem_limit_bytes=62 * 1024 * 1024
+        ),
+        cost_estimate=pl.CostEstimate(
+            flops=12 * total * features * ff_share,
+            bytes_accessed=400 * 1000 * 1000,
+            transcendentals=0,
+        ),
+    )(parts, grad_low, w_up, w_attn, w_down, gains)
+
+
+class LineSum:
+
+    def __init__(self, plane, parts, arrived, own, last, held, send_sem, recv_sem, load_sem):
+        self.plane, self.parts, self.arrived = plane, parts, arrived
+        self.own, self.last, self.held = own, last, held
+        self.send_sem, self.recv_sem, self.load_sem = send_sem, recv_sem, load_sem
+        self.rows = own.shape[0]
+
+    def part(self, way, b):
+        place = b if way == 0 else 3 - b
+        return self.parts.at[pl.ds(place * self.rows, self.rows)]
+
+    def message(self, way, t, a, source):
+        return pltpu.make_async_remote_copy(
+            src_ref=source,
+            dst_ref=self.arrived.at[way * 3 + t],
+            send_sem=self.send_sem.at[way * 3 + t],
+            recv_sem=self.recv_sem.at[way * 3 + t],
+            device_id=z_place(a + 1 if way == 0 else 2 - a),
+            device_id_type=DEVICE_MESH,
+        )
+
+    def origin(self, way, t):
+        return self.message(way, t, 0, self.part(way, 3 - t))
+
+    def relay(self, way, t, a):
+        return self.message(way, t, a, self.held.at[t if a == 1 else 2])
+
+    def start(self):
+        for place in (0, 3):
+
+            @pl.when(self.plane == place)
+            def _():
+                way = 0 if place == 0 else 1
+                self.origin(way, 0).start()
+                self.origin(way, 1).start()
+
+    def load(self, source, target, index):
+        copy = pltpu.make_async_copy(source, target, self.load_sem.at[index])
+        copy.start()
+        return copy
+
+    def service(self, sigma):
+        for place in range(4):
+
+            @pl.when(self.plane == place)
+            def _():
+                for way in (0, 1):
+                    a = place if way == 0 else 3 - place
+                    if a == 0:
+                        self.origin(way, sigma).wait_send()
+                        if sigma == 0:
+                            self.origin(way, 2).start()
+                        continue
+                    t = sigma - a + 1
+                    if t < 0 or 3 - t < a:
+                        continue
+                    b = 3 - t
+                    source = self.arrived.at[way * 3 + t]
+                    if b > a:
+                        relay = self.relay(way, t, a)
+                        target = self.held.at[t if a == 1 else 2]
+                        mine = self.load(self.part(way, b), self.own, 0)
+                        relay.wait_recv()
+                        came = self.load(source, target, 1)
+                        mine.wait()
+                        came.wait()
+                        add_into(target, self.own)
+                        relay.start()
+                    else:
+                        self.message(way, t, a - 1, self.own).wait_recv()
+                        self.load(source, self.last.at[way], 1).wait()
+                if sigma == 2:
+                    self.load(self.part(0, place), self.own, 0).wait()
+
+    def finish(self, target):
+        step = 16
+
+        def some_rows(r, carry):
+            piece = pl.ds(pl.multiple_of(r * step, step), step)
+            total = self.own[piece, :].astype(jnp.float32)
+            total = total + self.last[0, piece, :].astype(jnp.float32)
+            total = total + self.last[1, piece, :].astype(jnp.float32)
+            target[piece, :] = total.astype(jnp.bfloat16)
+            return carry
+
+        lax.fori_loop(0, self.rows // step, some_rows, 0)
+        for place in (1, 2):
+
+            @pl.when(self.plane == place)
+            def _():
+                for way in (0, 1):
+                    a = place if way == 0 else 3 - place
+                    for t in range(3 - a):
+                        self.relay(way, t, a).wait_send()
+
+
+class LineGather:
+
+    def __init__(self, plane, own, slot, send_sem, recv_sem, local_sem):
+        self.plane, self.own, self.slot = plane, own, slot
+        self.send_sem, self.recv_sem, self.local_sem = send_sem, recv_sem, local_sem
+
+    def message(self, way, a, distance):
+        origin = a - distance
+        plane_of_origin = origin if way == 0 else 3 - origin
+        target = self.slot(plane_of_origin)
+        return pltpu.make_async_remote_copy(
+            src_ref=self.own if distance == 0 else target,
+            dst_ref=target,
+            send_sem=self.send_sem.at[way * 3 + distance],
+            recv_sem=self.recv_sem.at[way * 3 + distance],
+            device_id=z_place(a + 1 if way == 0 else 2 - a),
+            device_id_type=DEVICE_MESH,
+        )
+
+    def service(self, step):
+        for place in range(4):
+
+            @pl.when(self.plane == place)
+            def _():
+                if step == 0:
+                    pltpu.make_async_copy(self.own, self.slot(place), self.local_sem).start()
+                for way in (0, 1):
+                    a = place if way == 0 else 3 - place
+                    if step > a:
+                        continue
+                    if step > 0:
+                        self.message(way, a - 1, step - 1).wait_recv()
+                    if a < 3:
+                        self.message(way, a, step).start()
+
+    def finish(self):
+        for place in range(4):
+
+            @pl.when(self.plane == place)
+            def _():
+                pltpu.make_async_copy(self.own, self.slot(place), self.local_sem).wait()
+                for way in (0, 1):
+                    a = place if way == 0 else 3 - place
+                    if a < 3:
+                        for distance in range(a + 1):
+                            self.message(way, a, distance).wait_send()
+
+
+def attend_column(
+    column,
+    plane,
+    length_ref,
+    cosine,
+    sine_part,
+    q_ref,
+    k_ref,
+    v_ref,
+    kv_before_ref,
+    out_grad_ref,
+    att_ref,
+    q_grad_ref,
+    kv_grad_ref,
+    kv_before_grad_ref,
+    rows,
+    micro_count,
+    sequence_length,
+):
+    here = pl.ds(pl.multiple_of(column * rows, 16), rows)
+    width = q_ref.shape[1]
+    scale = 1.0 / math.sqrt(HEAD_DIM)
+    row = plane * rows + lax.broadcasted_iota(jnp.int32, (rows, 1), 0)
+    start = jnp.zeros((rows, 1), jnp.int32)
+    limit = jnp.zeros((rows, 1), jnp.int32)
+    for m in range(micro_count):
+        inside = (row >= m * sequence_length) & (row < (m + 1) * sequence_length)
+        start = jnp.where(inside, m * sequence_length, start)
+        limit = jnp.where(inside, m * sequence_length + length_ref[column * micro_count + m], limit)
+    limit = jnp.minimum(limit, row + 1)
+    key_row = (plane - 1) * rows + lax.broadcasted_iota(jnp.int32, (1, 2 * rows), 1)
+    allowed = (key_row >= start) & (key_row < limit)
+    for head in range(width // HEAD_DIM):
+        lanes = slice(head * HEAD_DIM, (head + 1) * HEAD_DIM)
+        value_lanes = slice(width + head * HEAD_DIM, width + (head + 1) * HEAD_DIM)
+        query = q_ref[here, lanes]
+        keys = jnp.concatenate([kv_before_ref[here, lanes], k_ref[here, lanes]], axis=0)
+        values = jnp.concatenate([kv_before_ref[here, value_lanes], v_ref[here, lanes]], axis=0)
+        out_grad = out_grad_ref[here, lanes]
+        scores = (
+            lax.dot_general(query, keys, contract_cols, preferred_element_type=jnp.float32) * scale
+        )
+        scores = jnp.where(allowed, scores, masked_out)
+        raised = jnp.exp(scores - jnp.max(scores, axis=-1, keepdims=True))
+        weights = raised / jnp.sum(raised, axis=-1, keepdims=True)
+        weights_low = weights.astype(jnp.bfloat16)
+        att_ref[here, lanes] = matmul(weights_low, values).astype(jnp.bfloat16)
+        weight_grad = lax.dot_general(
+            out_grad, values, contract_cols, preferred_element_type=jnp.float32
+        )
+        inner = jnp.sum(weights * weight_grad, axis=-1, keepdims=True)
+        score_grad = (weights * (weight_grad - inner) * scale).astype(jnp.bfloat16)
+        query_grad = matmul(score_grad, keys)
+        swapped = jnp.concatenate(
+            [query_grad[:, HEAD_DIM // 2 :], query_grad[:, : HEAD_DIM // 2]], axis=1
+        )
+        q_grad_ref[here, lanes] = (query_grad * cosine - swapped * sine_part).astype(jnp.bfloat16)
+        key_grad = lax.dot_general(
+            score_grad, query, contract_rows, preferred_element_type=jnp.float32
+        )
+        value_grad = lax.dot_general(
+            weights_low, out_grad, contract_rows, preferred_element_type=jnp.float32
+        )
+        kv_before_grad_ref[here, lanes] = key_grad[:rows].astype(jnp.bfloat16)
+        kv_before_grad_ref[here, value_lanes] = value_grad[:rows].astype(jnp.bfloat16)
+        kv_grad_ref[here, lanes] = key_grad[rows:]
+        kv_grad_ref[here, value_lanes] = value_grad[rows:]
+
+
+def backward_kernel(
+    length_ref,
+    cos_ref,
+    sin_ref,
+    q_ref,
+    k_ref,
+    v_ref,
+    out_grad_ref,
+    normed_ref,
+    grad_all_ref,
+    hidden_ref,
+    w_out_ref,
+    w_down_ref,
+    attn_columns_ref,
+    x_ref,
+    gain_ref,
+    grad_ref,
+    back3_ref,
+    down_term_ref,
+    up_term_ref,
+    full_ref,
+    down_all_ref,
+    up_all_ref,
+    quarter_ref,
+    branch_ref,
+    gain_grad_ref,
+    attn_parts_ref,
+    arrived_ref,
+    big,
+    att,
+    q_grad,
+    kv_grad,
+    kv_before,
+    kv_before_grad,
+    kv_after,
+    out_buf,
+    side,
+    chip,
+    from_x,
+    from_y,
+    last,
+    line_own,
+    line_ends,
+    line_held,
+    down_own,
+    up_sum,
+    up_own,
+    stream_own,
+    back_buf,
+    x_buf,
+    stage,
+    scatter_send,
+    scatter_recv,
+    sum_send,
+    sum_recv,
+    load_sem,
+    spread_send,
+    spread_recv,
+    spread_local,
+    key_send,
+    key_recv,
+    swap_send,
+    swap_recv,
+    local_sem,
+    *,
+    micro_count,
+    sequence_length,
+):
+    column = lax.axis_index("dp")
+    plane = lax.axis_index("hist")
+    rows, features = grad_ref.shape
+    total = 8 * rows
+    width = q_ref.shape[1]
+    ff_share = w_down_ref.shape[0]
+    quarter = features // 8 // 4
+    k_grad, v_grad, attn_sum = q_grad, att, up_sum
+    tile = 512
+
+    barrier = pltpu.get_barrier_semaphore()
+    for mask in range(1, 8):
+        pl.semaphore_signal(
+            barrier, inc=1, device_id={"dp": partner(column, mask)}, device_id_type=DEVICE_MESH
+        )
+    for place in range(4):
+
+        @pl.when(plane == place)
+        def _():
+            nearby = [p for p in (place - 1, place + 1) if 0 <= p < 4]
+            for p in nearby:
+                pl.semaphore_signal(
+                    barrier, inc=1, device_id=z_place(p), device_id_type=DEVICE_MESH
+                )
+            pl.semaphore_wait(barrier, 7 + len(nearby))
+
+    def key_copies(place):
+        return [
+            pltpu.make_async_remote_copy(
+                src_ref=source,
+                dst_ref=kv_before.at[:, pl.ds(i * width, width)],
+                send_sem=key_send.at[i],
+                recv_sem=key_recv.at[i],
+                device_id=z_place(place + 1),
+                device_id_type=DEVICE_MESH,
+            )
+            for i, source in enumerate((k_ref, v_ref))
+        ]
+
+    def back_copy(place):
+        return pltpu.make_async_remote_copy(
+            src_ref=kv_before_grad,
+            dst_ref=kv_after,
+            send_sem=key_send.at[2],
+            recv_sem=key_recv.at[2],
+            device_id=z_place(place - 1),
+            device_id_type=DEVICE_MESH,
+        )
+
+    def clear(target):
+        step = 64
+
+        def some_rows(r, carry):
+            target[pl.ds(pl.multiple_of(r * step, step), step), :] = jnp.zeros(
+                (step, target.shape[1]), jnp.bfloat16
+            )
+            return carry
+
+        lax.fori_loop(0, target.shape[0] // step, some_rows, 0)
+
+    for place in range(3):
+
+        @pl.when(plane == place)
+        def _():
+            for copy in key_copies(place):
+                copy.start()
+
+    line_sums = [
+        LineSum(
+            plane,
+            parts,
+            arrived_ref.at[pl.ds(6 * i, 6)],
+            line_own,
+            line_ends,
+            line_held,
+            sum_send.at[i],
+            sum_recv.at[i],
+            load_sem,
+        )
+        for i, parts in enumerate((down_term_ref, up_term_ref, attn_parts_ref))
+    ]
+    down_sum, up_line, attn_line = line_sums
+
+    def spread(index, own, slot):
+        return LineGather(
+            plane, own, slot, spread_send.at[index], spread_recv.at[index], spread_local.at[index]
+        )
+
+    def stream_spread(item):
+        return spread(
+            item,
+            stream_own.at[item],
+            lambda p: full_ref.at[pl.ds((item * 4 + p) * rows, rows)],
+        )
+
+    def norm_back(item, back):
+        load = pltpu.make_async_copy(x_ref.at[item], x_buf, local_sem.at[0])
+        load.start()
+        load.wait()
+        gain = gain_ref[pl.ds(item, 1), :]
+
+        def some_rows(r, gain_sum):
+            piece = pl.ds(pl.multiple_of(r * 16, 16), 16)
+            x = x_buf[piece, :]
+            inverse = lax.rsqrt(jnp.mean(x * x, axis=-1, keepdims=True) + epsilon)
+            grad = back[piece, :].astype(jnp.float32)
+            scaled = grad * gain
+            mean = jnp.mean(scaled * x, axis=-1, keepdims=True)
+            result = inverse * scaled - x * (inverse * inverse * inverse) * mean
+            if item == 0:
+                result = result + grad_ref[piece, :].astype(jnp.float32)
+            stream_own[item, piece, :] = result.astype(jnp.bfloat16)
+            return gain_sum + jnp.sum(grad * x * inverse, axis=0, keepdims=True)
+
+        gain_grad_ref[pl.ds(item, 1), :] = lax.fori_loop(
+            0, rows // 16, some_rows, jnp.zeros((1, features), jnp.float32)
+        )
+
+    def scatter_of(product, index):
+        return PlaneScatterSteps(
+            column,
+            product,
+            (out_buf, side, chip)
+            + tuple(arriving.at[pl.ds(2 * (index % 2), 2)] for arriving in (from_x, from_y, last)),
+            scatter_send.at[index],
+            scatter_recv.at[index],
+        )
+
+    def projection_product(stream, grad):
+        def product(owner, target):
+            left = pl.ds(pl.multiple_of(owner * rows, 16), rows)
+
+            def one_tile(t, carry):
+                lanes = pl.ds(pl.multiple_of(t * tile, tile), tile)
+                target[:, lanes] = lax.dot_general(
+                    grad[left, :],
+                    attn_columns_ref[stream, lanes, :],
+                    contract_cols,
+                    preferred_element_type=jnp.float32,
+                ).astype(jnp.bfloat16)
+                return carry
+
+            lax.fori_loop(0, features // tile, one_tile, 0)
+
+        return product
+
+    def branch_product(owner, target):
+        left = pl.ds(pl.multiple_of(owner * rows, 16), rows)
+
+        def one_tile(t, carry):
+            lanes = pl.ds(pl.multiple_of(t * tile, tile), tile)
+            target[:, lanes] = (
+                matmul(att[left, :], w_out_ref[:, lanes])
+                + matmul(hidden_ref[left, :], w_down_ref[:, lanes])
+            ).astype(jnp.bfloat16)
+            return carry
+
+        lax.fori_loop(0, features // tile, one_tile, 0)
+
+    def attend(first, count):
+        def one_column(m, carry):
+            attend_column(
+                m,
+                plane,
+                length_ref,
+                cos_ref[...],
+                sin_ref[...],
+                q_ref,
+                k_ref,
+                v_ref,
+                kv_before,
+                out_grad_ref,
+                att,
+                q_grad,
+                kv_grad,
+                kv_before_grad,
+                rows,
+                micro_count,
+                sequence_length,
+            )
+            return carry
+
+        lax.fori_loop(first, first + count, one_column, 0)
+
+    def part_copies(first_row):
+        return [
+            pltpu.make_async_copy(
+                stage.at[pl.ds(p * quarter, quarter)],
+                attn_parts_ref.at[pl.ds(p * 4 * quarter + first_row, quarter)],
+                local_sem.at[4 + p],
+            )
+            for p in range(4)
+        ]
+
+    def load_big(source):
+        copy = pltpu.make_async_copy(source, big, local_sem.at[2])
+        copy.start()
+        return copy
+
+    def attn_term(stream, grad):
+        def one_owner(d, carry):
+            lanes = pl.ds(pl.multiple_of(d * width, width), width)
+            stage[:, lanes] = lax.dot_general(
+                big[:, lanes], grad[...], contract_rows, preferred_element_type=jnp.float32
+            ).astype(jnp.bfloat16)
+            return carry
+
+        lax.fori_loop(0, 8, one_owner, 0)
+        copies = part_copies(stream * quarter)
+        for copy in copies:
+            copy.start()
+        return copies
+
+    def out_term():
+        def one_tile(t, carry):
+            lanes = pl.ds(pl.multiple_of(t * tile, tile), tile)
+            stage[:, lanes] = lax.dot_general(
+                att[...], big[:, lanes], contract_rows, preferred_element_type=jnp.float32
+            ).astype(jnp.bfloat16)
+            return carry
+
+        lax.fori_loop(0, features // tile, one_tile, 0)
+        copies = part_copies(3 * quarter)
+        for copy in copies:
+            copy.start()
+        return copies
+
+    def swap(kind):
+        copies = []
+        for mask in (6, 7, 2, 3, 4, 5, 1):
+            owner = partner(column, mask)
+            if kind == 0:
+                source, target = up_piece(owner), up_target()
+            else:
+                source, target = attn_piece(owner), attn_target()
+            copies.append(
+                push(
+                    source,
+                    target,
+                    swap_send.at[8 * kind + mask],
+                    swap_recv.at[8 * kind + mask],
+                    owner,
+                )
+            )
+        if kind == 0:
+            source, target = up_piece(column), up_target()
+        else:
+            source, target = attn_piece(column), attn_target()
+        local = pltpu.make_async_copy(source, target, local_sem.at[3])
+        local.start()
+        return copies, local
+
+    def up_piece(owner):
+        return up_sum.at[
+            pl.ds(pl.multiple_of(lax.rem(owner, 4) * quarter, 16), quarter),
+            pl.ds(pl.multiple_of(lax.div(owner, 4) * ff_share, 128), ff_share),
+        ]
+
+    def up_target():
+        return up_own.at[:, pl.ds(pl.multiple_of(column * ff_share, 128), ff_share)]
+
+    def attn_piece(owner):
+        return attn_sum.at[
+            pl.ds(0, 3 * quarter), pl.ds(pl.multiple_of(owner * width, 128), width)
+        ]
+
+    def attn_target():
+        return quarter_ref.at[
+            pl.ds(0, 3 * quarter), pl.ds(pl.multiple_of(column * width, 128), width)
+        ]
+
+    def swapped_in(swapping):
+        copies, local = swapping
+        for copy in copies:
+            copy.wait_recv()
+        local.wait()
+        for copy in copies:
+            copy.wait_send()
+
+    down_sum.start()
+    norm_back(0, back3_ref)
+    spread3 = stream_spread(0)
+    spread3.service(0)
+
+    @pl.when(plane == 0)
+    def _():
+        clear(kv_before)
+        clear(line_ends.at[0])
+
+    @pl.when(plane == 3)
+    def _():
+        clear(kv_after)
+        clear(line_ends.at[1])
+
+    down_sum.service(0)
+    spread3.service(1)
+    down_sum.service(1)
+    for place in range(1, 4):
+
+        @pl.when(plane == place)
+        def _():
+            for copy in key_copies(place - 1):
+                copy.wait_recv()
+
+    attend(0, 4)
+    spread3.service(2)
+    down_sum.service(2)
+    up_line.start()
+    down_sum.finish(down_own)
+    down_spread = spread(4, down_own, lambda p: down_all_ref.at[pl.ds(p * 4 * quarter, 4 * quarter)])
+    down_spread.service(0)
+    attend(4, 4)
+    for place in range(1, 4):
+
+        @pl.when(plane == place)
+        def _():
+            back_copy(place).start()
+
+    spread3.service(3)
+    loading = load_big(normed_ref.at[0])
+    query_scatter = scatter_of(projection_product(0, q_grad), 0)
+    query_scatter.block(0)
+    query_scatter.block(1)
+    up_line.service(0)
+    query_scatter.block(2)
+    query_scatter.block(3)
+    down_spread.service(1)
+    query_scatter.turn()
+    loading.wait()
+    parts_out = attn_term(0, q_grad)
+    query_scatter.finish(back_buf)
+    up_line.service(1)
+    norm_back(1, back_buf)
+    query_spread = stream_spread(1)
+    query_spread.service(0)
+    down_spread.service(2)
+    for copy in parts_out:
+        copy.wait()
+    loading = load_big(grad_all_ref)
+    branch_scatter = scatter_of(branch_product, 1)
+    branch_scatter.block(0)
+    branch_scatter.block(1)
+    up_line.service(2)
+    up_line.finish(up_sum)
+    up_swap = swap(0)
+    branch_scatter.block(2)
+    down_spread.service(3)
+    branch_scatter.block(3)
+    query_spread.service(1)
+    branch_scatter.turn()
+    loading.wait()
+    parts_out = out_term()
+    branch_scatter.finish(branch_ref)
+    swapped_in(up_swap)
+    up_spread = spread(5, up_own, lambda p: up_all_ref.at[pl.ds(p * quarter, quarter)])
+    up_spread.service(0)
+    for copy in parts_out:
+        copy.wait()
+    loading = load_big(normed_ref.at[1])
+
+    for place in range(3):
+
+        @pl.when(plane == place)
+        def _():
+            back_copy(place + 1).wait_recv()
+
+    def key_value(m, carry):
+        here = pl.ds(pl.multiple_of(m * rows, 16), rows)
+        for head in range(width // HEAD_DIM):
+            lanes = slice(head * HEAD_DIM, (head + 1) * HEAD_DIM)
+            value_lanes = slice(width + head * HEAD_DIM, width + (head + 1) * HEAD_DIM)
+            grad = kv_grad[here, lanes] + kv_after[here, lanes].astype(jnp.float32)
+            turned_half = jnp.concatenate(
+                [grad[:, HEAD_DIM // 2 :], grad[:, : HEAD_DIM // 2]], axis=1
+            )
+            k_grad[here, lanes] = (grad * cos_ref[...] - turned_half * sin_ref[...]).astype(
+                jnp.bfloat16
+            )
+            v_grad[here, lanes] = (
+                kv_grad[here, value_lanes] + kv_after[here, value_lanes].astype(jnp.float32)
+            ).astype(jnp.bfloat16)
+        return carry
+
+    lax.fori_loop(0, 8, key_value, 0)
+    query_spread.service(2)
+    key_scatter = scatter_of(projection_product(1, k_grad), 2)
+    key_scatter.block(0)
+    key_scatter.block(1)
+    key_scatter.block(2)
+    key_scatter.block(3)
+    up_spread.service(1)
+    query_spread.service(3)
+    key_scatter.turn()
+    loading.wait()
+    parts_out = attn_term(1, k_grad)
+    key_scatter.finish(back_buf)
+    norm_back(2, back_buf)
+    key_spread = stream_spread(2)
+    key_spread.service(0)
+    for copy in parts_out:
+        copy.wait()
+    loading = load_big(normed_ref.at[2])
+    up_spread.service(2)
+    value_scatter = scatter_of(projection_product(2, v_grad), 3)
+    value_scatter.block(0)
+    value_scatter.block(1)
+    loading.wait()
+    parts_out = attn_term(2, v_grad)
+    for copy in parts_out:
+        copy.wait()
+    attn_line.start()
+    key_spread.service(1)
+    value_scatter.block(2)
+    value_scatter.block(3)
+    up_spread.service(3)
+    attn_line.service(0)
+    value_scatter.turn()
+    key_spread.service(2)
+    value_scatter.finish(back_buf)
+    norm_back(3, back_buf)
+    value_spread = stream_spread(3)
+    value_spread.service(0)
+    attn_line.service(1)
+    key_spread.service(3)
+    value_spread.service(1)
+    attn_line.service(2)
+    attn_line.finish(attn_sum)
+    attn_swap = swap(1)
+    quarter_ref[pl.ds(3 * quarter, quarter), :] = attn_sum[pl.ds(3 * quarter, quarter), :]
+    value_spread.service(2)
+    swapped_in(attn_swap)
+    value_spread.service(3)
+    for spreading in (
+        spread3,
+        down_spread,
+        query_spread,
+        up_spread,
+        key_spread,
+        value_spread,
+    ):
+        spreading.finish()
+    for place in range(3):
+
+        @pl.when(plane == place)
+        def _():
+            for copy in key_copies(place):
+                copy.wait_send()
+
+    for place in range(1, 4):
+
+        @pl.when(plane == place)
+        def _():
+            back_copy(place).wait_send()
+
+
+def attend_and_back(
+    lengths_all,
+    cosine,
+    sine_part,
+    q,
+    k,
+    v,
+    out_grad,
+    normed_all,
+    grad_all,
+    hidden,
+    w_out,
+    w_down,
+    attn_columns,
+    x_ordered,
+    gains,
+    grad_low,
+    back3,
+    down_term,
+    up_term,
+    micro_count,
+    sequence_length,
+):
+    rows, features = grad_low.shape
+    total, width = q.shape
+    ff_share = w_down.shape[0]
+    quarter = features // 32
+    block = (rows, features)
+    piece = (4 * quarter, features)
+    half = (4, rows // 2, features)
+    anywhere = pl.BlockSpec(memory_space=pl.ANY)
+    near = pl.BlockSpec(memory_space=pltpu.VMEM)
+    shape = jax.ShapeDtypeStruct
+    low_type = jnp.bfloat16
+    some = lambda *dims: pltpu.VMEM(dims, low_type)
+    dma = pltpu.SemaphoreType.DMA
+    return pl.pallas_call(
+        functools.partial(
+            backward_kernel, micro_count=micro_count, sequence_length=sequence_length
+        ),
+        in_specs=[pl.BlockSpec(memory_space=pltpu.SMEM)]
+        + [near] * 6
+        + [anywhere, anywhere]
+        + [near] * 4
+        + [anywhere]
+        + [near] * 3
+        + [anywhere, anywhere],
+        out_specs=[anywhere, anywhere, anywhere, near, near, near, anywhere, anywhere],
+        out_shape=[
+            shape((16 * rows, features), low_type),
+            shape((ff_share, features), low_type),
+            shape((4 * quarter, 8 * ff_share), low_type),
+            shape(piece, low_type),
+            shape(block, low_type),
+            shape((8, features), jnp.float32),
+            shape((16 * quarter, features), low_type),
+            shape((18,) + piece, low_type),
+        ],
+        scratch_shapes=[
+            some(total, features),
+            some(total, width),
+            some(total, width),
+            pltpu.VMEM((total, 2 * width), jnp.float32),
+            some(total, 2 * width),
+            some(total, 2 * width),
+            some(total, 2 * width),
+            some(4, *block),
+            some(4, *block),
+            some(4, *block),
+            some(*half),
+            some(*half),
+            some(*half),
+            some(*piece),
+            some(2, *piece),
+            some(3, *piece),
+            some(*piece),
+            some(*piece),
+            some(quarter, 8 * ff_share),
+            some(4, *block),
+            some(*block),
+            pltpu.VMEM(block, jnp.float32),
+            some(*piece),
+            dma((4, 10)),
+            dma((4, 10)),
+            dma((3, 6)),
+            dma((3, 6)),
+            dma((2,)),
+            dma((6, 6)),
+            dma((6, 6)),
+            dma((6,)),
+            dma((3,)),
+            dma((3,)),
+            dma((16,)),
+            dma((16,)),
+            dma((8,)),
+        ],
+        compiler_params=pltpu.CompilerParams(
+            collective_id=6, has_side_effects=True, vmem_limit_bytes=63 * 1024 * 1024
+        ),
+        cost_estimate=pl.CostEstimate(
+            flops=20 * total * features * width,
+            bytes_accessed=1000 * 1000 * 1000,
+            transcendentals=0,
+        ),
+    )(
+        lengths_all,
+        cosine,
+        sine_part,
+        q,
+        k,
+        v,
+        out_grad,
+        normed_all,
+        grad_all,
+        hidden,
+        w_out,
+        w_down,
+        attn_columns,
+        x_ordered,
+        gains,
+        grad_low,
+        back3,
+        down_term,
+        up_term,
+    )
+
+
+def rotary_table(row_positions, head_dim):
+    half_dim = head_dim // 2
+    frequency = jnp.exp(
+        jnp.arange(half_dim, dtype=jnp.float32) * (-2.0 * math.log(10000.0) / head_dim)
+    )
+    angles = row_positions.astype(jnp.float32)[:, None] * frequency[None, :]
+    cosine = jnp.cos(angles)
+    sine_part = jnp.sin(angles)
+    return (
+        jnp.concatenate([cosine, cosine], axis=-1),
+        jnp.concatenate([-sine_part, sine_part], axis=-1),
+    )
+
+
+def turned(values, cosine, sine_part, rows, sign):
+    total, width = values.shape
+    heads = values.reshape(total // rows, rows, width // HEAD_DIM, HEAD_DIM)
+    swapped = jnp.concatenate(
+        [heads[..., HEAD_DIM // 2 :], heads[..., : HEAD_DIM // 2]], axis=-1
+    )
+    return (
+        heads * cosine[None, :, None, :] + sign * swapped * sine_part[None, :, None, :]
+    ).reshape(total, width)
+
+
+def shards_split(
+    history,
+    history_layer_index,
+    lengths,
+    norm_gains,
+    mix_in,
+    mix_out,
+    w_attn,
+    w_out,
+    w_up,
+    w_down,
+    cotangent,
+):
+    local_slots, micro_count, sequence_length, features = history.shape
+    planes = lax.axis_size("hist")
+    columns = lax.axis_size("dp")
+    plane = lax.axis_index("hist")
+    slot_count = local_slots * planes
+    all_rows = micro_count * sequence_length
+    rows = all_rows // planes
+    share = features // columns
+    mix_width = mix_in.shape[1]
+    ff_share = w_down.shape[0]
+    low = lambda values: values.astype(jnp.bfloat16)
+
+    top = jnp.concatenate(
+        [mix_in, norm_gains.T, jnp.zeros((share, 128 - mix_width - 5), jnp.bfloat16)], axis=1
+    )
+    mix_rows = mix_out.shape[0]
+    bottom = jnp.zeros((16, 128), jnp.bfloat16)
+    bottom = bottom.at[:mix_rows, :mix_width].set(mix_out)
+    bottom = bottom.at[0, mix_width : mix_width + micro_count].set(low(lengths))
+    packed = lax.all_gather(jnp.concatenate([top, bottom], axis=0), "dp", axis=0, tiled=False)
+    mix_in_all = packed[:, :share, :mix_width].reshape(features, mix_width)
+    gains_all = (
+        packed[:, :share, mix_width : mix_width + 5].reshape(features, 5).astype(jnp.float32).T
+    )
+    mixer_output_wide = (
+        packed[:, share : share + mix_rows, :mix_width]
+        .reshape(mix_width, mix_width)
+        .astype(jnp.float32)
+    )
+    lengths_all = (
+        packed[:, share, mix_width : mix_width + micro_count].reshape(-1).astype(jnp.int32)
+    )
+
+    chunk = sequence_length // planes
+    inverse_step = pow(micro_count, -1, planes)
+    received = []
+    for i in range(micro_count):
+        target = lax.rem((plane - i + planes * micro_count) * inverse_step, planes)
+        which = lax.div(target * micro_count + i, planes)
+        piece = lax.dynamic_index_in_dim(cotangent, which, 0, keepdims=False)
+        pairs = [(t, ((t - i) * inverse_step) % planes) for t in range(planes)]
+        received.append(lax.ppermute(piece, "hist", pairs))
+    my_row = plane * rows + jnp.arange(rows, dtype=jnp.int32)
+    my_position = lax.rem(my_row, sequence_length)
+    my_sequence = lax.div(my_row, sequence_length)
+    my_length = jnp.sum(
+        jnp.where(
+            my_sequence[:, None] == jnp.arange(micro_count, dtype=jnp.int32)[None, :],
+            lengths[None, :],
+            0,
+        ),
+        axis=1,
+    )
+    valid_rows = (my_position < my_length).astype(jnp.float32)[:, None]
+    grad_rows = jnp.concatenate(received, axis=0).astype(jnp.float32) * valid_rows
+
+    layer_lookup = (
+        history_layer_index[:, None] == jnp.arange(slot_count, dtype=jnp.int32)[None, :]
+    ).astype(jnp.float32)
+    newest_output = jnp.sum(
+        jnp.arange(slot_count, dtype=jnp.int32)
+        * (history_layer_index == slot_count - 1).astype(jnp.int32)
+    )
+    root = newest_output // local_slots
+    on_root = (plane == root).astype(jnp.float32)
+    latest_local = lax.dynamic_index_in_dim(history, newest_output % local_slots, 0, keepdims=False)
+    dyn_local, kept_mix = mix_forward(
+        latest_local.reshape(all_rows, features), gains_all[0], mix_in_all, mixer_output_wide
+    )
+    dyn_every = lax.all_gather(dyn_local, "hist", axis=0, tiled=False)
+    dyn = lax.dynamic_index_in_dim(dyn_every, root, 0, keepdims=False)
+    own_table = lax.dynamic_slice_in_dim(layer_lookup, plane * local_slots, local_slots, 0)
+    factors = jnp.einsum(
+        "tcj,sj->sct",
+        dyn.reshape(all_rows, STREAM_COUNT, slot_count),
+        own_table,
+        precision=highest,
+    )
+    flat_history = history.reshape(local_slots, all_rows, features)
+
+    def mixed(stream):
+        total = jnp.zeros((all_rows, features), jnp.float32)
+        for slot in range(local_slots):
+            total = total + factors[slot, stream][:, None] * flat_history[slot].astype(jnp.float32)
+        return low(total)
+
+    order = (3, 0, 1, 2)
+    parts = jnp.concatenate([mixed(stream) for stream in order], axis=0)
+    gains_ordered = jnp.pad(jnp.stack([gains_all[stream + 1] for stream in order]), ((0, 4), (0, 0)))
+    (
+        x_ordered,
+        normed_all,
+        grad_all,
+        hidden,
+        up_term,
+        down_term,
+        back3,
+        attn_columns,
+        _,
+    ) = forward_and_feed(parts, low(grad_rows), w_up, w_attn, w_down, gains_ordered)
+    normed = [normed_all[0], normed_all[1], normed_all[2]]
+
+    cosine, sine_part = rotary_table(my_position, HEAD_DIM)
+    att_grad = low(
+        lax.dot_general(grad_all, w_out, contract_cols, preferred_element_type=jnp.float32)
+    )
+    q = low(turned(matmul(normed[0], attn_columns[0]), cosine, sine_part, rows, 1.0))
+    k = low(turned(matmul(normed[1], attn_columns[1]), cosine, sine_part, rows, 1.0))
+    v = low(matmul(normed[2], attn_columns[2]))
+    full, down_all, up_all, attn_quarter, branch, gain_sums, _, _ = attend_and_back(
+        lengths_all,
+        cosine,
+        sine_part,
+        q,
+        k,
+        v,
+        att_grad,
+        normed_all,
+        grad_all,
+        hidden,
+        w_out,
+        w_down,
+        attn_columns,
+        x_ordered,
+        gains_ordered,
+        low(grad_rows),
+        back3,
+        down_term,
+        up_term,
+        micro_count,
+        sequence_length,
+    )
+    block_rows = low((x_ordered[0] + branch.astype(jnp.float32)) * valid_rows)
+    block_out = jnp.zeros((micro_count, chunk, features), jnp.bfloat16)
+    for i in range(micro_count):
+        pairs = [(p, (micro_count * p + i) % planes) for p in range(planes)]
+        piece = lax.ppermute(block_rows[i * chunk : (i + 1) * chunk], "hist", pairs)
+        source = lax.rem((plane - i + planes * micro_count) * inverse_step, planes)
+        which = lax.div(source * micro_count + i, planes)
+        block_out = lax.dynamic_update_index_in_dim(block_out, piece, which, 0)
+
+    full_ordered = full.reshape(STREAM_COUNT, all_rows, features)
+    full_grads = [
+        full_ordered[order.index(stream)].astype(jnp.float32) for stream in range(STREAM_COUNT)
+    ]
+    inner = jnp.stack(
+        [
+            jnp.stack(
+                [
+                    jnp.sum(full_grads[stream] * flat_history[slot].astype(jnp.float32), axis=-1)
+                    for slot in range(local_slots)
+                ],
+                axis=-1,
+            )
+            for stream in range(STREAM_COUNT)
+        ],
+        axis=1,
+    )
+    dyn_part = jnp.einsum("tcs,sj->tcj", inner, own_table, precision=highest)
+    dyn_grad = jnp.sum(
+        lax.all_gather(
+            dyn_part.reshape(all_rows, STREAM_COUNT * slot_count), "hist", axis=0, tiled=False
+        ),
+        axis=0,
+    )
+    act_grad = precise(dyn_grad, mixer_output_wide.T)
+    mix_out_grad = precise(kept_mix[4].T, dyn_grad) * on_root
+    latest_grad, gain_zero, mix_in_grad = mix_backward(kept_mix, act_grad, gains_all[0], mix_in_all)
+    slot_grads = []
+    for slot in range(local_slots):
+        is_latest = (plane * local_slots + slot == newest_output).astype(jnp.float32)
+        slot_grad = latest_grad * is_latest
+        for stream in range(STREAM_COUNT):
+            slot_grad = slot_grad + factors[slot, stream][:, None] * full_grads[stream]
+        slot_grads.append(low(slot_grad))
+    history_grad = jnp.stack(slot_grads).reshape(history.shape)
+
+    attn_every = lax.all_gather(attn_quarter, "hist", axis=0, tiled=False).astype(jnp.float32)
+    part = share // planes
+    w_attn_grad = (
+        attn_every[:, : 3 * part]
+        .reshape(planes, 3, part, features)
+        .transpose(1, 0, 2, 3)
+        .reshape(3, share, features)
+    )
+    w_out_grad = attn_every[:, 3 * part :].reshape(share, features)
+    w_down_grad = down_all.astype(jnp.float32)
+    w_up_grad = up_all.astype(jnp.float32)
+
+    small_top = jnp.concatenate(
+        [
+            mix_in_grad * on_root,
+            jnp.stack(
+                [gain_zero * on_root]
+                + [gain_sums[order.index(stream)] for stream in range(STREAM_COUNT)]
+            ).T,
+            jnp.zeros((features, 128 - mix_width - 5), jnp.float32),
+        ],
+        axis=1,
+    ).reshape(columns, share, 128)
+    small_bottom = jnp.pad(
+        mix_out_grad.reshape(columns, mix_rows, mix_width),
+        ((0, 0), (0, 16 - mix_rows), (0, 128 - mix_width)),
+    )
+    small = low(jnp.concatenate([small_top, small_bottom], axis=1))
+    small = lax.psum_scatter(small, "dp", scatter_dimension=0, tiled=False)
+    small = lax.psum(small, "hist").astype(jnp.float32)
+    return (
+        block_out,
+        history_grad,
+        small[:share, mix_width : mix_width + 5].T,
+        small[:share, :mix_width],
+        small[share : share + mix_rows, :mix_width],
+        w_attn_grad,
+        w_out_grad,
+        w_up_grad,
+        w_down_grad,
+    )
+
+
+def splits_by_heads(mesh, micro_count, sequence_length):
+    columns, planes = mesh.shape["dp"], mesh.shape["hist"]
+    all_rows = micro_count * sequence_length
+    rows = all_rows // planes
+    return (
+        columns == 8
+        and planes == 4
+        and HEADS % columns == 0
+        and all_rows % planes == 0
+        and sequence_length % planes == 0
+        and rows % 64 == 0
+        and math.gcd(micro_count, planes) == 1
+        and all(
+            (p * rows) // sequence_length * sequence_length >= (p - 1) * rows
+            for p in range(planes)
+        )
+    )
+
+
 def solution(mesh):
     placed = (
         P("hist", "dp", None, None),
@@ -479,8 +2317,14 @@
         P("dp", None),
         P("dp", "hist", None),
     )
+    def plan(*arrays):
+        micro_count = arrays[2].shape[0]
+        if splits_by_heads(mesh, micro_count, arrays[0].shape[2]):
+            return shards_split(*arrays)
+        return shards(*arrays)
+
     return jax.shard_map(
-        shards,
+        plan,
         mesh=mesh,
         in_specs=placed,
         out_specs=(

time: 2700 us -> 1250 us (0.46)
  waiting for transfers between devices: 1840 us -> 102 us
  Pallas kernels: 0 us -> 836 us
  local copies, waits for them, and re-layouts: 387 us -> 60.9 us
  matrix products: 231 us -> 31.4 us
  other arithmetic: 181 us -> 127 us
    pallas_call x0 -> x2, Pallas kernels: none -> 836 us  [the longest x1 537 us: attend_and_back(): pl.pallas_call(functools.partial(backward_kernel, micro_count=micro_count...]
    reduce_scatter x5 -> x1, waiting for transfers between devices: 831 us -> 31.5 us  [shards_split(): small = lax.psum_scatter(small, 'dp', scatter_dimension=0, tiled=False)]
    all_gather x9 -> x1, waiting for transfers between devices: 546 us -> 57.1 us  [shards_split(): lax.all_gather(attn_quarter, 'hist', axis=0, tiled=False)]
    psum x3 -> x1, waiting for transfers between devices: 458 us -> 0.02 us  [shards_split(): small = lax.psum(small, 'hist').astype(jnp.float32)]
    concatenate x1, local copies, waits for them, and re-layouts: 155 us -> 0.59 us  [shards_split(): jnp.concatenate([mix_in_grad * on_root, jnp.stack([gain_zero * on_root] +...]
    dot_general x19 -> x3, matrix products: 155 us -> 3.39 us  [the longest x1 2.79 us: shards_split(): lax.dot_general(grad_all, w_out, contract_cols, preferred_element_type=jn...]
    reshape x6 -> x2, local copies, waits for them, and re-layouts: 132 us -> 5.17 us  [the longest x1 3.13 us: shards_split(): w_attn_grad = attn_every[:, :3 * part].reshape(planes, 3, part, features)...]
    dot_general x7 -> x4, matrix products: 60.9 us -> 16.2 us  [matmul(): return jnp.dot(left_side, right_side, preferred_element_type=jnp.float32)]
  transfers between devices with their start and end apart: 17 -> 9, of which waited for: 11 -> 4; matrix products, arithmetic and copies ran while one was open for 24% -> 10% of each run, Pallas kernels for 0% -> 0%
where the time goes in v2:
time: 1250 us; the launch traced here: 1240 us
  Pallas kernels  836 us (67%)
  other arithmetic  127 us (10%)
  waiting for transfers between devices  102 us (8%)
  local copies, waits for them, and re-layouts  60.9 us (5%)
  blocking collectives  46.7 us (4%)
  matrix products  31.4 us (3%)
  between operations  20.6 us (2%)
  starting transfers between devices  17.8 us (1%)
    pallas_call x1, Pallas kernels, attend_and_back(): pl.pallas_call(functools.partial(backward_kernel, micro_count=micro_count...  537 us
    pallas_call x1, Pallas kernels, forward_and_feed(): pl.pallas_call(forward_kernel, in_specs=[anywhere, near, anywhere, anywhe...  299 us
    all_gather x1, waiting for transfers between devices, shards_split(): lax.all_gather(attn_quarter, 'hist', axis=0, tiled=False)  57.1 us
    convert_element_type x8, other arithmetic, shards_split(): low = lambda values: values.astype(jnp.bfloat16)  43.1 us
    reduce_scatter x1, waiting for transfers between devices, shards_split(): small = lax.psum_scatter(small, 'dp', scatter_dimension=0, tiled=False)  31.5 us
    concatenate x1, other arithmetic, shards_split(): parts = jnp.concatenate([mixed(stream) for stream in order], axis=0)  27.4 us
  transfers between devices with their start and end apart: 9, of which 4 were waited for; matrix products, arithmetic and copies ran while one was open for 10% of the time, Pallas kernels for 0%

profile of v2, /device:TPU:0, one launch (start us, length us, event | category | flops | bytes accessed | tf_op | source)
XLA Modules:
  0.0 1242.0 jit_solution(4590527983746291597)
XLA Ops:
  9.3 3.6 collective-permute-start
  12.9 4.0 collective-permute-start.1
  31.0 10.0 all-gather
  44.0 7.8 fusion.115
  51.8 3.7 fusion.52
  63.2 19.9 %all-gather.1 = f32[3072,64]{0,1:T(8,128)} all-gather(f32[768,64]{0,1:T(8,128)S(1)} %fusion.103), channel_id=3, replica_groups=mesh['dp'=8,'hist'=4] {'hist'}, dimensions={0}, use_global_device_ids=true | all-gather | bytes 983040 | tf_op jit(solution)/shard_map/all_gather | solution.py:2136
  91.0 6.1 fusion.27
  97.5 8.4 fusion.23
  105.9 27.4 %pad_maximum_fusion.part_ref = bf16[3072,2048]{1,0:T(8,128)(2,1)} fusion(bf16[768,2048]{1,0:T(8,128)(2,1)S(1)} %get-tuple-element.165, bf16[768,2048]{1,0:T(8,128)(2,1)S(1)} %get-tuple-element.166, bf16[768,2048]{1,0:T(8,128)(2,1)S(1)} %fusion.27, bf16[768,2048]{1,0:T(8,128)(2,1)S(1)} %get-tuple-element.164), kind=kLoop, calls=%fused_computation.48 | loop fusion | flops 50331648 | bytes 25165824 | tf_op jit(solution)/shard_map/concatenate | solution.py:2154
  138.9 298.5 %shard_map.178 = (f32[4,192,2048]{2,1,0:T(8,128)}, bf16[3,1536,2048]{2,1,0:T(8,128)(2,1)}, bf16[1536,2048]{1,0:T(8,128)(2,1)}, bf16[1536,1024]{1,0:T(8,128)(2,1)...) custom-call(bf16[3072,2048]{1,0:T(8,128)(2,1)} %pad_maximum_fusion.p, ...), custom_call_target="tpu_custom_call" | custom-call | flops 38654705664 | bytes 400000000 | tf_op jit(solution)/shard_map/pallas_call | solution.py:1108
  437.4 10.9 fusion.114
  448.3 5.5 fusion.65.v_ref
  455.5 4.0 fusion.121
  463.4 4.8 fusion.122
  476.4 537.3 %shard_map.179 = (bf16[3072,2048]{1,0:T(8,128)(2,1)}, bf16[1024,2048]{1,0:T(8,128)(2,1)}, bf16[256,8192]{1,0:T(8,128)(2,1)}, bf16[256,2048]{1,0:T(8,128)(2,1)}, ...) custom-call(s32[24]{0:T(128)} %reshape.279.length_ref, ...), custom_call_target="tpu_custom_call" | custom-call | flops 16106127360 | bytes 1000000000 | tf_op jit(solution)/shard_map/pallas_call | solution.py:1938
  1015.7 13.9 %fusion.40 = (f32[768]{0:T(1024)S(1)}, f32[768]{0:T(1024)S(1)}, f32[768]{0:T(1024)S(1)}, f32[768]{0:T(1024)S(1)}, f32[768]{0:T(1024)S(1)}, /*index=5*/f32[768]{0...) fusion(bf16[1,3,256,2048]{3,2,1,0:T(8,128)(2,1)} %get-tuple-ele, ...), kind=kLoop, calls=%fused_computation.90 | loop fusion | flops 62902272 | bytes 25214976 | tf_op jit(solution)/shard_map/reduce_sum | solution.py:2216
  1030.3 16.7 %all_gather.25 = f32[4,768,64]{1,2,0:T(8,128)S(1)} all-gather(f32[1,768,64]{1,2,0:T(8,128)S(1)} %bitcast.230), channel_id=1, replica_groups=mesh['dp'=8,'hist'=4] {'hist'}, dimensions={0}, use_global_device_ids=true | all-gather | bytes 983040 | tf_op jit(solution)/shard_map/all_gather | solution.py:2227
  1048.2 6.7 fusion.61
  1056.2 7.3 fusion.59
  1070.4 31.5 %reduce-scatter.2.cloned.1.call-done = bf16[1,272,128]{2,1,0:T(8,128)(2,1)} async-done(((bf16[8,272,128]{2,1,0:T(8,128)(2,1)}), bf16[1,272,128]{2,1,0:T(8,128)(2,1)}) %reduce-scatter.2.cloned.1.call-update) | async-done | bytes 69648 | tf_op jit(solution)/shard_map/reduce_scatter | solution.py:2272
  1107.0 12.0 fusion.4
  1119.2 5.7 fusion.14
  1124.9 5.7 fusion.19
  1130.6 5.7 pad_maximum_fusion.1
  1136.3 4.4 convert_element_type.247
  1140.7 4.4 convert_element_type.248
  1145.2 2.9 collective-permute-start.4
  1148.1 3.8 collective-permute-start.5
  1152.1 12.2 collective-permute-done.4
  1170.2 57.1 %all-gather.5.cloned.1.call-done = bf16[1024,2048]{1,0:T(8,128)(2,1)} async-done(((bf16[256,2048]{1,0:T(8,128)(2,1)}), bf16[1024,2048]{1,0:T(8,128)(2,1)}) %all-gather.5.cloned.1.call-update) | async-done | bytes 4194320 | tf_op jit(solution)/shard_map/all_gather | solution.py:2244
  1227.3 2.9 slice.348
  1232.0 3.1 copy.71
  (256 shorter events, 73.6 us)
Async XLA Ops:
  7.2 1094.7 %reduce-scatter.2.cloned.1.call-start = ((), (), s32[]{:S(2)}) async-start(), calls=%async_computation.1 | async-start | bytes 626688 | tf_op jit(solution)/shard_map/reduce_scatter | solution.py:2272
  9.3 127.4 %collective-permute-start = (bf16[64,2048]{1,0:T(8,128)(2,1)}, bf16[64,2048]{1,0:T(8,128)(2,1)}, u32[]{:S(2)}, u32[]{:S(2)}) collective-permute-start(bf16[64,2048]{1,0:T(8,128)(2,1)} %get-tuple-element.180), channel_id=1, source_target_pairs={{0,0},{1,3},{2,2},{3,1},{4,4},{5,7},{6,6},{7,5},{8,8},{9,11},{10,1... | collective-permute-start | bytes 786440 | tf_op jit(solution)/shard_map/ppermute | solution.py:2108
  12.9 123.8 %collective-permute-start.1 = (bf16[64,2048]{1,0:T(8,128)(2,1)}, bf16[64,2048]{1,0:T(8,128)(2,1)}, u32[]{:S(2)}, u32[]{:S(2)}) collective-permute-start(bf16[64,2048]{1,0:T(8,128)(2,1)} %get-tuple-element.182), channel_id=1, source_target_pairs={{0,1},{1,0},{2,3},{3,2},{4,5},{5,4},{6,7},{7,6},{8,9},{9,8},{10,11... | collective-permute-start | bytes 786440 | tf_op jit(solution)/shard_map/ppermute | solution.py:2108
  16.9 119.8 %collective-permute-start.2 = (bf16[64,2048]{1,0:T(8,128)(2,1)}, bf16[64,2048]{1,0:T(8,128)(2,1)}, u32[]{:S(2)}, u32[]{:S(2)}) collective-permute-start(bf16[64,2048]{1,0:T(8,128)(2,1)} %get-tuple-element.181), channel_id=1, source_target_pairs={{0,2},{1,1},{2,0},{3,3},{4,6},{5,5},{6,4},{7,7},{8,10},{9,9},{10,8... | collective-permute-start | bytes 786440 | tf_op jit(solution)/shard_map/ppermute | solution.py:2108
  51.8 45.3 %copy-start.2 = (bf16[1,3,256,2048]{3,2,1,0:T(8,128)(2,1)}, bf16[1,3,256,2048]{3,2,1,0:T(8,128)(2,1)S(1)}, u32[]{:S(2)}) copy-start(bf16[1,3,256,2048]{3,2,1,0:T(8,128)(2,1)S(1)} %get-tuple-element.167) | copy-start | bytes 9437188
  60.2 28.7 %copy-start.57 = (s32[3]{0:T(128)S(1)}, s32[3]{0:T(128)}, u32[]{:S(2)}) copy-start(s32[3]{0:T(128)} %param.17) | copy-start | bytes 40
  90.7 378.0 %copy-start.15 = (f32[192,128]{1,0:T(8,128)}, f32[192,128]{1,0:T(8,128)S(1)}, u32[]{:S(2)}) copy-start(f32[192,128]{1,0:T(8,128)S(1)} %pad_maximum_fusion.2.cos_ref) | copy-start | bytes 294916
  90.8 377.9 %copy-start.16 = (f32[192,128]{1,0:T(8,128)}, f32[192,128]{1,0:T(8,128)S(1)}, u32[]{:S(2)}) copy-start(f32[192,128]{1,0:T(8,128)S(1)} %pad_maximum_fusion.3.sin_ref) | copy-start | bytes 294916
  105.9 28.2 %copy-start.18 = (f32[1,5,8,256]{3,1,2,0:T(8,128)S(1)}, f32[1,5,8,256]{3,1,2,0:T(8,128)}, u32[]{:S(2)}) copy-start(f32[1,5,8,256]{3,1,2,0:T(8,128)} %copy-done.17) | copy-start | bytes 122884
  105.9 30.1 %copy-start.52 = (f32[1,2048]{1,0:T(1,128)S(1)}, f32[1,2048]{1,0:T(1,128)}, u32[]{:S(2)}) copy-start(f32[1,2048]{1,0:T(1,128)} %get-tuple-element.185) | copy-start | bytes 24580
  105.9 30.7 %copy-start.53 = (f32[192]{0:T(256)S(1)}, f32[192]{0:T(256)}, u32[]{:S(2)}) copy-start(f32[192]{0:T(256)} %compare_convert_fusion) | copy-start | bytes 2308
  1015.7 14.2 %copy-start.56 = (s32[4]{0:T(128)S(1)}, s32[4]{0:T(128)}, u32[]{:S(2)}) copy-start(s32[4]{0:T(128)} %copy-done.55) | copy-start | bytes 52
  1015.7 31.3 %copy-start.60 = (f32[768,64]{0,1:T(8,128)S(1)}, f32[768,64]{0,1:T(8,128)}, u32[]{:S(2)}) copy-start(f32[768,64]{0,1:T(8,128)} %get-tuple-element.193) | copy-start | bytes 589828
  1015.7 32.4 %copy-start.14 = (bf16[8,256,64]{2,1,0:T(8,128)(2,1)S(1)}, bf16[8,256,64]{2,1,0:T(8,128)(2,1)}, u32[]{:S(2)}) copy-start(bf16[8,256,64]{2,1,0:T(8,128)(2,1)} %slice.315) | copy-start | bytes 786436
  1063.6 40.3 %copy-start.54 = (f32[192]{0:T(256)S(1)}, f32[192]{0:T(256)}, u32[]{:S(2)}) copy-start(f32[192]{0:T(256)} %compare_convert_fusion) | copy-start | bytes 2308
  1065.3 41.6 %copy-start.20 = (f32[768]{0:T(1024)S(1)}, f32[768]{0:T(1024)}, u32[]{:S(2)}) copy-start(f32[768]{0:T(1024)} %copy-done.19) | copy-start | bytes 9220
  1065.4 41.6 %copy-start.38 = (f32[768]{0:T(1024)S(1)}, f32[768]{0:T(1024)}, u32[]{:S(2)}) copy-start(f32[768]{0:T(1024)} %get-tuple-element.132) | copy-start | bytes 9220
  1065.4 41.6 %copy-start.40 = (f32[768]{0:T(1024)S(1)}, f32[768]{0:T(1024)}, u32[]{:S(2)}) copy-start(f32[768]{0:T(1024)} %get-tuple-element.136) | copy-start | bytes 9220
  1065.4 41.6 %copy-start.42 = (f32[768]{0:T(1024)S(1)}, f32[768]{0:T(1024)}, u32[]{:S(2)}) copy-start(f32[768]{0:T(1024)} %get-tuple-element.140) | copy-start | bytes 9220
  1065.4 41.6 %copy-start.43 = (f32[768]{0:T(1024)S(1)}, f32[768]{0:T(1024)}, u32[]{:S(2)}) copy-start(f32[768]{0:T(1024)} %get-tuple-element.144) | copy-start | bytes 9220
  1070.4 95.3 %all-reduce.5.cloned.1.call-start = ((), (), s32[]{:S(2)}) async-start(), calls=%async_computation.2 | async-start | bytes 139264 | tf_op jit(solution)/shard_map/psum | solution.py:2273
  1101.9 125.4 %all-gather.5.cloned.1.call-start = ((), (), s32[]{:S(2)}) async-start(), calls=%async_computation.3 | async-start | bytes 5242880 | tf_op jit(solution)/shard_map/all_gather | solution.py:2244
  1105.7 13.3 %slice-start = ((s8[12582912]{0:T(1024)(128)(4,1)}), s8[4194304]{0:T(1024)(128)(4,1)S(1)}, s32[]{:S(2)}) async-start(s8[12582912]{0:T(1024)(128)(4,1)} %bitcast.201), calls=%async_computation.4 | async-start | bytes 8388608
  1105.8 13.3 %slice-start.3 = ((s8[6291456]{0:T(1024)(128)(4,1)}), s8[4194304]{0:T(1024)(128)(4,1)S(1)}, s32[]{:S(2)}) async-start(s8[6291456]{0:T(1024)(128)(4,1)} %bitcast.203), calls=%async_computation.7 | async-start | bytes 8388608
  1105.8 13.3 %slice-start.1 = ((s8[12582912]{0:T(1024)(128)(4,1)}), s8[4194304]{0:T(1024)(128)(4,1)S(1)}, s32[]{:S(2)}) async-start(s8[12582912]{0:T(1024)(128)(4,1)} %bitcast.201), calls=%async_computation.5 | async-start | bytes 8388608
  1105.8 13.3 %slice-start.2 = ((s8[12582912]{0:T(1024)(128)(4,1)}), s8[4194304]{0:T(1024)(128)(4,1)S(1)}, s32[]{:S(2)}) async-start(s8[12582912]{0:T(1024)(128)(4,1)} %bitcast.201), calls=%async_computation.6 | async-start | bytes 8388608
  1105.8 13.3 %slice-start.4 = ((s8[6291456]{0:T(1024)(128)(4,1)}), s8[2097152]{0:T(1024)(128)(4,1)S(1)}, s32[]{:S(2)}) async-start(s8[6291456]{0:T(1024)(128)(4,1)} %bitcast.203), calls=%async_computation.8 | async-start | bytes 4194304
  1105.9 13.3 %copy-start.31 = (f32[768]{0:T(1024)S(1)}, f32[768]{0:T(1024)}, u32[]{:S(2)}) copy-start(f32[768]{0:T(1024)} %get-tuple-element.134) | copy-start | bytes 9220
  1105.9 46.1 %collective-permute-start.3 = (bf16[64,2048]{1,0:T(8,128)(2,1)S(1)}, bf16[64,2048]{1,0:T(8,128)(2,1)S(1)}, u32[]{:S(2)}, u32[]{:S(2)}) collective-permute-start(bf16[64,2048]{1,0:T(8,128)(2,1)S(1)} %get-tuple-element.179), channel_id=1, source_target_pairs={{0,0},{1,3},{2,2},{3,1},{4,4},{5,7},{6,6},{7,5},{8,8},{9,11},{10,1... | collective-permute-start | bytes 786440 | tf_op jit(solution)/shard_map/ppermute | solution.py:2203
  1145.2 19.1 %collective-permute-start.4 = (bf16[64,2048]{1,0:T(8,128)(2,1)S(1)}, bf16[64,2048]{1,0:T(8,128)(2,1)S(1)}, u32[]{:S(2)}, u32[]{:S(2)}) collective-permute-start(bf16[64,2048]{1,0:T(8,128)(2,1)S(1)} %get-tuple-element.178), channel_id=1, source_target_pairs={{0,1},{1,0},{2,3},{3,2},{4,5},{5,4},{6,7},{7,6},{8,9},{9,8},{10,11... | collective-permute-start | bytes 786440 | tf_op jit(solution)/shard_map/ppermute | solution.py:2203
  1148.1 17.5 %collective-permute-start.5 = (bf16[64,2048]{1,0:T(8,128)(2,1)S(1)}, bf16[64,2048]{1,0:T(8,128)(2,1)S(1)}, u32[]{:S(2)}, u32[]{:S(2)}) collective-permute-start(bf16[64,2048]{1,0:T(8,128)(2,1)S(1)} %get-tuple-element.177), channel_id=1, source_target_pairs={{0,2},{1,1},{2,0},{3,3},{4,6},{5,5},{6,4},{7,7},{8,10},{9,9},{10,8... | collective-permute-start | bytes 786440 | tf_op jit(solution)/shard_map/ppermute | solution.py:2203
  1165.6 64.6 %copy-start.12 = (bf16[3,64,2048]{2,1,0:T(8,128)(2,1)}, bf16[3,64,2048]{2,1,0:T(8,128)(2,1)S(1)}, u32[]{:S(2)}) copy-start(bf16[3,64,2048]{2,1,0:T(8,128)(2,1)S(1)} %bitcast_dynamic-update-slice_fusion) | copy-start | bytes 2359300
  (45 other events, 309.9 us)
Sparse Core Ops, SparseCore 0:
  1070.5 31.3 reduce-scatter.1
  1104.3 38.8 all-reduce.4
  1144.8 82.5 all-gather.4

commit v3 on v2

--- a/solution.py
+++ b/solution.py
@@ -481,15 +481,6 @@
     return moved
 
 
-def greet(column, masks):
-    barrier = pltpu.get_barrier_semaphore()
-    for mask in masks:
-        pl.semaphore_signal(
-            barrier, inc=1, device_id={"dp": partner(column, mask)}, device_id_type=DEVICE_MESH
-        )
-    pl.semaphore_wait(barrier, len(masks))
-
-
 def push(source, target, send_sem, recv_sem, place):
     copy = pltpu.make_async_remote_copy(
         src_ref=source,
@@ -586,10 +577,12 @@
 
     def block(self, i):
         mask = (6, 2, 4, 0)[i]
-        self.product(partner(self.column, mask + CORE), self.out_buf.at[i])
+        if i >= 2:
+            self.pair[i - 2].wait_send()
+        self.product(partner(self.column, mask + CORE), self.out_buf.at[i % 2])
         self.pair.append(
             push(
-                self.out_buf.at[i],
+                self.out_buf.at[i % 2],
                 self.side.at[i],
                 self.send_sem.at[i],
                 self.recv_sem.at[i],
@@ -630,8 +623,9 @@
         add_into(self.chip.at[3, self.first], self.last.at[0])
         self.sends[5].wait_recv()
         add_into(self.chip.at[3, self.second], self.last.at[1])
-        out_ref[...] = self.chip[3]
-        for copy in self.pair + self.sends:
+        if out_ref is not None:
+            out_ref[...] = self.chip[3]
+        for copy in self.pair[2:] + self.sends:
             copy.wait_send()
 
 
@@ -763,405 +757,6 @@
                         self.relay(way, sent[-1], a).wait_send()
 
 
-def forward_kernel(
-    part_ref,
-    grad_ref,
-    w_up_ref,
-    w_attn_ref,
-    w_down_ref,
-    gain_ref,
-    x_ref,
-    normed_ref,
-    grad_all_ref,
-    hidden_ref,
-    up_term_ref,
-    down_term_ref,
-    back_ref,
-    attn_columns_ref,
-    arrived_ref,
-    normed3,
-    grads,
-    up_columns,
-    up_grad,
-    out_buf,
-    side,
-    chip,
-    from_x,
-    from_y,
-    last,
-    own,
-    ends,
-    held,
-    x_buf,
-    normed_buf,
-    term_buf,
-    gather_send,
-    gather_recv,
-    gather_local,
-    scatter_send,
-    scatter_recv,
-    line_send,
-    line_recv,
-    line_load,
-    swap_send,
-    swap_recv,
-    swap_local,
-    out_sem,
-):
-    column = lax.axis_index("dp")
-    plane = lax.axis_index("hist")
-    rows, features = grad_ref.shape
-    total = 8 * rows
-    share = w_up_ref.shape[0]
-    ff_share = w_down_ref.shape[0]
-    tile = 256
-
-    barrier = pltpu.get_barrier_semaphore()
-    for mask in range(1, 8):
-        pl.semaphore_signal(
-            barrier, inc=1, device_id={"dp": partner(column, mask)}, device_id_type=DEVICE_MESH
-        )
-    for place in range(4):
-
-        @pl.when(plane == place)
-        def _():
-            nearby = [p for p in (place - 1, place + 1) if 0 <= p < 4]
-            for p in nearby:
-                pl.semaphore_signal(
-                    barrier, inc=1, device_id=z_place(p), device_id_type=DEVICE_MESH
-                )
-            pl.semaphore_wait(barrier, 7 + len(nearby))
-
-    line = LineSums(
-        plane, part_ref, arrived_ref, own, ends, held, line_send, line_recv, line_load
-    )
-    line.start()
-    zeros = jnp.zeros((16, features), jnp.bfloat16)
-
-    def clear(r, carry):
-        ends[0, pl.ds(pl.multiple_of(r * 16, 16), 16), :] = zeros
-        ends[1, pl.ds(pl.multiple_of(r * 16, 16), 16), :] = zeros
-        return carry
-
-    lax.fori_loop(0, rows // 16, clear, 0)
-
-    my_rows = pl.ds(pl.multiple_of(column * share, 16), share)
-
-    def up_piece(owner):
-        return w_up_ref.at[:, pl.ds(pl.multiple_of(owner * ff_share, 128), ff_share)]
-
-    up_local = pltpu.make_async_copy(up_piece(column), up_columns.at[my_rows], swap_local.at[0])
-    up_local.start()
-    up_swaps = [
-        push(
-            up_piece(partner(column, mask)),
-            up_columns.at[my_rows],
-            swap_send.at[mask],
-            swap_recv.at[mask],
-            partner(column, mask),
-        )
-        for mask in (6, 7, 2, 3, 4, 5, 1)
-    ]
-
-    def gather(index, own_rows, whole):
-        return PlaneGatherSteps(
-            column,
-            own_rows,
-            whole,
-            gather_send.at[index],
-            gather_recv.at[index],
-            gather_local.at[index],
-        )
-
-    grad_gather = gather(4, grad_ref, grads)
-    grad_gather.begin()
-
-    x_copies = []
-
-    def combine(item):
-        if item >= 2:
-            x_copies[item - 2].wait()
-        x_now = x_buf.at[item % 2]
-
-        def some_rows(r, carry):
-            piece = pl.ds(pl.multiple_of(r * 16, 16), 16)
-            x = (
-                own[piece, :].astype(jnp.float32)
-                + ends[0, piece, :].astype(jnp.float32)
-                + ends[1, piece, :].astype(jnp.float32)
-            )
-            x_now[piece, :] = x
-            inverse = lax.rsqrt(jnp.mean(x * x, axis=-1, keepdims=True) + epsilon)
-            normed_buf[item, piece, :] = (x * inverse * gain_ref[pl.ds(item, 1), :]).astype(
-                jnp.bfloat16
-            )
-            return carry
-
-        lax.fori_loop(0, rows // 16, some_rows, 0)
-        copy = pltpu.make_async_copy(x_now, x_ref.at[item], out_sem.at[item % 2])
-        copy.start()
-        x_copies.append(copy)
-        steps = gather(
-            item, normed_buf.at[item], normed3 if item == 0 else normed_ref.at[item - 1]
-        )
-        steps.begin()
-        return steps
-
-    line.service(0)
-    grad_gather.corners()
-    line.service(1)
-    grad_gather.siblings()
-    line.service(2)
-    gather3 = combine(0)
-    grad_gather.rest()
-    gather3.corners()
-    line.service(3)
-    grad_gather.finish()
-    grads_out = pltpu.make_async_copy(grads, grad_all_ref, out_sem.at[2])
-    grads_out.start()
-    gather3.siblings()
-    gather3.rest()
-    line.service(4)
-    for copy in up_swaps:
-        copy.wait_recv()
-    up_local.wait()
-    gather3.finish()
-
-    def attn_piece(stream, owner):
-        return w_attn_ref.at[stream, :, pl.ds(pl.multiple_of(owner * share, 128), share)]
-
-    def attn_place(stream):
-        return attn_columns_ref.at[stream, my_rows]
-
-    attn_swaps, attn_locals = [], []
-    for stream in range(3):
-        local = pltpu.make_async_copy(
-            attn_piece(stream, column), attn_place(stream), swap_local.at[1 + stream]
-        )
-        local.start()
-        attn_locals.append(local)
-        for mask in (6, 7, 2, 3, 4, 5, 1):
-            attn_swaps.append(
-                push(
-                    attn_piece(stream, partner(column, mask)),
-                    attn_place(stream),
-                    swap_send.at[8 * (stream + 1) + mask],
-                    swap_recv.at[8 * (stream + 1) + mask],
-                    partner(column, mask),
-                )
-            )
-
-    def feed(first_block, count):
-        def one_tile(step, carry):
-            piece = pl.ds(pl.multiple_of((step // (ff_share // tile)) * rows, 16), rows)
-            lanes = pl.ds(pl.multiple_of((step % (ff_share // tile)) * tile, tile), tile)
-            up = jnp.dot(normed3[piece, :], up_columns[:, lanes], preferred_element_type=jnp.float32)
-            spread = 0.5 * (1.0 + lax.erf(up * (1.0 / math.sqrt(2.0))))
-            hidden_ref[piece, lanes] = (up * spread).astype(jnp.bfloat16)
-            slope = spread + up * jnp.exp(-0.5 * up * up) * (1.0 / math.sqrt(2.0 * math.pi))
-            hidden_grad = lax.dot_general(
-                grads[piece, :],
-                w_down_ref[lanes, :],
-                contract_cols,
-                preferred_element_type=jnp.float32,
-            )
-            up_grad[piece, lanes] = (hidden_grad * slope).astype(jnp.bfloat16)
-            return carry
-
-        per_block = ff_share // tile
-        lax.fori_loop(first_block * per_block, (first_block + count) * per_block, one_tile, 0)
-
-    feed(0, 1)
-    line.service(5)
-    gather0 = combine(1)
-    feed(1, 3)
-    gather0.corners()
-    line.service(6)
-    feed(4, 2)
-    gather0.siblings()
-    gather0.rest()
-    line.service(7)
-    feed(6, 2)
-
-    def back_product(owner, target):
-        left_rows = pl.ds(pl.multiple_of(owner * rows, 16), rows)
-
-        def one_tile(t, carry):
-            lanes = pl.ds(pl.multiple_of(t * 2 * tile, 2 * tile), 2 * tile)
-            target[:, lanes] = lax.dot_general(
-                up_grad[left_rows, :],
-                up_columns[lanes, :],
-                contract_cols,
-                preferred_element_type=jnp.float32,
-            ).astype(jnp.bfloat16)
-            return carry
-
-        lax.fori_loop(0, features // (2 * tile), one_tile, 0)
-
-    scatter = PlaneScatterSteps(
-        column,
-        back_product,
-        (out_buf, side, chip, from_x, from_y, last),
-        scatter_send,
-        scatter_recv,
-    )
-    scatter.block(0)
-    line.service(8)
-    gather1 = combine(2)
-    gather0.finish()
-    scatter.block(1)
-    scatter.block(2)
-    scatter.block(3)
-    scatter.turn()
-    gather1.corners()
-    line.service(9)
-    scatter.finish(back_ref)
-
-    term_slots = 2
-    part = share // 4
-
-    def term_copies(kind, slot, index):
-        if kind == 0:
-            return [
-                pltpu.make_async_copy(
-                    term_buf.at[slot, pl.ds(h * part, part), pl.ds(0, ff_share)],
-                    up_term_ref.at[
-                        pl.ds(h * 4 * part + index % 4 * part, part),
-                        pl.ds(index // 4 * ff_share, ff_share),
-                    ],
-                    out_sem.at[3 + 4 * slot + h],
-                )
-                for h in range(4)
-            ]
-        return [
-            pltpu.make_async_copy(
-                term_buf.at[slot], down_term_ref.at[pl.ds(index * tile, tile)], out_sem.at[3 + 4 * slot]
-            )
-        ]
-
-    def terms(kind, first, count):
-        width = ff_share if kind == 0 else features
-        pending = []
-        for index in range(first, first + count):
-            slot = index % term_slots
-            if len(pending) >= term_slots:
-                for copy in pending[-term_slots]:
-                    copy.wait()
-
-            def one_tile(t, carry):
-                lanes = pl.ds(pl.multiple_of(t * 2 * tile, 2 * tile), 2 * tile)
-                if kind == 0:
-                    left, right = normed3[:, index * tile : (index + 1) * tile], up_grad[:, lanes]
-                else:
-                    left, right = hidden_ref[:, index * tile : (index + 1) * tile], grads[:, lanes]
-                term_buf[slot, :, lanes] = lax.dot_general(
-                    left, right, contract_rows, preferred_element_type=jnp.float32
-                ).astype(jnp.bfloat16)
-                return carry
-
-            lax.fori_loop(0, width // (2 * tile), one_tile, 0)
-            copies = term_copies(kind, slot, index)
-            for copy in copies:
-                copy.start()
-            pending.append(copies)
-        for copies in pending[-term_slots:]:
-            for copy in copies:
-                copy.wait()
-
-    terms(1, 0, 2)
-    gather1.siblings()
-    gather1.rest()
-    terms(1, 2, ff_share // tile - 2)
-    line.service(10)
-    terms(0, 0, 4)
-    gather1.finish()
-    line.service(11)
-    gather2 = combine(3)
-    terms(0, 4, features // tile - 4)
-    gather2.corners()
-    gather2.siblings()
-    gather2.rest()
-    line.drain()
-    for copy in attn_swaps:
-        copy.wait_recv()
-    for copy in attn_locals:
-        copy.wait()
-    for copy in up_swaps + attn_swaps:
-        copy.wait_send()
-    grads_out.wait()
-    for copy in x_copies[-2:]:
-        copy.wait()
-    gather2.finish()
-
-
-def forward_and_feed(parts, grad_low, w_up, w_attn, w_down, gains):
-    rows, features = grad_low.shape
-    total = 8 * rows
-    share = w_up.shape[0]
-    ff_share = w_down.shape[0]
-    block = (rows, features)
-    half = (2, rows // 2, features)
-    anywhere = pl.BlockSpec(memory_space=pl.ANY)
-    near = pl.BlockSpec(memory_space=pltpu.VMEM)
-    shape = jax.ShapeDtypeStruct
-    low_type = jnp.bfloat16
-    return pl.pallas_call(
-        forward_kernel,
-        in_specs=[anywhere, near, anywhere, anywhere, near, near],
-        out_specs=[anywhere, anywhere, anywhere, near, anywhere, anywhere, near]
-        + [anywhere, anywhere],
-        out_shape=[
-            shape((4,) + block, jnp.float32),
-            shape((3, total, features), low_type),
-            shape((total, features), low_type),
-            shape((total, ff_share), low_type),
-            shape((features * ff_share // features, features), low_type),
-            shape((ff_share, features), low_type),
-            shape(block, low_type),
-            shape((3, features, share), low_type),
-            shape((24,) + block, low_type),
-        ],
-        scratch_shapes=[
-            pltpu.VMEM((total, features), low_type),
-            pltpu.VMEM((total, features), low_type),
-            pltpu.VMEM((features, ff_share), low_type),
-            pltpu.VMEM((total, ff_share), low_type),
-            pltpu.VMEM((4,) + block, low_type),
-            pltpu.VMEM((4,) + block, low_type),
-            pltpu.VMEM((4,) + block, low_type),
-            pltpu.VMEM(half, low_type),
-            pltpu.VMEM(half, low_type),
-            pltpu.VMEM(half, low_type),
-            pltpu.VMEM(block, low_type),
-            pltpu.VMEM((2,) + block, low_type),
-            pltpu.VMEM((4,) + block, low_type),
-            pltpu.VMEM((2,) + block, jnp.float32),
-            pltpu.VMEM((4,) + block, low_type),
-            pltpu.VMEM((2, 256, features), low_type),
-            pltpu.SemaphoreType.DMA((5, 11)),
-            pltpu.SemaphoreType.DMA((5, 11)),
-            pltpu.SemaphoreType.DMA((5,)),
-            pltpu.SemaphoreType.DMA((10,)),
-            pltpu.SemaphoreType.DMA((10,)),
-            pltpu.SemaphoreType.DMA((24,)),
-            pltpu.SemaphoreType.DMA((24,)),
-            pltpu.SemaphoreType.DMA((2,)),
-            pltpu.SemaphoreType.DMA((32,)),
-            pltpu.SemaphoreType.DMA((32,)),
-            pltpu.SemaphoreType.DMA((4,)),
-            pltpu.SemaphoreType.DMA((11,)),
-        ],
-        compiler_params=pltpu.CompilerParams(
-            collective_id=5, has_side_effects=True, vmem_limit_bytes=62 * 1024 * 1024
-        ),
-        cost_estimate=pl.CostEstimate(
-            flops=12 * total * features * ff_share,
-            bytes_accessed=400 * 1000 * 1000,
-            transcendentals=0,
-        ),
-    )(parts, grad_low, w_up, w_attn, w_down, gains)
-
-
 class LineSum:
 
     def __init__(self, plane, parts, arrived, own, last, held, send_sem, recv_sem, load_sem):
@@ -1305,6 +900,997 @@
                     if a < 3:
                         for distance in range(a + 1):
                             self.message(way, a, distance).wait_send()
+
+
+GAIN_ROW = (4, 1, 2, 3)
+
+
+def norm_rows_back(x_buf, back, gain_ref, gain_grad_ref, item, extra, target):
+    gain = gain_ref[pl.ds(GAIN_ROW[item], 1), :]
+    rows, features = target.shape
+
+    def some_rows(r, gain_sum):
+        piece = pl.ds(pl.multiple_of(r * 16, 16), 16)
+        x = x_buf[piece, :]
+        inverse = lax.rsqrt(jnp.mean(x * x, axis=-1, keepdims=True) + epsilon)
+        grad = back[piece, :].astype(jnp.float32)
+        scaled = grad * gain
+        mean = jnp.mean(scaled * x, axis=-1, keepdims=True)
+        result = inverse * scaled - x * (inverse * inverse * inverse) * mean
+        if extra is not None:
+            result = result + extra[piece, :].astype(jnp.float32)
+        target[piece, :] = result.astype(jnp.bfloat16)
+        return gain_sum + jnp.sum(grad * x * inverse, axis=0, keepdims=True)
+
+    gain_grad_ref[pl.ds(item, 1), :] = lax.fori_loop(
+        0, rows // 16, some_rows, jnp.zeros((1, features), jnp.float32)
+    )
+
+
+def forward_kernel(
+    length_ref,
+    pack_ref,
+    latest_ref,
+    history_ref,
+    select_ref,
+    root_ref,
+    cotangent_ref,
+    w_up_ref,
+    w_attn_ref,
+    w_down_ref,
+    w_out_ref,
+    cos_ref,
+    sin_ref,
+    packed_ref,
+    gain_ref,
+    pre_ref,
+    factor_ref,
+    x_ref,
+    normed_ref,
+    grad_all_ref,
+    hidden_ref,
+    up_term_ref,
+    down_sum_ref,
+    full3_ref,
+    gain_grad_ref,
+    attn_columns,
+    q_ref,
+    k_ref,
+    v_ref,
+    out_grad_ref,
+    kv_before_ref,
+    part_ref,
+    down_term_ref,
+    arrived_ref,
+    arrived_down_ref,
+    normed3,
+    grads,
+    up_columns,
+    up_grad,
+    out_buf,
+    side,
+    chip,
+    from_x,
+    from_y,
+    last,
+    own,
+    ends,
+    held,
+    x_buf,
+    normed_buf,
+    term_buf,
+    grad_own,
+    stream_own,
+    mix_out_buf,
+    dyn_got,
+    gather_send,
+    gather_recv,
+    gather_local,
+    scatter_send,
+    scatter_recv,
+    line_send,
+    line_recv,
+    line_load,
+    swap_send,
+    swap_recv,
+    swap_local,
+    out_sem,
+    small_send,
+    small_recv,
+    dyn_send,
+    dyn_recv,
+    route_send,
+    route_recv,
+    block_sem,
+    spread_send,
+    spread_recv,
+    sum_send,
+    sum_recv,
+    key_send,
+    key_recv,
+    ready_sem,
+    *,
+    micro_count,
+    sequence_length,
+):
+    column = lax.axis_index("dp")
+    plane = lax.axis_index("hist")
+    rows, features = grad_own.shape
+    total = 8 * rows
+    share = w_up_ref.shape[0]
+    ff_share = w_down_ref.shape[0]
+    width = share
+    tile = 256
+    mix_rows = pack_ref.shape[0] - share - 32 + 8
+    every_mask = (6, 7, 2, 3, 4, 5, 1)
+
+    barrier = pltpu.get_barrier_semaphore()
+    for mask in every_mask:
+        pl.semaphore_signal(
+            barrier, inc=1, device_id={"dp": partner(column, mask)}, device_id_type=DEVICE_MESH
+        )
+    for place in range(4):
+
+        @pl.when(plane == place)
+        def _():
+            for p in range(4):
+                if p != place:
+                    pl.semaphore_signal(
+                        barrier, inc=1, device_id=z_place(p), device_id_type=DEVICE_MESH
+                    )
+
+    pl.semaphore_wait(barrier, 10)
+
+    def block_load(source, target, index):
+        copy = pltpu.make_async_copy(source, target, block_sem.at[index])
+        copy.start()
+        return copy
+
+    small_copies = [
+        push(
+            pack_ref,
+            packed_ref.at[column],
+            small_send.at[mask],
+            small_recv.at[mask],
+            partner(column, mask),
+        )
+        for mask in every_mask
+    ]
+    small_local = pltpu.make_async_copy(pack_ref, packed_ref.at[column], small_send.at[0])
+    small_local.start()
+    latest_loads = [
+        block_load(latest_ref.at[pl.ds(q * rows, rows)], normed_buf.at[q], 8 + q) for q in range(4)
+    ]
+
+    my_rows = pl.ds(pl.multiple_of(column * share, 16), share)
+
+    def up_piece(owner):
+        return w_up_ref.at[:, pl.ds(pl.multiple_of(owner * ff_share, 128), ff_share)]
+
+    up_local = pltpu.make_async_copy(up_piece(column), up_columns.at[my_rows], swap_local.at[0])
+    up_local.start()
+    up_swaps = [
+        push(
+            up_piece(partner(column, mask)),
+            up_columns.at[my_rows],
+            swap_send.at[mask],
+            swap_recv.at[mask],
+            partner(column, mask),
+        )
+        for mask in every_mask
+    ]
+
+    chunk = rows // micro_count
+
+    def route_source(place, s):
+        return cotangent_ref.at[pl.ds(s * chunk, chunk)]
+
+    def route_copy(place, s, target_place, slot):
+        return pltpu.make_async_remote_copy(
+            src_ref=route_source(place, s),
+            dst_ref=grad_own.at[pl.ds(slot * chunk, chunk)],
+            send_sem=route_send.at[s],
+            recv_sem=route_recv.at[slot],
+            device_id=z_place(target_place),
+            device_id_type=DEVICE_MESH,
+        )
+
+    def route_local(place, s, slot):
+        return pltpu.make_async_copy(
+            route_source(place, s), grad_own.at[pl.ds(slot * chunk, chunk)], route_recv.at[slot]
+        )
+
+    for place in range(4):
+
+        @pl.when(plane == place)
+        def _():
+            for s in range(micro_count):
+                target_place, slot = divmod(s * 4 + place, micro_count)
+                if target_place == place:
+                    route_local(place, s, slot).start()
+                else:
+                    route_copy(place, s, target_place, slot).start()
+
+    block_order = (3, 0, 2, 1)
+
+    def history_loads(i):
+        p, h = block_order[i], i % 2
+        return [
+            block_load(
+                history_ref.at[pl.ds((slot * 4 + p) * rows, rows)],
+                normed3.at[pl.ds((h * 4 + slot) * rows, rows)],
+                h * 4 + slot,
+            )
+            for slot in range(4)
+        ]
+
+    loads = [history_loads(0), history_loads(1)]
+    zeros = jnp.zeros((16, features), jnp.bfloat16)
+
+    def clear(r, carry):
+        ends[0, pl.ds(pl.multiple_of(r * 16, 16), 16), :] = zeros
+        ends[1, pl.ds(pl.multiple_of(r * 16, 16), 16), :] = zeros
+        return carry
+
+    lax.fori_loop(0, ends.shape[1] // 16, clear, 0)
+
+    small_local.wait()
+    for copy in small_copies:
+        copy.wait_recv()
+    for d in range(8):
+        gains = packed_ref[d, pl.ds(share + 16, 16), :].astype(jnp.float32)
+        gain_ref[:, pl.ds(d * share, share // 2)] = gains[:8]
+        gain_ref[:, pl.ds(d * share + share // 2, share // 2)] = gains[8:]
+        mix_out_buf[pl.ds(d * mix_rows, mix_rows), :] = packed_ref[
+            d, pl.ds(share, 16), :
+        ].astype(jnp.float32)[:mix_rows]
+    for copy in latest_loads:
+        copy.wait()
+    for q in range(4):
+
+        def norm_rows(r, carry):
+            piece = pl.ds(pl.multiple_of(r * 16, 16), 16)
+            x = normed_buf[q, piece, :].astype(jnp.float32)
+            inverse = lax.rsqrt(jnp.mean(x * x, axis=-1, keepdims=True) + epsilon)
+            normed_buf[q, piece, :] = (x * inverse * gain_ref[pl.ds(0, 1), :]).astype(jnp.bfloat16)
+            return carry
+
+        lax.fori_loop(0, rows // 16, norm_rows, 0)
+        pre = None
+        for d in range(8):
+            term = matmul(normed_buf[q, :, d * share : (d + 1) * share], packed_ref[d, :share, :])
+            pre = term if pre is None else pre + term
+        pre_ref[pl.ds(q * rows, rows), :] = pre
+    pre = pre_ref[...]
+    act = 0.5 * pre * (1.0 + lax.erf(pre * (1.0 / math.sqrt(2.0))))
+    dyn = precise(act[:, : 8 * mix_rows], mix_out_buf[...])
+    dyn_columns = (jnp.transpose(dyn)[: 8 * mix_rows] * root_ref[pl.ds(0, 1), :]).astype(jnp.bfloat16)
+
+    def dyn_copy(source_place, target_place):
+        return pltpu.make_async_remote_copy(
+            src_ref=dyn_got.at[source_place],
+            dst_ref=dyn_got.at[source_place],
+            send_sem=dyn_send.at[target_place],
+            recv_sem=dyn_recv.at[source_place],
+            device_id=z_place(target_place),
+            device_id_type=DEVICE_MESH,
+        )
+
+    for place in range(4):
+
+        @pl.when(plane == place)
+        def _():
+            dyn_got[place] = dyn_columns
+            for p in range(4):
+                if p != place:
+                    dyn_copy(place, p).start()
+            for p in range(4):
+                if p != place:
+                    dyn_copy(p, place).wait_recv()
+
+    dyn_sum = dyn_got[0] + dyn_got[1] + dyn_got[2] + dyn_got[3]
+    factor_ref[...] = lax.dot_general(
+        dyn_sum, select_ref[...], contract_rows, preferred_element_type=jnp.float32
+    )
+
+    stores = [None, None]
+    for i, p in enumerate(block_order):
+        h = i % 2
+        for copy in loads[i]:
+            copy.wait()
+        if stores[h] is not None:
+            for copy in stores[h]:
+                copy.wait()
+
+        def mix_rows_of(r, carry):
+            factors = factor_ref[pl.ds(pl.multiple_of(p * rows + r * 16, 16), 16), :]
+            for lane in range(0, features, 512):
+                slots = [
+                    normed3[
+                        pl.ds(pl.multiple_of((h * 4 + slot) * rows + r * 16, 16), 16),
+                        lane : lane + 512,
+                    ].astype(jnp.float32)
+                    for slot in range(4)
+                ]
+                for item in range(4):
+                    mixed = None
+                    for slot in range(4):
+                        one = item * 4 + slot
+                        term = factors[:, one : one + 1] * slots[slot]
+                        mixed = term if mixed is None else mixed + term
+                    grads[
+                        pl.ds(pl.multiple_of((h * 4 + item) * rows + r * 16, 16), 16),
+                        lane : lane + 512,
+                    ] = mixed.astype(jnp.bfloat16)
+            return carry
+
+        lax.fori_loop(0, rows // 16, mix_rows_of, 0)
+        stores[h] = [
+            pltpu.make_async_copy(
+                grads.at[pl.ds((h * 4 + item) * rows, rows)],
+                part_ref.at[pl.ds((item * 4 + p) * rows, rows)],
+                block_sem.at[12 + h * 4 + item],
+            )
+            for item in range(4)
+        ]
+        for copy in stores[h]:
+            copy.start()
+        if i + 2 < 4:
+            loads.append(history_loads(i + 2))
+    for copies in stores:
+        for copy in copies:
+            copy.wait()
+
+    block = pl.ds(0, rows)
+    line = LineSums(
+        plane,
+        part_ref,
+        arrived_ref,
+        own.at[block],
+        ends.at[:, block],
+        held.at[:, block],
+        line_send,
+        line_recv,
+        line_load,
+    )
+    line.start()
+    for mask in (CORE, ACROSS_X, ACROSS_Y):
+        pl.semaphore_signal(
+            ready_sem, inc=1, device_id={"dp": partner(column, mask)}, device_id_type=DEVICE_MESH
+        )
+
+    def attn_piece(stream, owner):
+        return w_attn_ref.at[stream, :, pl.ds(pl.multiple_of(owner * share, 128), share)]
+
+    attn_swaps, attn_locals = [], []
+    for stream in range(3):
+        local = pltpu.make_async_copy(
+            attn_piece(stream, column),
+            attn_columns.at[stream, my_rows],
+            swap_local.at[1 + stream],
+        )
+        local.start()
+        attn_locals.append(local)
+        for mask in every_mask:
+            attn_swaps.append(
+                push(
+                    attn_piece(stream, partner(column, mask)),
+                    attn_columns.at[stream, my_rows],
+                    swap_send.at[8 * (stream + 1) + mask],
+                    swap_recv.at[8 * (stream + 1) + mask],
+                    partner(column, mask),
+                )
+            )
+
+    def gather(index, own_rows, whole):
+        return PlaneGatherSteps(
+            column,
+            own_rows,
+            whole,
+            gather_send.at[index],
+            gather_recv.at[index],
+            gather_local.at[index],
+        )
+
+    for place in range(4):
+
+        @pl.when(plane == place)
+        def _():
+            for slot in range(micro_count):
+                s, source_place = divmod(place * micro_count + slot, 4)
+                if source_place == place:
+                    route_local(place, s, slot).wait()
+                else:
+                    route_copy(source_place, s, place, slot).wait_recv()
+
+    def mask_rows(r, carry):
+        piece = pl.ds(pl.multiple_of(r * 16, 16), 16)
+        row = plane * rows + r * 16 + lax.broadcasted_iota(jnp.int32, (16, 1), 0)
+        limit = jnp.zeros((16, 1), jnp.int32)
+        for m in range(micro_count):
+            inside = (row >= m * sequence_length) & (row < (m + 1) * sequence_length)
+            limit = jnp.where(inside, m * sequence_length + length_ref[m], limit)
+        kept = jnp.where(row < limit, grad_own[piece, :].astype(jnp.float32), 0.0)
+        grad_own[piece, :] = kept.astype(jnp.bfloat16)
+        return carry
+
+    lax.fori_loop(0, rows // 16, mask_rows, 0)
+    pl.semaphore_wait(ready_sem, 3)
+    grad_gather = gather(4, grad_own, grads)
+    grad_gather.begin()
+
+    x_copies = []
+
+    def combine(item):
+        if x_copies:
+            x_copies[-1].wait()
+
+        def some_rows(r, carry):
+            piece = pl.ds(pl.multiple_of(r * 16, 16), 16)
+            x = (
+                own[piece, :].astype(jnp.float32)
+                + ends[0, piece, :].astype(jnp.float32)
+                + ends[1, piece, :].astype(jnp.float32)
+            )
+            x_buf[piece, :] = x
+            inverse = lax.rsqrt(jnp.mean(x * x, axis=-1, keepdims=True) + epsilon)
+            normed_buf[item, piece, :] = (
+                x * inverse * gain_ref[pl.ds(GAIN_ROW[item], 1), :]
+            ).astype(jnp.bfloat16)
+            return carry
+
+        lax.fori_loop(0, rows // 16, some_rows, 0)
+        copy = pltpu.make_async_copy(x_buf, x_ref.at[item], out_sem.at[0])
+        copy.start()
+        x_copies.append(copy)
+        steps = gather(
+            item, normed_buf.at[item], normed3 if item == 0 else normed_ref.at[item - 1]
+        )
+        steps.begin()
+        return steps
+
+    line.service(0)
+    line.service(1)
+    line.service(2)
+    gather3 = combine(0)
+    grad_gather.corners()
+    grad_gather.siblings()
+    line.service(3)
+    grad_gather.rest()
+    gather3.corners()
+    line.service(4)
+    grad_gather.finish()
+    grads_out = pltpu.make_async_copy(grads, grad_all_ref, out_sem.at[2])
+    grads_out.start()
+    gather3.siblings()
+    gather3.rest()
+    for copy in up_swaps:
+        copy.wait_recv()
+    up_local.wait()
+    gather3.finish()
+
+    def feed(first_block, count):
+        def one_tile(step, carry):
+            piece = pl.ds(pl.multiple_of((step // (ff_share // tile)) * rows, 16), rows)
+            lanes = pl.ds(pl.multiple_of((step % (ff_share // tile)) * tile, tile), tile)
+            up = jnp.dot(normed3[piece, :], up_columns[:, lanes], preferred_element_type=jnp.float32)
+            spread = 0.5 * (1.0 + lax.erf(up * (1.0 / math.sqrt(2.0))))
+            hidden_ref[piece, lanes] = (up * spread).astype(jnp.bfloat16)
+            slope = spread + up * jnp.exp(-0.5 * up * up) * (1.0 / math.sqrt(2.0 * math.pi))
+            hidden_grad = lax.dot_general(
+                grads[piece, :],
+                w_down_ref[lanes, :],
+                contract_cols,
+                preferred_element_type=jnp.float32,
+            )
+            up_grad[piece, lanes] = (hidden_grad * slope).astype(jnp.bfloat16)
+            return carry
+
+        per_block = ff_share // tile
+        lax.fori_loop(first_block * per_block, (first_block + count) * per_block, one_tile, 0)
+
+    def back_product(owner, target):
+        left_rows = pl.ds(pl.multiple_of(owner * rows, 16), rows)
+
+        def one_tile(t, carry):
+            lanes = pl.ds(pl.multiple_of(t * 2 * tile, 2 * tile), 2 * tile)
+            target[:, lanes] = lax.dot_general(
+                up_grad[left_rows, :],
+                up_columns[lanes, :],
+                contract_cols,
+                preferred_element_type=jnp.float32,
+            ).astype(jnp.bfloat16)
+            return carry
+
+        lax.fori_loop(0, features // (2 * tile), one_tile, 0)
+
+    term_slots = 2
+    part = share // 4
+
+    def term_copies(kind, slot, index):
+        if kind == 0:
+            return [
+                pltpu.make_async_copy(
+                    term_buf.at[slot, pl.ds(h * part, part), pl.ds(0, ff_share)],
+                    up_term_ref.at[
+                        pl.ds(h * 4 * part + index % 4 * part, part),
+                        pl.ds(index // 4 * ff_share, ff_share),
+                    ],
+                    out_sem.at[3 + 4 * slot + h],
+                )
+                for h in range(4)
+            ]
+        return [
+            pltpu.make_async_copy(
+                term_buf.at[slot],
+                down_term_ref.at[pl.ds(index * tile, tile)],
+                out_sem.at[3 + 4 * slot],
+            )
+        ]
+
+    def terms(kind, first, count):
+        term_width = ff_share if kind == 0 else features
+        pending = []
+        for index in range(first, first + count):
+            slot = index % term_slots
+            if len(pending) >= term_slots:
+                for copy in pending[-term_slots]:
+                    copy.wait()
+
+            def one_tile(t, carry):
+                lanes = pl.ds(pl.multiple_of(t * 2 * tile, 2 * tile), 2 * tile)
+                if kind == 0:
+                    left, right = normed3[:, index * tile : (index + 1) * tile], up_grad[:, lanes]
+                else:
+                    left, right = hidden_ref[:, index * tile : (index + 1) * tile], grads[:, lanes]
+                term_buf[slot, :, lanes] = lax.dot_general(
+                    left, right, contract_rows, preferred_element_type=jnp.float32
+                ).astype(jnp.bfloat16)
+                return carry
+
+            lax.fori_loop(0, term_width // (2 * tile), one_tile, 0)
+            copies = term_copies(kind, slot, index)
+            for copy in copies:
+                copy.start()
+            pending.append(copies)
+        for copies in pending[-term_slots:]:
+            for copy in copies:
+                copy.wait()
+
+    def project(stream, target):
+        def one_block(b, carry):
+            piece = pl.ds(pl.multiple_of(b * rows, 16), rows)
+            value = matmul(normed3[piece, :], attn_columns[stream])
+            if stream < 2:
+                parts = []
+                for head in range(width // HEAD_DIM):
+                    one = value[:, head * HEAD_DIM : (head + 1) * HEAD_DIM]
+                    swapped = jnp.concatenate(
+                        [one[:, HEAD_DIM // 2 :], one[:, : HEAD_DIM // 2]], axis=1
+                    )
+                    parts.append(one * cos_ref[...] + swapped * sin_ref[...])
+                value = jnp.concatenate(parts, axis=1)
+            target[piece, :] = value.astype(jnp.bfloat16)
+            return carry
+
+        lax.fori_loop(0, 8, one_block, 0)
+
+    def out_grads(b, carry):
+        piece = pl.ds(pl.multiple_of(b * rows, 16), rows)
+        out_grad_ref[piece, :] = lax.dot_general(
+            grads[piece, :], w_out_ref[...], contract_cols, preferred_element_type=jnp.float32
+        ).astype(jnp.bfloat16)
+        return carry
+
+    def key_copy(i, place):
+        return pltpu.make_async_remote_copy(
+            src_ref=(k_ref, v_ref)[i],
+            dst_ref=kv_before_ref.at[:, pl.ds(i * width, width)],
+            send_sem=key_send.at[i],
+            recv_sem=key_recv.at[i],
+            device_id=z_place(place + 1),
+            device_id_type=DEVICE_MESH,
+        )
+
+    def send_keys(i):
+        for place in range(3):
+
+            @pl.when(plane == place)
+            def _():
+                key_copy(i, place).start()
+
+    feed(0, 2)
+    line.service(5)
+    gather0 = combine(1)
+    feed(2, 3)
+    gather0.corners()
+    line.service(6)
+    feed(5, 2)
+    gather0.siblings()
+    line.service(7)
+    feed(7, 1)
+    gather0.rest()
+    scatter = PlaneScatterSteps(
+        column,
+        back_product,
+        (out_buf, side, chip, from_x, from_y, last),
+        scatter_send,
+        scatter_recv,
+    )
+    scatter.block(0)
+    scatter.block(1)
+    line.service(8)
+    gather1 = combine(2)
+    scatter.block(2)
+    scatter.block(3)
+    gather0.finish()
+    scatter.turn()
+    terms(1, 0, 2)
+    gather1.corners()
+    line.service(9)
+    scatter.finish(None)
+    x_copies[-1].wait()
+    x_load = pltpu.make_async_copy(x_ref.at[0], x_buf, out_sem.at[1])
+    x_load.start()
+    x_load.wait()
+    norm_rows_back(x_buf, chip.at[3], gain_ref, gain_grad_ref, 0, grad_own, stream_own)
+    x_copies.clear()
+    spread3 = LineGather(
+        plane,
+        stream_own,
+        lambda p: full3_ref.at[pl.ds(p * rows, rows)],
+        spread_send,
+        spread_recv,
+        out_sem.at[11],
+    )
+    spread3.service(0)
+    gather1.siblings()
+    terms(1, 2, ff_share // tile - 2)
+    gather1.rest()
+    down_line = LineSum(
+        plane, down_term_ref, arrived_down_ref, own, ends, held, sum_send, sum_recv, line_load
+    )
+    line.service(10)
+    spread3.service(1)
+    down_line.start()
+    terms(0, 0, 2)
+    spread3.service(2)
+    line.service(11)
+    gather2 = combine(3)
+    terms(0, 2, features // tile - 2)
+    spread3.service(3)
+    line.drain()
+    gather1.finish()
+    for copy in attn_swaps:
+        copy.wait_recv()
+    for copy in attn_locals:
+        copy.wait()
+    load = block_load(normed_ref.at[1], normed3, 0)
+    gather2.corners()
+    load.wait()
+    project(1, k_ref)
+    send_keys(0)
+    down_line.service(0)
+    load = block_load(normed_ref.at[0], normed3, 0)
+    gather2.siblings()
+    gather2.rest()
+    load.wait()
+    project(0, q_ref)
+    gather2.finish()
+    load = block_load(normed_ref.at[2], normed3, 0)
+    lax.fori_loop(0, 8, out_grads, 0)
+    load.wait()
+    project(2, v_ref)
+    send_keys(1)
+    down_line.service(1)
+    for copy in small_copies + up_swaps + attn_swaps:
+        copy.wait_send()
+    grads_out.wait()
+    x_copies[-1].wait()
+    for place in range(4):
+
+        @pl.when(plane == place)
+        def _():
+            for p in range(4):
+                if p != place:
+                    dyn_copy(place, p).wait_send()
+            for s in range(micro_count):
+                target_place, slot = divmod(s * 4 + place, micro_count)
+                if target_place != place:
+                    route_copy(place, s, target_place, slot).wait_send()
+
+    down_line.service(2)
+    down_line.finish(down_sum_ref)
+    spread3.finish()
+    for place in range(4):
+
+        @pl.when(plane == place)
+        def _():
+            for i in range(2):
+                if place > 0:
+                    key_copy(i, place - 1).wait_recv()
+                if place < 3:
+                    key_copy(i, place).wait_send()
+
+
+def forward_and_feed(
+    lengths,
+    pack,
+    latest,
+    history,
+    select,
+    root,
+    cotangent,
+    w_up,
+    w_attn,
+    w_down,
+    w_out,
+    cosine,
+    sine_part,
+    sequence_length,
+):
+    rows, features = cotangent.shape
+    micro_count = lengths.shape[0]
+    total = 8 * rows
+    share = w_up.shape[0]
+    ff_share = w_down.shape[0]
+    mix_width = select.shape[0]
+    block = (rows, features)
+    piece = (4 * (share // 4), features)
+    half = (2, rows // 2, features)
+    anywhere = pl.BlockSpec(memory_space=pl.ANY)
+    near = pl.BlockSpec(memory_space=pltpu.VMEM)
+    shape = jax.ShapeDtypeStruct
+    low_type = jnp.bfloat16
+    some = lambda *dims: pltpu.VMEM(dims, low_type)
+    wide = lambda *dims: pltpu.VMEM(dims, jnp.float32)
+    dma = pltpu.SemaphoreType.DMA
+    outputs = [
+        (near, shape((8,) + pack.shape, low_type)),
+        (near, shape((8, features), jnp.float32)),
+        (near, shape((4 * rows, 128), jnp.float32)),
+        (near, shape((4 * rows, 128), jnp.float32)),
+        (anywhere, shape((4,) + block, jnp.float32)),
+        (anywhere, shape((3, total, features), low_type)),
+        (anywhere, shape((total, features), low_type)),
+        (near, shape((total, ff_share), low_type)),
+        (anywhere, shape((ff_share, features), low_type)),
+        (near, shape(piece, low_type)),
+        (anywhere, shape((4 * rows, features), low_type)),
+        (near, shape((8, features), jnp.float32)),
+        (near, shape((3, features, share), low_type)),
+        (near, shape((total, share), low_type)),
+        (near, shape((total, share), low_type)),
+        (near, shape((total, share), low_type)),
+        (near, shape((total, share), low_type)),
+        (anywhere, shape((total, 2 * share), low_type)),
+        (anywhere, shape((16 * rows, features), low_type)),
+        (anywhere, shape((ff_share, features), low_type)),
+        (anywhere, shape((24,) + block, low_type)),
+        (anywhere, shape((6,) + piece, low_type)),
+    ]
+    return pl.pallas_call(
+        functools.partial(
+            forward_kernel, micro_count=micro_count, sequence_length=sequence_length
+        ),
+        in_specs=[pl.BlockSpec(memory_space=pltpu.SMEM), near, anywhere, anywhere]
+        + [near, near, anywhere, anywhere, anywhere]
+        + [near] * 4,
+        out_specs=[spec for spec, _ in outputs],
+        out_shape=[out for _, out in outputs],
+        scratch_shapes=[
+            some(total, features),
+            some(total, features),
+            some(features, ff_share),
+            some(total, ff_share),
+            some(2, *block),
+            some(4, *block),
+            some(4, *block),
+            some(*half),
+            some(*half),
+            some(*half),
+            some(*piece),
+            some(2, *piece),
+            some(4, *piece),
+            wide(*block),
+            some(4, *block),
+            some(2, 256, features),
+            some(*block),
+            some(*block),
+            wide(mix_width, 128),
+            some(4, mix_width, 4 * rows),
+            dma((5, 11)),
+            dma((5, 11)),
+            dma((5,)),
+            dma((10,)),
+            dma((10,)),
+            dma((24,)),
+            dma((24,)),
+            dma((2,)),
+            dma((32,)),
+            dma((32,)),
+            dma((4,)),
+            dma((12,)),
+            dma((8,)),
+            dma((8,)),
+            dma((4,)),
+            dma((4,)),
+            dma((micro_count,)),
+            dma((micro_count,)),
+            dma((20,)),
+            dma((6,)),
+            dma((6,)),
+            dma((6,)),
+            dma((6,)),
+            dma((2,)),
+            dma((2,)),
+            pltpu.SemaphoreType.REGULAR,
+        ],
+        compiler_params=pltpu.CompilerParams(
+            collective_id=5, has_side_effects=True, vmem_limit_bytes=63 * 1024 * 1024
+        ),
+        cost_estimate=pl.CostEstimate(
+            flops=12 * total * features * ff_share,
+            bytes_accessed=600 * 1000 * 1000,
+            transcendentals=0,
+        ),
+    )(
+        lengths,
+        pack,
+        latest,
+        history,
+        select,
+        root,
+        cotangent,
+        w_up,
+        w_attn,
+        w_down,
+        w_out,
+        cosine,
+        sine_part,
+    )
+
+
+def small_sum_kernel(parts_ref, out_ref, got, sums, send_sem, recv_sem, z_send, z_recv):
+    column = lax.axis_index("dp")
+    plane = lax.axis_index("hist")
+    every_mask = (6, 7, 2, 3, 4, 5, 1)
+    barrier = pltpu.get_barrier_semaphore()
+    for mask in every_mask:
+        pl.semaphore_signal(
+            barrier, inc=1, device_id={"dp": partner(column, mask)}, device_id_type=DEVICE_MESH
+        )
+    for place in range(4):
+
+        @pl.when(plane == place)
+        def _():
+            for p in range(4):
+                if p != place:
+                    pl.semaphore_signal(
+                        barrier, inc=1, device_id=z_place(p), device_id_type=DEVICE_MESH
+                    )
+
+    pl.semaphore_wait(barrier, 10)
+    copies = [
+        push(
+            parts_ref.at[partner(column, mask)],
+            got.at[mask],
+            send_sem.at[mask],
+            recv_sem.at[mask],
+            partner(column, mask),
+        )
+        for mask in every_mask
+    ]
+    total = parts_ref[column].astype(jnp.float32)
+    for mask, copy in zip(every_mask, copies):
+        copy.wait_recv()
+        total = total + got[mask].astype(jnp.float32)
+
+    def line_copy(source_place, target_place):
+        return pltpu.make_async_remote_copy(
+            src_ref=sums.at[source_place],
+            dst_ref=sums.at[source_place],
+            send_sem=z_send.at[target_place],
+            recv_sem=z_recv.at[source_place],
+            device_id=z_place(target_place),
+            device_id_type=DEVICE_MESH,
+        )
+
+    for place in range(4):
+
+        @pl.when(plane == place)
+        def _():
+            others = [p for p in range(4) if p != place]
+            sums[place] = total.astype(jnp.bfloat16)
+            for p in others:
+                line_copy(place, p).start()
+            for p in others:
+                line_copy(p, place).wait_recv()
+            for p in others:
+                line_copy(place, p).wait_send()
+
+    out_ref[...] = (sums[0].astype(jnp.float32) + sums[1].astype(jnp.float32)) + (
+        sums[2].astype(jnp.float32) + sums[3].astype(jnp.float32)
+    )
+    for copy in copies:
+        copy.wait_send()
+
+
+def small_sums(parts):
+    dims = parts.shape[1:]
+    dma = pltpu.SemaphoreType.DMA
+    return pl.pallas_call(
+        small_sum_kernel,
+        out_shape=jax.ShapeDtypeStruct(dims, jnp.float32),
+        in_specs=[pl.BlockSpec(memory_space=pltpu.VMEM)],
+        out_specs=pl.BlockSpec(memory_space=pltpu.VMEM),
+        scratch_shapes=[
+            pltpu.VMEM((8,) + dims, jnp.bfloat16),
+            pltpu.VMEM((4,) + dims, jnp.bfloat16),
+            dma((8,)),
+            dma((8,)),
+            dma((4,)),
+            dma((4,)),
+        ],
+        compiler_params=pltpu.CompilerParams(collective_id=7, has_side_effects=True),
+        cost_estimate=pl.CostEstimate(
+            flops=0, bytes_accessed=40 * 1000 * 1000, transcendentals=0
+        ),
+    )(parts)
+
+
+def line_share_kernel(own_ref, all_ref, send_sem, recv_sem):
+    plane = lax.axis_index("hist")
+    barrier = pltpu.get_barrier_semaphore()
+    for place in range(4):
+
+        @pl.when(plane == place)
+        def _():
+            for p in range(4):
+                if p != place:
+                    pl.semaphore_signal(
+                        barrier, inc=1, device_id=z_place(p), device_id_type=DEVICE_MESH
+                    )
+
+    pl.semaphore_wait(barrier, 3)
+
+    def line_copy(source_place, target_place):
+        return pltpu.make_async_remote_copy(
+            src_ref=own_ref,
+            dst_ref=all_ref.at[source_place],
+            send_sem=send_sem.at[target_place],
+            recv_sem=recv_sem.at[source_place],
+            device_id=z_place(target_place),
+            device_id_type=DEVICE_MESH,
+        )
+
+    for place in range(4):
+
+        @pl.when(plane == place)
+        def _():
+            others = [p for p in range(4) if p != place]
+            for p in others:
+                line_copy(place, p).start()
+            all_ref[place] = own_ref[...]
+            for p in others:
+                line_copy(p, place).wait_recv()
+            for p in others:
+                line_copy(place, p).wait_send()
+
+
+def line_share(own):
+    dma = pltpu.SemaphoreType.DMA
+    return pl.pallas_call(
+        line_share_kernel,
+        out_shape=jax.ShapeDtypeStruct((4,) + own.shape, own.dtype),
+        in_specs=[pl.BlockSpec(memory_space=pltpu.VMEM)],
+        out_specs=pl.BlockSpec(memory_space=pltpu.VMEM),
+        scratch_shapes=[dma((4,)), dma((4,))],
+        compiler_params=pltpu.CompilerParams(collective_id=8, has_side_effects=True),
+        cost_estimate=pl.CostEstimate(
+            flops=0, bytes_accessed=20 * 1000 * 1000, transcendentals=0
+        ),
+    )(own)
 
 
 def attend_column(
@@ -1392,10 +1978,9 @@
     attn_columns_ref,
     x_ref,
     gain_ref,
-    grad_ref,
-    back3_ref,
-    down_term_ref,
+    down_own,
     up_term_ref,
+    kv_ref,
     full_ref,
     down_all_ref,
     up_all_ref,
@@ -1420,7 +2005,6 @@
     line_own,
     line_ends,
     line_held,
-    down_own,
     up_sum,
     up_own,
     stream_own,
@@ -1446,9 +2030,8 @@
 ):
     column = lax.axis_index("dp")
     plane = lax.axis_index("hist")
-    rows, features = grad_ref.shape
-    total = 8 * rows
-    width = q_ref.shape[1]
+    total, width = q_ref.shape
+    rows, features = total // 8, w_down_ref.shape[1]
     ff_share = w_down_ref.shape[0]
     quarter = features // 8 // 4
     k_grad, v_grad, attn_sum = q_grad, att, up_sum
@@ -1470,25 +2053,12 @@
                 )
             pl.semaphore_wait(barrier, 7 + len(nearby))
 
-    def key_copies(place):
-        return [
-            pltpu.make_async_remote_copy(
-                src_ref=source,
-                dst_ref=kv_before.at[:, pl.ds(i * width, width)],
-                send_sem=key_send.at[i],
-                recv_sem=key_recv.at[i],
-                device_id=z_place(place + 1),
-                device_id_type=DEVICE_MESH,
-            )
-            for i, source in enumerate((k_ref, v_ref))
-        ]
-
     def back_copy(place):
         return pltpu.make_async_remote_copy(
             src_ref=kv_before_grad,
             dst_ref=kv_after,
-            send_sem=key_send.at[2],
-            recv_sem=key_recv.at[2],
+            send_sem=key_send.at[0],
+            recv_sem=key_recv.at[0],
             device_id=z_place(place - 1),
             device_id_type=DEVICE_MESH,
         )
@@ -1503,13 +2073,6 @@
             return carry
 
         lax.fori_loop(0, target.shape[0] // step, some_rows, 0)
-
-    for place in range(3):
-
-        @pl.when(plane == place)
-        def _():
-            for copy in key_copies(place):
-                copy.start()
 
     line_sums = [
         LineSum(
@@ -1523,9 +2086,9 @@
             sum_recv.at[i],
             load_sem,
         )
-        for i, parts in enumerate((down_term_ref, up_term_ref, attn_parts_ref))
+        for i, parts in enumerate((up_term_ref, attn_parts_ref))
     ]
-    down_sum, up_line, attn_line = line_sums
+    up_line, attn_line = line_sums
 
     def spread(index, own, slot):
         return LineGather(
@@ -1535,31 +2098,16 @@
     def stream_spread(item):
         return spread(
             item,
-            stream_own.at[item],
-            lambda p: full_ref.at[pl.ds((item * 4 + p) * rows, rows)],
+            stream_own.at[item - 1],
+            lambda p: full_ref.at[pl.ds(((item - 1) * 4 + p) * rows, rows)],
         )
 
     def norm_back(item, back):
         load = pltpu.make_async_copy(x_ref.at[item], x_buf, local_sem.at[0])
         load.start()
         load.wait()
-        gain = gain_ref[pl.ds(item, 1), :]
-
-        def some_rows(r, gain_sum):
-            piece = pl.ds(pl.multiple_of(r * 16, 16), 16)
-            x = x_buf[piece, :]
-            inverse = lax.rsqrt(jnp.mean(x * x, axis=-1, keepdims=True) + epsilon)
-            grad = back[piece, :].astype(jnp.float32)
-            scaled = grad * gain
-            mean = jnp.mean(scaled * x, axis=-1, keepdims=True)
-            result = inverse * scaled - x * (inverse * inverse * inverse) * mean
-            if item == 0:
-                result = result + grad_ref[piece, :].astype(jnp.float32)
-            stream_own[item, piece, :] = result.astype(jnp.bfloat16)
-            return gain_sum + jnp.sum(grad * x * inverse, axis=0, keepdims=True)
-
-        gain_grad_ref[pl.ds(item, 1), :] = lax.fori_loop(
-            0, rows // 16, some_rows, jnp.zeros((1, features), jnp.float32)
+        norm_rows_back(
+            x_buf, back, gain_ref, gain_grad_ref, item, None, stream_own.at[item - 1]
         )
 
     def scatter_of(product, index):
@@ -1723,46 +2271,33 @@
         for copy in copies:
             copy.wait_send()
 
-    down_sum.start()
-    norm_back(0, back3_ref)
-    spread3 = stream_spread(0)
-    spread3.service(0)
+    up_line.start()
+    down_spread = spread(4, down_own, lambda p: down_all_ref.at[pl.ds(p * 4 * quarter, 4 * quarter)])
+    down_spread.service(0)
+    kv_load = pltpu.make_async_copy(kv_ref, kv_before, local_sem.at[0])
 
     @pl.when(plane == 0)
     def _():
         clear(kv_before)
         clear(line_ends.at[0])
 
+    @pl.when(plane > 0)
+    def _():
+        kv_load.start()
+        kv_load.wait()
+
     @pl.when(plane == 3)
     def _():
         clear(kv_after)
         clear(line_ends.at[1])
 
-    down_sum.service(0)
-    spread3.service(1)
-    down_sum.service(1)
-    for place in range(1, 4):
-
-        @pl.when(plane == place)
-        def _():
-            for copy in key_copies(place - 1):
-                copy.wait_recv()
-
-    attend(0, 4)
-    spread3.service(2)
-    down_sum.service(2)
-    up_line.start()
-    down_sum.finish(down_own)
-    down_spread = spread(4, down_own, lambda p: down_all_ref.at[pl.ds(p * 4 * quarter, 4 * quarter)])
-    down_spread.service(0)
-    attend(4, 4)
+    attend(0, 8)
     for place in range(1, 4):
 
         @pl.when(plane == place)
         def _():
             back_copy(place).start()
 
-    spread3.service(3)
     loading = load_big(normed_ref.at[0])
     query_scatter = scatter_of(projection_product(0, q_grad), 0)
     query_scatter.block(0)
@@ -1877,7 +2412,6 @@
     swapped_in(attn_swap)
     value_spread.service(3)
     for spreading in (
-        spread3,
         down_spread,
         query_spread,
         up_spread,
@@ -1885,13 +2419,6 @@
         value_spread,
     ):
         spreading.finish()
-    for place in range(3):
-
-        @pl.when(plane == place)
-        def _():
-            for copy in key_copies(place):
-                copy.wait_send()
-
     for place in range(1, 4):
 
         @pl.when(plane == place)
@@ -1915,15 +2442,14 @@
     attn_columns,
     x_ordered,
     gains,
-    grad_low,
-    back3,
-    down_term,
+    down_own,
     up_term,
+    kv_before,
     micro_count,
     sequence_length,
 ):
-    rows, features = grad_low.shape
     total, width = q.shape
+    rows, features = total // 8, w_down.shape[1]
     ff_share = w_down.shape[0]
     quarter = features // 32
     block = (rows, features)
@@ -1944,18 +2470,18 @@
         + [anywhere, anywhere]
         + [near] * 4
         + [anywhere]
-        + [near] * 3
+        + [near] * 2
         + [anywhere, anywhere],
         out_specs=[anywhere, anywhere, anywhere, near, near, near, anywhere, anywhere],
         out_shape=[
-            shape((16 * rows, features), low_type),
+            shape((12 * rows, features), low_type),
             shape((ff_share, features), low_type),
             shape((4 * quarter, 8 * ff_share), low_type),
             shape(piece, low_type),
             shape(block, low_type),
             shape((8, features), jnp.float32),
             shape((16 * quarter, features), low_type),
-            shape((18,) + piece, low_type),
+            shape((12,) + piece, low_type),
         ],
         scratch_shapes=[
             some(total, features),
@@ -1965,7 +2491,7 @@
             some(total, 2 * width),
             some(total, 2 * width),
             some(total, 2 * width),
-            some(4, *block),
+            some(2, *block),
             some(4, *block),
             some(4, *block),
             some(*half),
@@ -1975,9 +2501,8 @@
             some(2, *piece),
             some(3, *piece),
             some(*piece),
-            some(*piece),
             some(quarter, 8 * ff_share),
-            some(4, *block),
+            some(3, *block),
             some(*block),
             pltpu.VMEM(block, jnp.float32),
             some(*piece),
@@ -2019,10 +2544,9 @@
         attn_columns,
         x_ordered,
         gains,
-        grad_low,
-        back3,
-        down_term,
+        down_own,
         up_term,
+        kv_before,
     )
 
 
@@ -2038,17 +2562,6 @@
         jnp.concatenate([cosine, cosine], axis=-1),
         jnp.concatenate([-sine_part, sine_part], axis=-1),
     )
-
-
-def turned(values, cosine, sine_part, rows, sign):
-    total, width = values.shape
-    heads = values.reshape(total // rows, rows, width // HEAD_DIM, HEAD_DIM)
-    swapped = jnp.concatenate(
-        [heads[..., HEAD_DIM // 2 :], heads[..., : HEAD_DIM // 2]], axis=-1
-    )
-    return (
-        heads * cosine[None, :, None, :] + sign * swapped * sine_part[None, :, None, :]
-    ).reshape(total, width)
 
 
 def shards_split(
@@ -2073,39 +2586,47 @@
     rows = all_rows // planes
     share = features // columns
     mix_width = mix_in.shape[1]
-    ff_share = w_down.shape[0]
+    mix_rows = mix_out.shape[0]
     low = lambda values: values.astype(jnp.bfloat16)
-
-    top = jnp.concatenate(
-        [mix_in, norm_gains.T, jnp.zeros((share, 128 - mix_width - 5), jnp.bfloat16)], axis=1
-    )
-    mix_rows = mix_out.shape[0]
-    bottom = jnp.zeros((16, 128), jnp.bfloat16)
-    bottom = bottom.at[:mix_rows, :mix_width].set(mix_out)
-    bottom = bottom.at[0, mix_width : mix_width + micro_count].set(low(lengths))
-    packed = lax.all_gather(jnp.concatenate([top, bottom], axis=0), "dp", axis=0, tiled=False)
-    mix_in_all = packed[:, :share, :mix_width].reshape(features, mix_width)
-    gains_all = (
-        packed[:, :share, mix_width : mix_width + 5].reshape(features, 5).astype(jnp.float32).T
-    )
-    mixer_output_wide = (
-        packed[:, share : share + mix_rows, :mix_width]
-        .reshape(mix_width, mix_width)
-        .astype(jnp.float32)
-    )
-    lengths_all = (
-        packed[:, share, mix_width : mix_width + micro_count].reshape(-1).astype(jnp.int32)
-    )
-
-    chunk = sequence_length // planes
-    inverse_step = pow(micro_count, -1, planes)
-    received = []
-    for i in range(micro_count):
-        target = lax.rem((plane - i + planes * micro_count) * inverse_step, planes)
-        which = lax.div(target * micro_count + i, planes)
-        piece = lax.dynamic_index_in_dim(cotangent, which, 0, keepdims=False)
-        pairs = [(t, ((t - i) * inverse_step) % planes) for t in range(planes)]
-        received.append(lax.ppermute(piece, "hist", pairs))
+    order = (3, 0, 1, 2)
+
+    spare = 128 - mix_width
+    middle = jnp.concatenate(
+        [
+            jnp.pad(mix_out, ((0, 8 - mix_rows), (0, spare))),
+            jnp.pad(low(lengths)[None, :], ((0, 7), (0, 128 - micro_count))),
+        ],
+        axis=0,
+    )
+    gain_rows = jnp.pad(norm_gains, ((0, 3), (0, 0))).reshape(8, 2, share // 2)
+    pack = jnp.concatenate(
+        [
+            jnp.pad(mix_in, ((0, 0), (0, spare))),
+            middle,
+            gain_rows.transpose(1, 0, 2).reshape(16, share // 2),
+        ],
+        axis=0,
+    )
+
+    layer_lookup = (
+        history_layer_index[:, None] == jnp.arange(slot_count, dtype=jnp.int32)[None, :]
+    ).astype(jnp.float32)
+    newest_output = jnp.sum(
+        jnp.arange(slot_count, dtype=jnp.int32)
+        * (history_layer_index == slot_count - 1).astype(jnp.int32)
+    )
+    root = newest_output // local_slots
+    on_root = (plane == root).astype(jnp.float32)
+    latest_rows = lax.dynamic_index_in_dim(
+        history, newest_output % local_slots, 0, keepdims=False
+    ).reshape(all_rows, features)
+    own_table = lax.dynamic_slice_in_dim(layer_lookup, plane * local_slots, local_slots, 0)
+    ordered = jnp.eye(STREAM_COUNT, dtype=jnp.float32)[:, jnp.array(order)]
+    select = jnp.einsum("ci,sj->cjis", ordered, own_table).reshape(
+        STREAM_COUNT * slot_count, STREAM_COUNT * local_slots
+    )
+    select = low(jnp.pad(select, ((0, 0), (0, 128 - STREAM_COUNT * local_slots))))
+
     my_row = plane * rows + jnp.arange(rows, dtype=jnp.int32)
     my_position = lax.rem(my_row, sequence_length)
     my_sequence = lax.div(my_row, sequence_length)
@@ -2118,61 +2639,48 @@
         axis=1,
     )
     valid_rows = (my_position < my_length).astype(jnp.float32)[:, None]
-    grad_rows = jnp.concatenate(received, axis=0).astype(jnp.float32) * valid_rows
-
-    layer_lookup = (
-        history_layer_index[:, None] == jnp.arange(slot_count, dtype=jnp.int32)[None, :]
-    ).astype(jnp.float32)
-    newest_output = jnp.sum(
-        jnp.arange(slot_count, dtype=jnp.int32)
-        * (history_layer_index == slot_count - 1).astype(jnp.int32)
-    )
-    root = newest_output // local_slots
-    on_root = (plane == root).astype(jnp.float32)
-    latest_local = lax.dynamic_index_in_dim(history, newest_output % local_slots, 0, keepdims=False)
-    dyn_local, kept_mix = mix_forward(
-        latest_local.reshape(all_rows, features), gains_all[0], mix_in_all, mixer_output_wide
-    )
-    dyn_every = lax.all_gather(dyn_local, "hist", axis=0, tiled=False)
-    dyn = lax.dynamic_index_in_dim(dyn_every, root, 0, keepdims=False)
-    own_table = lax.dynamic_slice_in_dim(layer_lookup, plane * local_slots, local_slots, 0)
-    factors = jnp.einsum(
-        "tcj,sj->sct",
-        dyn.reshape(all_rows, STREAM_COUNT, slot_count),
-        own_table,
-        precision=highest,
-    )
-    flat_history = history.reshape(local_slots, all_rows, features)
-
-    def mixed(stream):
-        total = jnp.zeros((all_rows, features), jnp.float32)
-        for slot in range(local_slots):
-            total = total + factors[slot, stream][:, None] * flat_history[slot].astype(jnp.float32)
-        return low(total)
-
-    order = (3, 0, 1, 2)
-    parts = jnp.concatenate([mixed(stream) for stream in order], axis=0)
-    gains_ordered = jnp.pad(jnp.stack([gains_all[stream + 1] for stream in order]), ((0, 4), (0, 0)))
+    cosine, sine_part = rotary_table(my_position, HEAD_DIM)
+
     (
+        packed,
+        gains,
+        pre,
+        factors,
         x_ordered,
         normed_all,
         grad_all,
         hidden,
         up_term,
-        down_term,
-        back3,
+        down_own,
+        full3,
+        gain_sum3,
         attn_columns,
+        q,
+        k,
+        v,
+        out_grad,
+        kv_before,
         _,
-    ) = forward_and_feed(parts, low(grad_rows), w_up, w_attn, w_down, gains_ordered)
-    normed = [normed_all[0], normed_all[1], normed_all[2]]
-
-    cosine, sine_part = rotary_table(my_position, HEAD_DIM)
-    att_grad = low(
-        lax.dot_general(grad_all, w_out, contract_cols, preferred_element_type=jnp.float32)
-    )
-    q = low(turned(matmul(normed[0], attn_columns[0]), cosine, sine_part, rows, 1.0))
-    k = low(turned(matmul(normed[1], attn_columns[1]), cosine, sine_part, rows, 1.0))
-    v = low(matmul(normed[2], attn_columns[2]))
+        _,
+        _,
+        _,
+    ) = forward_and_feed(
+        lengths,
+        pack,
+        latest_rows,
+        history.reshape(local_slots * all_rows, features),
+        select,
+        jnp.broadcast_to(on_root, (8, all_rows)),
+        cotangent.reshape(rows, features),
+        w_up,
+        w_attn,
+        w_down,
+        w_out,
+        cosine,
+        sine_part,
+        sequence_length,
+    )
+    lengths_all = packed[:, share + 8, :micro_count].reshape(-1).astype(jnp.int32)
     full, down_all, up_all, attn_quarter, branch, gain_sums, _, _ = attend_and_back(
         lengths_all,
         cosine,
@@ -2180,7 +2688,7 @@
         q,
         k,
         v,
-        att_grad,
+        out_grad,
         normed_all,
         grad_all,
         hidden,
@@ -2188,14 +2696,17 @@
         w_down,
         attn_columns,
         x_ordered,
-        gains_ordered,
-        low(grad_rows),
-        back3,
-        down_term,
+        gains,
+        down_own,
         up_term,
+        kv_before,
         micro_count,
         sequence_length,
     )
+    attn_every = lax.all_gather(attn_quarter, "hist", axis=0, tiled=False)
+
+    chunk = sequence_length // planes
+    inverse_step = pow(micro_count, -1, planes)
     block_rows = low((x_ordered[0] + branch.astype(jnp.float32)) * valid_rows)
     block_out = jnp.zeros((micro_count, chunk, features), jnp.bfloat16)
     for i in range(micro_count):
@@ -2205,60 +2716,57 @@
         which = lax.div(source * micro_count + i, planes)
         block_out = lax.dynamic_update_index_in_dim(block_out, piece, which, 0)
 
-    full_ordered = full.reshape(STREAM_COUNT, all_rows, features)
-    full_grads = [
-        full_ordered[order.index(stream)].astype(jnp.float32) for stream in range(STREAM_COUNT)
+    flat_history = history.reshape(local_slots, all_rows, features)
+    full_rest = full.reshape(3, all_rows, features)
+    item_grads = [full3.astype(jnp.float32)] + [
+        full_rest[i].astype(jnp.float32) for i in range(3)
     ]
     inner = jnp.stack(
         [
-            jnp.stack(
-                [
-                    jnp.sum(full_grads[stream] * flat_history[slot].astype(jnp.float32), axis=-1)
-                    for slot in range(local_slots)
-                ],
-                axis=-1,
-            )
-            for stream in range(STREAM_COUNT)
+            jnp.sum(item_grads[item] * flat_history[slot].astype(jnp.float32), axis=-1)
+            for item in range(STREAM_COUNT)
+            for slot in range(local_slots)
         ],
-        axis=1,
-    )
-    dyn_part = jnp.einsum("tcs,sj->tcj", inner, own_table, precision=highest)
-    dyn_grad = jnp.sum(
-        lax.all_gather(
-            dyn_part.reshape(all_rows, STREAM_COUNT * slot_count), "hist", axis=0, tiled=False
-        ),
         axis=0,
     )
+    inner_all = line_share(inner)
+    mixer_output_wide = (
+        packed[:, share : share + mix_rows, :mix_width]
+        .reshape(mix_width, mix_width)
+        .astype(jnp.float32)
+    )
+    mix_in_all = packed[:, :share, :mix_width].reshape(features, mix_width)
+    tables = layer_lookup.reshape(planes, local_slots, slot_count)
+    dyn_grad = jnp.einsum(
+        "pist,ic,psj->tcj",
+        inner_all.reshape(planes, STREAM_COUNT, local_slots, all_rows),
+        ordered.T,
+        tables,
+        precision=highest,
+    ).reshape(all_rows, STREAM_COUNT * slot_count)
+    mixer_preactivation = pre[:, :mix_width]
+    mix_act = jax.nn.gelu(mixer_preactivation, approximate=False)
+    latest_values = latest_rows.astype(jnp.float32)
+    latest_scaled, latest_inverse = rms_scale(latest_values, gains[0])
+    kept_mix = (latest_values, latest_inverse, low(latest_scaled), mixer_preactivation, mix_act)
     act_grad = precise(dyn_grad, mixer_output_wide.T)
-    mix_out_grad = precise(kept_mix[4].T, dyn_grad) * on_root
-    latest_grad, gain_zero, mix_in_grad = mix_backward(kept_mix, act_grad, gains_all[0], mix_in_all)
+    mix_out_grad = precise(mix_act.T, dyn_grad) * on_root
+    latest_grad, gain_zero, mix_in_grad = mix_backward(kept_mix, act_grad, gains[0], mix_in_all)
     slot_grads = []
     for slot in range(local_slots):
         is_latest = (plane * local_slots + slot == newest_output).astype(jnp.float32)
         slot_grad = latest_grad * is_latest
-        for stream in range(STREAM_COUNT):
-            slot_grad = slot_grad + factors[slot, stream][:, None] * full_grads[stream]
+        for item in range(STREAM_COUNT):
+            one = item * local_slots + slot
+            slot_grad = slot_grad + factors[:, one : one + 1] * item_grads[item]
         slot_grads.append(low(slot_grad))
     history_grad = jnp.stack(slot_grads).reshape(history.shape)
-
-    attn_every = lax.all_gather(attn_quarter, "hist", axis=0, tiled=False).astype(jnp.float32)
-    part = share // planes
-    w_attn_grad = (
-        attn_every[:, : 3 * part]
-        .reshape(planes, 3, part, features)
-        .transpose(1, 0, 2, 3)
-        .reshape(3, share, features)
-    )
-    w_out_grad = attn_every[:, 3 * part :].reshape(share, features)
-    w_down_grad = down_all.astype(jnp.float32)
-    w_up_grad = up_all.astype(jnp.float32)
 
     small_top = jnp.concatenate(
         [
             mix_in_grad * on_root,
             jnp.stack(
-                [gain_zero * on_root]
-                + [gain_sums[order.index(stream)] for stream in range(STREAM_COUNT)]
+                [gain_zero * on_root, gain_sums[1], gain_sums[2], gain_sums[3], gain_sum3[0]]
             ).T,
             jnp.zeros((features, 128 - mix_width - 5), jnp.float32),
         ],
@@ -2268,9 +2776,17 @@
         mix_out_grad.reshape(columns, mix_rows, mix_width),
         ((0, 0), (0, 16 - mix_rows), (0, 128 - mix_width)),
     )
-    small = low(jnp.concatenate([small_top, small_bottom], axis=1))
-    small = lax.psum_scatter(small, "dp", scatter_dimension=0, tiled=False)
-    small = lax.psum(small, "hist").astype(jnp.float32)
+    small = small_sums(low(jnp.concatenate([small_top, small_bottom], axis=1)))
+
+    part = share // planes
+    w_attn_grad = (
+        attn_every[:, : 3 * part]
+        .astype(jnp.float32)
+        .reshape(planes, 3, part, features)
+        .transpose(1, 0, 2, 3)
+        .reshape(3, share, features)
+    )
+    w_out_grad = attn_every[:, 3 * part :].astype(jnp.float32).reshape(share, features)
     return (
         block_out,
         history_grad,
@@ -2279,8 +2795,8 @@
         small[share : share + mix_rows, :mix_width],
         w_attn_grad,
         w_out_grad,
-        w_up_grad,
-        w_down_grad,
+        up_all.astype(jnp.float32),
+        down_all.astype(jnp.float32),
     )
 
 

time: 1250 us -> 998 us (0.80)
  waiting for transfers between devices: 102 us -> 0.05 us
  other arithmetic: 127 us -> 69 us
  blocking collectives: 46.7 us -> 0 us
  local copies, waits for them, and re-layouts: 60.9 us -> 42.6 us
  matrix products: 31.4 us -> 17.4 us
    pallas_call x1, Pallas kernels: 537 us -> 406 us  [attend_and_back(): pl.pallas_call(functools.partial(backward_kernel, micro_count=micro_count...]
    pallas_call x1 -> x3, Pallas kernels: 299 us -> 428 us  [the longest x1 392 us: forward_and_feed(): pl.pallas_call(functools.partial(forward_kernel, micro_count=micro_count,...]
    all_gather x1, waiting for transfers between devices: 57.1 us -> 0.02 us  [shards_split(): attn_every = lax.all_gather(attn_quarter, 'hist', axis=0, tiled=False)]
    all_gather x3 -> x0, blocking collectives: 46.7 us -> none  [the longest x1 19.9 us: shards_split(): dyn_every = lax.all_gather(dyn_local, 'hist', axis=0, tiled=False)]
    reduce_scatter x1 -> x0, waiting for transfers between devices: 31.5 us -> none  [shards_split(): small = lax.psum_scatter(small, 'dp', scatter_dimension=0, tiled=False)]
    concatenate x4 -> x3, other arithmetic: 30.3 us -> 1.62 us  [the longest x1 0.84 us: shards_split(): small = small_sums(low(jnp.concatenate([small_top, small_bottom], axis=1)))]
    dot_general x7 -> x2, matrix products: 19.6 us -> 0.73 us  [shards_split(): jnp.einsum('pist,ic,psj->tcj', inner_all.reshape(planes, STREAM_COUNT, lo...]
    convert_element_type x8 -> x5, other arithmetic: 43.1 us -> 25.9 us  [shards_split(): low = lambda values: values.astype(jnp.bfloat16)]
  transfers between devices with their start and end apart: 9 -> 4, of which waited for: 4 -> 0; matrix products, arithmetic and copies ran while one was open for 10% -> 10% of each run, Pallas kernels for 0% -> 4%
where the time goes in v3:
time: 998 us; the launch traced here: 989 us
  Pallas kernels  833 us (83%)
  other arithmetic  69 us (7%)
  local copies, waits for them, and re-layouts  42.6 us (4%)
  between operations  20 us (2%)
  matrix products  17.4 us (2%)
    pallas_call x1, Pallas kernels, attend_and_back(): pl.pallas_call(functools.partial(backward_kernel, micro_count=micro_count...  406 us
    pallas_call x1, Pallas kernels, forward_and_feed(): pl.pallas_call(functools.partial(forward_kernel, micro_count=micro_count,...  392 us
    convert_element_type x5, other arithmetic, shards_split(): low = lambda values: values.astype(jnp.bfloat16)  25.9 us
    pallas_call x1, Pallas kernels, small_sums(): pl.pallas_call(small_sum_kernel, out_shape=jax.ShapeDtypeStruct(dims, jnp...  23.2 us
  transfers between devices with their start and end apart: 4, of which 0 were waited for; matrix products, arithmetic and copies ran while one was open for 10% of the time, Pallas kernels for 4%

profile of v3, /device:TPU:0, one launch (start us, length us, event | category | flops | bytes accessed | tf_op | source)
XLA Modules:
  0.0 988.8 jit_solution(14661762341907194022)
XLA Ops:
  7.2 1.3 fusion.174
  16.9 4.2 multiply_reduce_fusion
  23.7 392.2 %shard_map.187 = (bf16[8,288,128]{2,1,0:T(8,128)(2,1)}, f32[8,2048]{1,0:T(8,128)}, f32[768,128]{1,0:T(8,128)}, f32[768,128]{1,0:T(8,128)}, f32[4,192,2048]{2,1,0...) custom-call(s32[3]{0:T(128)} %length_ref.1, ...), custom_call_target="tpu_custom_call" | custom-call | flops 38654705664 | bytes 600000000 | tf_op jit(solution)/shard_map/pallas_call | solution.py:1672
  417.3 405.5 %shard_map.188 = (bf16[2304,2048]{1,0:T(8,128)(2,1)}, bf16[1024,2048]{1,0:T(8,128)(2,1)}, bf16[256,8192]{1,0:T(8,128)(2,1)}, bf16[256,2048]{1,0:T(8,128)(2,1)}, ...) custom-call(s32[24]{0:T(128)} %reshape.202.length_ref, ...), custom_call_target="tpu_custom_call" | custom-call | flops 16106127360 | bytes 1000000000 | tf_op jit(solution)/shard_map/pallas_call | solution.py:2464
  822.9 1.9 fusion.54
  825.7 3.6 collective-permute-start
  829.3 3.0 collective-permute-start.2
  832.3 8.6 fusion.206
  841.8 1.9 slice.156
  843.7 13.5 %fusion.42 = (f32[768]{0:T(1024)S(1)}, f32[768]{0:T(1024)S(1)}, f32[768]{0:T(1024)S(1)}, f32[768]{0:T(1024)S(1)}, f32[768]{0:T(1024)S(1)}, /*index=5*/f32[768]{0...) fusion(bf16[1,3,256,2048]{3,2,1,0:T(8,128)(2,1)} %get-tuple-ele, ...), kind=kLoop, calls=%fused_computation.80 | loop fusion | flops 62902272 | bytes 25214976 | tf_op jit(solution)/shard_map/reduce_sum | solution.py:2726
  857.4 1.3 stack.88.own_ref
  858.7 12.2 %shard_map.189 = f32[4,16,768]{2,1,0:T(8,128)} custom-call(f32[16,768]{1,0:T(8,128)} %stack.88.own_ref), custom_call_target="tpu_custom_call" | custom-call | bytes 20000000 | tf_op jit(solution)/shard_map/pallas_call | solution.py:1883
  870.9 1.0 reshape.191
  872.7 2.3 convolution_multiply_fusion
  874.9 2.5 fusion.57
  878.2 3.2 fusion.50
  881.3 8.7 fusion.6
  892.4 3.2 slice_reduce_fusion.15
  897.6 10.4 %fusion.15 = bf16[768,2048]{1,0:T(8,128)(2,1)S(1)} fusion(bf16[768,2048]{1,0:T(8,128)(2,1)} %get-tuple-element.48, f32[768]{0:T(1024)S(1)} %get-tuple-element.124, f32[768]{0:T(1024)S(1)} %get-tuple-element.125, f32[768]{0:T(1024)S(1)} %get-tuple-element.126, f32[768]{0:T(1024)S(1)} %get-tuple-element.111, f32[]{:T(128)S(6)} %convert_element_type.162, ...), kind=kLoop, calls=%fused_computation.53 | loop fusion | flops 31457280 | bytes 25195524 | tf_op jit(solution)/shard_map/convert_element_type | solution.py:2590
  910.7 4.5 fusion.20
  915.2 4.6 fusion.25
  919.8 4.6 fusion.30
  924.3 5.5 pad_maximum_fusion
  930.6 23.2 %shard_map.190 = f32[272,128]{1,0:T(8,128)} custom-call(bf16[8,272,128]{2,1,0:T(8,128)(2,1)} %fusion.58.parts_ref), custom_call_target="tpu_custom_call" | custom-call | bytes 40000000 | tf_op jit(solution)/shard_map/pallas_call | solution.py:1822
  954.7 1.3 slice.178
  956.7 1.0 slice_bitcast_fusion
  958.4 6.7 convert_element_type.171
  965.1 4.4 convert_element_type.172
  972.7 2.6 slice.188
  975.2 1.3 slice.189
  976.6 3.6 copy.42
  980.1 1.6 bitcast_convert_fusion
  (105 shorter events, 23.6 us)
Async XLA Ops:
  7.2 15.2 %copy-start.7 = (bf16[8,64]{1,0:T(8,128)(2,1)S(1)}, bf16[8,64]{1,0:T(8,128)(2,1)}, u32[]{:S(2)}) copy-start(bf16[8,64]{1,0:T(8,128)(2,1)} %param.17) | copy-start | bytes 3076
  7.2 965.5 %all-gather.3.cloned.1.call-start = ((), (), s32[]{:S(2)}) async-start(), calls=%async_computation | async-start | bytes 5242880 | tf_op jit(solution)/shard_map/all_gather | solution.py:2706
  417.3 405.5 %copy-start.8 = (s32[3]{0:T(128)S(1)}, s32[3]{0:T(128)}, u32[]{:S(2)}) copy-start(s32[3]{0:T(128)} %length_ref.1) | copy-start | bytes 40
  825.7 143.9 %collective-permute-start = (bf16[64,2048]{1,0:T(8,128)(2,1)}, bf16[64,2048]{1,0:T(8,128)(2,1)}, u32[]{:S(2)}, u32[]{:S(2)}) collective-permute-start(bf16[64,2048]{1,0:T(8,128)(2,1)} %get-tuple-element.135), channel_id=1, source_target_pairs={{0,0},{1,3},{2,2},{3,1},{4,4},{5,7},{6,6},{7,5},{8,8},{9,11},{10,1... | collective-permute-start | bytes 786440 | tf_op jit(solution)/shard_map/ppermute | solution.py:2714
  829.3 141.3 %collective-permute-start.1 = (bf16[64,2048]{1,0:T(8,128)(2,1)}, bf16[64,2048]{1,0:T(8,128)(2,1)}, u32[]{:S(2)}, u32[]{:S(2)}) collective-permute-start(bf16[64,2048]{1,0:T(8,128)(2,1)} %get-tuple-element.134), channel_id=1, source_target_pairs={{0,1},{1,0},{2,3},{3,2},{4,5},{5,4},{6,7},{7,6},{8,9},{9,8},{10,11... | collective-permute-start | bytes 786440 | tf_op jit(solution)/shard_map/ppermute | solution.py:2714
  829.3 11.6 %copy-start.9 = (s32[16]{0:T(128)S(1)}, s32[16]{0:T(128)}, u32[]{:S(2)}) copy-start(s32[16]{0:T(128)} %param.13) | copy-start | bytes 196
  829.3 14.4 %copy-start.3 = (bf16[768,2048]{1,0:T(8,128)(2,1)S(1)}, bf16[768,2048]{1,0:T(8,128)(2,1)}, u32[]{:S(2)}) copy-start(bf16[768,2048]{1,0:T(8,128)(2,1)} %get-tuple-element.48) | copy-start | bytes 9437188
  829.3 142.3 %collective-permute-start.2 = (bf16[64,2048]{1,0:T(8,128)(2,1)}, bf16[64,2048]{1,0:T(8,128)(2,1)}, u32[]{:S(2)}, u32[]{:S(2)}) collective-permute-start(bf16[64,2048]{1,0:T(8,128)(2,1)} %get-tuple-element.133), channel_id=1, source_target_pairs={{0,2},{1,1},{2,0},{3,3},{4,6},{5,5},{6,4},{7,7},{8,10},{9,9},{10,8... | collective-permute-start | bytes 786440 | tf_op jit(solution)/shard_map/ppermute | solution.py:2714
  857.2 20.9 %copy-start.1 = (bf16[1,3,256,2048]{3,2,1,0:T(8,128)(2,1)S(1)}, bf16[1,3,256,2048]{3,2,1,0:T(8,128)(2,1)}, u32[]{:S(2)}) copy-start(bf16[1,3,256,2048]{3,2,1,0:T(8,128)(2,1)} %get-tuple-element.128) | copy-start | bytes 9437188
  881.3 11.0 %copy-start = (f32[768,128]{1,0:T(8,128)S(1)}, f32[768,128]{1,0:T(8,128)}, u32[]{:S(2)}) copy-start(f32[768,128]{1,0:T(8,128)} %get-tuple-element.51) | copy-start | bytes 1179652
  892.3 15.7 %slice-start.3 = ((s8[6291456]{0:T(1024)(128)(4,1)}), s8[2097152]{0:T(1024)(128)(4,1)S(1)}, s32[]{:S(2)}) async-start(s8[6291456]{0:T(1024)(128)(4,1)} %bitcast.108), calls=%async_computation.4 | async-start | bytes 4194304
  897.5 10.5 %slice-start = ((s8[9437184]{0:T(1024)(128)(4,1)}), s8[4194304]{0:T(1024)(128)(4,1)S(1)}, s32[]{:S(2)}) async-start(s8[9437184]{0:T(1024)(128)(4,1)} %bitcast.106), calls=%async_computation.1 | async-start | bytes 8388608
  897.6 10.5 %slice-start.1 = ((s8[9437184]{0:T(1024)(128)(4,1)}), s8[4194304]{0:T(1024)(128)(4,1)S(1)}, s32[]{:S(2)}) async-start(s8[9437184]{0:T(1024)(128)(4,1)} %bitcast.106), calls=%async_computation.2 | async-start | bytes 8388608
  897.6 10.5 %slice-start.2 = ((s8[9437184]{0:T(1024)(128)(4,1)}), s8[1048576]{0:T(1024)(128)(4,1)S(1)}, s32[]{:S(2)}) async-start(s8[9437184]{0:T(1024)(128)(4,1)} %bitcast.106), calls=%async_computation.3 | async-start | bytes 2097152
  897.6 11.3 %slice-start.4 = ((s8[6291456]{0:T(1024)(128)(4,1)}), s8[4194304]{0:T(1024)(128)(4,1)S(1)}, s32[]{:S(2)}) async-start(s8[6291456]{0:T(1024)(128)(4,1)} %bitcast.108), calls=%async_computation.5 | async-start | bytes 8388608
  897.6 12.2 %copy-start.2 = (bf16[1,3,256,2048]{3,2,1,0:T(8,128)(2,1)S(1)}, bf16[1,3,256,2048]{3,2,1,0:T(8,128)(2,1)}, u32[]{:S(2)}) copy-start(bf16[1,3,256,2048]{3,2,1,0:T(8,128)(2,1)} %get-tuple-element.128) | copy-start | bytes 9437188
  897.6 13.1 %copy-start.4 = (bf16[768,2048]{1,0:T(8,128)(2,1)S(1)}, bf16[768,2048]{1,0:T(8,128)(2,1)}, u32[]{:S(2)}) copy-start(bf16[768,2048]{1,0:T(8,128)(2,1)} %get-tuple-element.48) | copy-start | bytes 9437188
  958.4 6.7 copy-start.5
  972.6 7.5 copy-start.6
Sparse Core Ops, SparseCore 0:
  822.9 90.2 all-gather.2

commit v4 on v3

--- a/solution.py
+++ b/solution.py
@@ -677,14 +677,12 @@
     def relay(self, way, turn, a):
         return self.message(way, turn, a, self.held.at[self.slot(way, a, turn)])
 
-    def start(self):
+    def start(self, turn):
         for place in (0, 3):
 
             @pl.when(self.plane == place)
             def _():
-                way = 0 if place == 0 else 1
-                self.origin(way, 0).start()
-                self.origin(way, 1).start()
+                self.origin(0 if place == 0 else 1, turn).start()
 
     def load(self, source, target, index):
         return pltpu.make_async_copy(source, target, self.load_sem.at[index])
@@ -759,15 +757,17 @@
 
 class LineSum:
 
-    def __init__(self, plane, parts, arrived, own, last, held, send_sem, recv_sem, load_sem):
+    def __init__(
+        self, plane, parts, arrived, own, last, held, send_sem, recv_sem, load_sem, stride, first
+    ):
         self.plane, self.parts, self.arrived = plane, parts, arrived
         self.own, self.last, self.held = own, last, held
         self.send_sem, self.recv_sem, self.load_sem = send_sem, recv_sem, load_sem
-        self.rows = own.shape[0]
+        self.rows, self.stride, self.first = own.shape[0], stride, first
 
     def part(self, way, b):
         place = b if way == 0 else 3 - b
-        return self.parts.at[pl.ds(place * self.rows, self.rows)]
+        return self.parts.at[pl.ds(place * self.stride + self.first, self.rows)]
 
     def message(self, way, t, a, source):
         return pltpu.make_async_remote_copy(
@@ -889,12 +889,18 @@
                     if a < 3:
                         self.message(way, a, step).start()
 
-    def finish(self):
+    def placed(self):
         for place in range(4):
 
             @pl.when(self.plane == place)
             def _():
                 pltpu.make_async_copy(self.own, self.slot(place), self.local_sem).wait()
+
+    def finish(self):
+        for place in range(4):
+
+            @pl.when(self.plane == place)
+            def _():
                 for way in (0, 1):
                     a = place if way == 0 else 3 - place
                     if a < 3:
@@ -958,7 +964,7 @@
     k_ref,
     v_ref,
     out_grad_ref,
-    kv_before_ref,
+    key_before_ref,
     part_ref,
     down_term_ref,
     arrived_ref,
@@ -1193,6 +1199,18 @@
         dyn_sum, select_ref[...], contract_rows, preferred_element_type=jnp.float32
     )
 
+    block = pl.ds(0, rows)
+    line = LineSums(
+        plane,
+        part_ref,
+        arrived_ref,
+        own.at[block],
+        ends.at[:, block],
+        held.at[:, block],
+        line_send,
+        line_recv,
+        line_load,
+    )
     stores = [None, None]
     for i, p in enumerate(block_order):
         h = i % 2
@@ -1237,23 +1255,15 @@
             copy.start()
         if i + 2 < 4:
             loads.append(history_loads(i + 2))
-    for copies in stores:
-        for copy in copies:
-            copy.wait()
-
-    block = pl.ds(0, rows)
-    line = LineSums(
-        plane,
-        part_ref,
-        arrived_ref,
-        own.at[block],
-        ends.at[:, block],
-        held.at[:, block],
-        line_send,
-        line_recv,
-        line_load,
-    )
-    line.start()
+        if i % 2 == 1:
+            for copies in stores:
+                for copy in copies:
+                    copy.wait()
+            stores = [None, None]
+        if i == 1:
+            line.start(0)
+
+    line.start(1)
     for mask in (CORE, ACROSS_X, ACROSS_Y):
         pl.semaphore_signal(
             ready_sem, inc=1, device_id={"dp": partner(column, mask)}, device_id_type=DEVICE_MESH
@@ -1261,26 +1271,6 @@
 
     def attn_piece(stream, owner):
         return w_attn_ref.at[stream, :, pl.ds(pl.multiple_of(owner * share, 128), share)]
-
-    attn_swaps, attn_locals = [], []
-    for stream in range(3):
-        local = pltpu.make_async_copy(
-            attn_piece(stream, column),
-            attn_columns.at[stream, my_rows],
-            swap_local.at[1 + stream],
-        )
-        local.start()
-        attn_locals.append(local)
-        for mask in every_mask:
-            attn_swaps.append(
-                push(
-                    attn_piece(stream, partner(column, mask)),
-                    attn_columns.at[stream, my_rows],
-                    swap_send.at[8 * (stream + 1) + mask],
-                    swap_recv.at[8 * (stream + 1) + mask],
-                    partner(column, mask),
-                )
-            )
 
     def gather(index, own_rows, whole):
         return PlaneGatherSteps(
@@ -1351,23 +1341,42 @@
 
     line.service(0)
     line.service(1)
+    grad_gather.corners()
+    grad_gather.siblings()
     line.service(2)
     gather3 = combine(0)
-    grad_gather.corners()
-    grad_gather.siblings()
-    line.service(3)
     grad_gather.rest()
-    gather3.corners()
-    line.service(4)
     grad_gather.finish()
     grads_out = pltpu.make_async_copy(grads, grad_all_ref, out_sem.at[2])
     grads_out.start()
+    gather3.corners()
+    line.service(3)
     gather3.siblings()
     gather3.rest()
+    line.service(4)
     for copy in up_swaps:
         copy.wait_recv()
     up_local.wait()
     gather3.finish()
+    attn_swaps, attn_locals = [], []
+    for stream in range(3):
+        local = pltpu.make_async_copy(
+            attn_piece(stream, column),
+            attn_columns.at[stream, my_rows],
+            swap_local.at[1 + stream],
+        )
+        local.start()
+        attn_locals.append(local)
+        for mask in every_mask:
+            attn_swaps.append(
+                push(
+                    attn_piece(stream, partner(column, mask)),
+                    attn_columns.at[stream, my_rows],
+                    swap_send.at[8 * (stream + 1) + mask],
+                    swap_recv.at[8 * (stream + 1) + mask],
+                    partner(column, mask),
+                )
+            )
 
     def feed(first_block, count):
         def one_tile(step, carry):
@@ -1482,33 +1491,26 @@
         ).astype(jnp.bfloat16)
         return carry
 
-    def key_copy(i, place):
+    def key_copy(place):
         return pltpu.make_async_remote_copy(
-            src_ref=(k_ref, v_ref)[i],
-            dst_ref=kv_before_ref.at[:, pl.ds(i * width, width)],
-            send_sem=key_send.at[i],
-            recv_sem=key_recv.at[i],
+            src_ref=k_ref,
+            dst_ref=key_before_ref,
+            send_sem=key_send.at[0],
+            recv_sem=key_recv.at[0],
             device_id=z_place(place + 1),
             device_id_type=DEVICE_MESH,
         )
-
-    def send_keys(i):
-        for place in range(3):
-
-            @pl.when(plane == place)
-            def _():
-                key_copy(i, place).start()
 
     feed(0, 2)
     line.service(5)
     gather0 = combine(1)
-    feed(2, 3)
+    feed(2, 2)
+    line.service(6)
     gather0.corners()
-    line.service(6)
-    feed(5, 2)
+    feed(4, 2)
+    line.service(7)
     gather0.siblings()
-    line.service(7)
-    feed(7, 1)
+    feed(6, 2)
     gather0.rest()
     scatter = PlaneScatterSteps(
         column,
@@ -1518,16 +1520,18 @@
         scatter_recv,
     )
     scatter.block(0)
-    scatter.block(1)
     line.service(8)
     gather1 = combine(2)
+    scatter.block(1)
     scatter.block(2)
     scatter.block(3)
     gather0.finish()
+    terms(1, 0, 2)
+    line.service(9)
     scatter.turn()
-    terms(1, 0, 2)
     gather1.corners()
-    line.service(9)
+    terms(1, 2, ff_share // tile - 2)
+    line.service(10)
     scatter.finish(None)
     x_copies[-1].wait()
     x_load = pltpu.make_async_copy(x_ref.at[0], x_buf, out_sem.at[1])
@@ -1545,44 +1549,55 @@
     )
     spread3.service(0)
     gather1.siblings()
-    terms(1, 2, ff_share // tile - 2)
-    gather1.rest()
     down_line = LineSum(
-        plane, down_term_ref, arrived_down_ref, own, ends, held, sum_send, sum_recv, line_load
-    )
-    line.service(10)
-    spread3.service(1)
-    down_line.start()
-    terms(0, 0, 2)
-    spread3.service(2)
+        plane,
+        down_term_ref,
+        arrived_down_ref,
+        own,
+        ends,
+        held,
+        sum_send,
+        sum_recv,
+        line_load,
+        share,
+        0,
+    )
     line.service(11)
     gather2 = combine(3)
-    terms(0, 2, features // tile - 2)
-    spread3.service(3)
+    down_line.start()
+    gather1.rest()
+    terms(0, 0, features // tile)
     line.drain()
     gather1.finish()
+    load = block_load(normed_ref.at[1], normed3, 0)
+    gather2.corners()
     for copy in attn_swaps:
         copy.wait_recv()
     for copy in attn_locals:
         copy.wait()
-    load = block_load(normed_ref.at[1], normed3, 0)
-    gather2.corners()
+    spread3.service(1)
     load.wait()
     project(1, k_ref)
-    send_keys(0)
+    for place in range(3):
+
+        @pl.when(plane == place)
+        def _():
+            key_copy(place).start()
+
+    load = block_load(normed_ref.at[0], normed3, 0)
     down_line.service(0)
-    load = block_load(normed_ref.at[0], normed3, 0)
     gather2.siblings()
     gather2.rest()
     load.wait()
     project(0, q_ref)
+    spread3.service(2)
+    lax.fori_loop(0, 8, out_grads, 0)
     gather2.finish()
     load = block_load(normed_ref.at[2], normed3, 0)
-    lax.fori_loop(0, 8, out_grads, 0)
+    down_line.service(1)
     load.wait()
     project(2, v_ref)
-    send_keys(1)
-    down_line.service(1)
+    spread3.service(3)
     for copy in small_copies + up_swaps + attn_swaps:
         copy.wait_send()
     grads_out.wait()
@@ -1601,16 +1616,16 @@
 
     down_line.service(2)
     down_line.finish(down_sum_ref)
+    spread3.placed()
     spread3.finish()
     for place in range(4):
 
         @pl.when(plane == place)
         def _():
-            for i in range(2):
-                if place > 0:
-                    key_copy(i, place - 1).wait_recv()
-                if place < 3:
-                    key_copy(i, place).wait_send()
+            if place > 0:
+                key_copy(place - 1).wait_recv()
+            if place < 3:
+                key_copy(place).wait_send()
 
 
 def forward_and_feed(
@@ -1636,7 +1651,7 @@
     ff_share = w_down.shape[0]
     mix_width = select.shape[0]
     block = (rows, features)
-    piece = (4 * (share // 4), features)
+    piece = (share, features)
     half = (2, rows // 2, features)
     anywhere = pl.BlockSpec(memory_space=pl.ANY)
     near = pl.BlockSpec(memory_space=pltpu.VMEM)
@@ -1663,7 +1678,7 @@
         (near, shape((total, share), low_type)),
         (near, shape((total, share), low_type)),
         (near, shape((total, share), low_type)),
-        (anywhere, shape((total, 2 * share), low_type)),
+        (anywhere, shape((total, share), low_type)),
         (anywhere, shape((16 * rows, features), low_type)),
         (anywhere, shape((ff_share, features), low_type)),
         (anywhere, shape((24,) + block, low_type)),
@@ -1722,8 +1737,8 @@
             dma((6,)),
             dma((6,)),
             dma((6,)),
-            dma((2,)),
-            dma((2,)),
+            dma((1,)),
+            dma((1,)),
             pltpu.SemaphoreType.REGULAR,
         ],
         compiler_params=pltpu.CompilerParams(
@@ -1839,58 +1854,77 @@
     )(parts)
 
 
-def line_share_kernel(own_ref, all_ref, send_sem, recv_sem):
-    plane = lax.axis_index("hist")
-    barrier = pltpu.get_barrier_semaphore()
-    for place in range(4):
-
-        @pl.when(plane == place)
-        def _():
-            for p in range(4):
-                if p != place:
-                    pl.semaphore_signal(
-                        barrier, inc=1, device_id=z_place(p), device_id_type=DEVICE_MESH
-                    )
-
-    pl.semaphore_wait(barrier, 3)
-
-    def line_copy(source_place, target_place):
-        return pltpu.make_async_remote_copy(
-            src_ref=own_ref,
-            dst_ref=all_ref.at[source_place],
-            send_sem=send_sem.at[target_place],
-            recv_sem=recv_sem.at[source_place],
-            device_id=z_place(target_place),
-            device_id_type=DEVICE_MESH,
-        )
-
-    for place in range(4):
-
-        @pl.when(plane == place)
-        def _():
-            others = [p for p in range(4) if p != place]
-            for p in others:
-                line_copy(place, p).start()
-            all_ref[place] = own_ref[...]
-            for p in others:
-                line_copy(p, place).wait_recv()
-            for p in others:
-                line_copy(place, p).wait_send()
-
-
-def line_share(own):
-    dma = pltpu.SemaphoreType.DMA
+def slot_grad_kernel(
+    latest_ref, factor_ref, first_ref, rest_ref, latest_grad_ref, out_ref
+):
+    grads = [first_ref[...].astype(jnp.float32)] + [
+        rest_ref[i].astype(jnp.float32) for i in range(3)
+    ]
+    latest_grad = latest_grad_ref[...]
+    factors = factor_ref[...]
+    for slot in range(4):
+        total = latest_grad * latest_ref[slot]
+        for item in range(4):
+            one = item * 4 + slot
+            total = total + factors[:, one : one + 1] * grads[item]
+        out_ref[slot] = total.astype(jnp.bfloat16)
+
+
+def slot_grads_of(latest_here, factors, first, rest, latest_grad):
+    total, features = first.shape
+    step = 32
+    rows_of = lambda *lead: pl.BlockSpec(
+        lead + (step, features), lambda r: (0,) * len(lead) + (r, 0)
+    )
     return pl.pallas_call(
-        line_share_kernel,
-        out_shape=jax.ShapeDtypeStruct((4,) + own.shape, own.dtype),
-        in_specs=[pl.BlockSpec(memory_space=pltpu.VMEM)],
-        out_specs=pl.BlockSpec(memory_space=pltpu.VMEM),
-        scratch_shapes=[dma((4,)), dma((4,))],
-        compiler_params=pltpu.CompilerParams(collective_id=8, has_side_effects=True),
+        slot_grad_kernel,
+        grid=(total // step,),
+        in_specs=[
+            pl.BlockSpec(memory_space=pltpu.SMEM),
+            pl.BlockSpec((step, 128), lambda r: (r, 0)),
+            rows_of(),
+            rows_of(3),
+            rows_of(),
+        ],
+        out_specs=rows_of(4),
+        out_shape=jax.ShapeDtypeStruct((4, total, features), jnp.bfloat16),
+        compiler_params=pltpu.CompilerParams(vmem_limit_bytes=24 * 1024 * 1024),
         cost_estimate=pl.CostEstimate(
-            flops=0, bytes_accessed=20 * 1000 * 1000, transcendentals=0
+            flops=40 * total * features, bytes_accessed=20 * total * features, transcendentals=0
         ),
-    )(own)
+    )(latest_here, factors, first, rest, latest_grad)
+
+
+def lay_out_kernel(part_ref, attn_ref, out_ref):
+    quarter = out_ref.shape[0]
+    for stream in range(3):
+        attn_ref[stream] = part_ref[stream * quarter : (stream + 1) * quarter, :].astype(
+            jnp.float32
+        )
+    out_ref[...] = part_ref[3 * quarter :, :].astype(jnp.float32)
+
+
+def lay_out(parts):
+    total, features = parts.shape
+    step = total // 4
+    quarter = step // 4
+    return pl.pallas_call(
+        lay_out_kernel,
+        grid=(4,),
+        in_specs=[pl.BlockSpec((step, features), lambda p: (p, 0))],
+        out_specs=[
+            pl.BlockSpec((3, quarter, features), lambda p: (0, p, 0)),
+            pl.BlockSpec((quarter, features), lambda p: (p, 0)),
+        ],
+        out_shape=[
+            jax.ShapeDtypeStruct((3, step, features), jnp.float32),
+            jax.ShapeDtypeStruct((step, features), jnp.float32),
+        ],
+        compiler_params=pltpu.CompilerParams(vmem_limit_bytes=16 * 1024 * 1024),
+        cost_estimate=pl.CostEstimate(
+            flops=0, bytes_accessed=6 * total * features, transcendentals=0
+        ),
+    )(parts)
 
 
 def attend_column(
@@ -1980,10 +2014,13 @@
     gain_ref,
     down_own,
     up_term_ref,
-    kv_ref,
+    full3_ref,
+    history_ref,
+    key_before_ref,
     full_ref,
     down_all_ref,
     up_all_ref,
+    inner_ref,
     quarter_ref,
     branch_ref,
     gain_grad_ref,
@@ -2011,6 +2048,7 @@
     back_buf,
     x_buf,
     stage,
+    inner_columns,
     scatter_send,
     scatter_recv,
     sum_send,
@@ -2024,6 +2062,9 @@
     swap_send,
     swap_recv,
     local_sem,
+    inner_sem,
+    share_send,
+    share_recv,
     *,
     micro_count,
     sequence_length,
@@ -2034,7 +2075,9 @@
     rows, features = total // 8, w_down_ref.shape[1]
     ff_share = w_down_ref.shape[0]
     quarter = features // 8 // 4
-    k_grad, v_grad, attn_sum = q_grad, att, up_sum
+    v_grad = kv_before.at[:, pl.ds(0, width)]
+    k_grad = kv_before.at[:, pl.ds(width, width)]
+    attn_sum = up_sum
     tile = 512
 
     barrier = pltpu.get_barrier_semaphore()
@@ -2046,12 +2089,29 @@
 
         @pl.when(plane == place)
         def _():
-            nearby = [p for p in (place - 1, place + 1) if 0 <= p < 4]
-            for p in nearby:
-                pl.semaphore_signal(
-                    barrier, inc=1, device_id=z_place(p), device_id_type=DEVICE_MESH
-                )
-            pl.semaphore_wait(barrier, 7 + len(nearby))
+            for p in range(4):
+                if p != place:
+                    pl.semaphore_signal(
+                        barrier, inc=1, device_id=z_place(p), device_id_type=DEVICE_MESH
+                    )
+
+    pl.semaphore_wait(barrier, 10)
+
+    def value_copy(place):
+        return pltpu.make_async_remote_copy(
+            src_ref=v_ref,
+            dst_ref=kv_before.at[:, pl.ds(width, width)],
+            send_sem=key_send.at[1],
+            recv_sem=key_recv.at[1],
+            device_id=z_place(place + 1),
+            device_id_type=DEVICE_MESH,
+        )
+
+    for place in range(3):
+
+        @pl.when(plane == place)
+        def _():
+            value_copy(place).start()
 
     def back_copy(place):
         return pltpu.make_async_remote_copy(
@@ -2085,6 +2145,8 @@
             sum_send.at[i],
             sum_recv.at[i],
             load_sem,
+            4 * quarter,
+            0,
         )
         for i, parts in enumerate((up_term_ref, attn_parts_ref))
     ]
@@ -2175,6 +2237,55 @@
             return carry
 
         lax.fori_loop(first, first + count, one_column, 0)
+
+    step_rows = rows // 2
+
+    def inner_loads(item, i):
+        source = full3_ref if item == 0 else full_ref
+        first = 0 if item == 0 else (item - 1) * 4 * rows
+        base = (i % 2) * 5 * step_rows
+        copies = [
+            pltpu.make_async_copy(
+                source.at[pl.ds(first + i * step_rows, step_rows)],
+                big.at[pl.ds(base + 4 * step_rows, step_rows)],
+                inner_sem.at[(i % 2) * 5 + 4],
+            )
+        ] + [
+            pltpu.make_async_copy(
+                history_ref.at[pl.ds(slot * 4 * rows + i * step_rows, step_rows)],
+                big.at[pl.ds(base + slot * step_rows, step_rows)],
+                inner_sem.at[(i % 2) * 5 + slot],
+            )
+            for slot in range(4)
+        ]
+        for copy in copies:
+            copy.start()
+        return copies
+
+    def inner_products(item):
+        loads = [inner_loads(item, 0)]
+        for i in range(8):
+            if i + 1 < 8:
+                loads.append(inner_loads(item, i + 1))
+            for copy in loads[i]:
+                copy.wait()
+            base = (i % 2) * 5 * step_rows
+
+            def some_rows(r, carry):
+                grad = big[
+                    pl.ds(pl.multiple_of(base + 4 * step_rows + r * 16, 16), 16), :
+                ].astype(jnp.float32)
+                for slot in range(4):
+                    values = big[
+                        pl.ds(pl.multiple_of(base + slot * step_rows + r * 16, 16), 16), :
+                    ].astype(jnp.float32)
+                    one = item * 4 + slot
+                    inner_columns[
+                        pl.ds(pl.multiple_of(i * step_rows + r * 16, 16), 16), one : one + 1
+                    ] = jnp.sum(grad * values, axis=-1, keepdims=True)
+                return carry
+
+            lax.fori_loop(0, step_rows // 16, some_rows, 0)
 
     def part_copies(first_row):
         return [
@@ -2274,7 +2385,6 @@
     up_line.start()
     down_spread = spread(4, down_own, lambda p: down_all_ref.at[pl.ds(p * 4 * quarter, 4 * quarter)])
     down_spread.service(0)
-    kv_load = pltpu.make_async_copy(kv_ref, kv_before, local_sem.at[0])
 
     @pl.when(plane == 0)
     def _():
@@ -2283,67 +2393,16 @@
 
     @pl.when(plane > 0)
     def _():
-        kv_load.start()
-        kv_load.wait()
+        load = pltpu.make_async_copy(
+            key_before_ref, kv_before.at[:, pl.ds(0, width)], local_sem.at[0]
+        )
+        load.start()
+        load.wait()
 
     @pl.when(plane == 3)
     def _():
         clear(kv_after)
         clear(line_ends.at[1])
-
-    attend(0, 8)
-    for place in range(1, 4):
-
-        @pl.when(plane == place)
-        def _():
-            back_copy(place).start()
-
-    loading = load_big(normed_ref.at[0])
-    query_scatter = scatter_of(projection_product(0, q_grad), 0)
-    query_scatter.block(0)
-    query_scatter.block(1)
-    up_line.service(0)
-    query_scatter.block(2)
-    query_scatter.block(3)
-    down_spread.service(1)
-    query_scatter.turn()
-    loading.wait()
-    parts_out = attn_term(0, q_grad)
-    query_scatter.finish(back_buf)
-    up_line.service(1)
-    norm_back(1, back_buf)
-    query_spread = stream_spread(1)
-    query_spread.service(0)
-    down_spread.service(2)
-    for copy in parts_out:
-        copy.wait()
-    loading = load_big(grad_all_ref)
-    branch_scatter = scatter_of(branch_product, 1)
-    branch_scatter.block(0)
-    branch_scatter.block(1)
-    up_line.service(2)
-    up_line.finish(up_sum)
-    up_swap = swap(0)
-    branch_scatter.block(2)
-    down_spread.service(3)
-    branch_scatter.block(3)
-    query_spread.service(1)
-    branch_scatter.turn()
-    loading.wait()
-    parts_out = out_term()
-    branch_scatter.finish(branch_ref)
-    swapped_in(up_swap)
-    up_spread = spread(5, up_own, lambda p: up_all_ref.at[pl.ds(p * quarter, quarter)])
-    up_spread.service(0)
-    for copy in parts_out:
-        copy.wait()
-    loading = load_big(normed_ref.at[1])
-
-    for place in range(3):
-
-        @pl.when(plane == place)
-        def _():
-            back_copy(place + 1).wait_recv()
 
     def key_value(m, carry):
         here = pl.ds(pl.multiple_of(m * rows, 16), rows)
@@ -2362,55 +2421,148 @@
             ).astype(jnp.bfloat16)
         return carry
 
+    for place in range(1, 4):
+
+        @pl.when(plane == place)
+        def _():
+            value_copy(place - 1).wait_recv()
+
+    attend(0, 8)
+    for place in range(1, 4):
+
+        @pl.when(plane == place)
+        def _():
+            back_copy(place).start()
+
+    loading = load_big(grad_all_ref)
+    query_scatter = scatter_of(projection_product(0, q_grad), 0)
+    query_scatter.block(0)
+    query_scatter.block(1)
+    query_scatter.block(2)
+    query_scatter.block(3)
+    up_line.service(0)
+    query_scatter.turn()
+    loading.wait()
+    parts_out = out_term()
+    query_scatter.finish(back_buf)
+    norm_back(1, back_buf)
+    query_spread = stream_spread(1)
+    query_spread.service(0)
+    down_spread.service(1)
+    up_line.service(1)
+    for copy in parts_out:
+        copy.wait()
+    loading = load_big(normed_ref.at[0])
+
+    for place in range(3):
+
+        @pl.when(plane == place)
+        def _():
+            back_copy(place + 1).wait_recv()
+
     lax.fori_loop(0, 8, key_value, 0)
-    query_spread.service(2)
-    key_scatter = scatter_of(projection_product(1, k_grad), 2)
+    key_scatter = scatter_of(projection_product(1, k_grad), 1)
     key_scatter.block(0)
     key_scatter.block(1)
     key_scatter.block(2)
     key_scatter.block(3)
-    up_spread.service(1)
-    query_spread.service(3)
+    down_spread.service(2)
+    loading.wait()
+    parts_out = attn_term(0, q_grad)
     key_scatter.turn()
-    loading.wait()
-    parts_out = attn_term(1, k_grad)
     key_scatter.finish(back_buf)
     norm_back(2, back_buf)
     key_spread = stream_spread(2)
     key_spread.service(0)
+    up_line.service(2)
+    up_line.finish(up_sum)
+    up_swap = swap(0)
+    for copy in parts_out:
+        copy.wait()
+    loading = load_big(normed_ref.at[1])
+    value_scatter = scatter_of(projection_product(2, v_grad), 2)
+    value_scatter.block(0)
+    value_scatter.block(1)
+    value_scatter.block(2)
+    value_scatter.block(3)
+    down_spread.service(3)
+    query_spread.service(1)
+    loading.wait()
+    parts_out = attn_term(1, k_grad)
+    value_scatter.turn()
+    swapped_in(up_swap)
+    up_spread = spread(5, up_own, lambda p: up_all_ref.at[pl.ds(p * quarter, quarter)])
+    up_spread.service(0)
+    value_scatter.finish(back_buf)
+    norm_back(3, back_buf)
+    value_spread = stream_spread(3)
     for copy in parts_out:
         copy.wait()
     loading = load_big(normed_ref.at[2])
-    up_spread.service(2)
-    value_scatter = scatter_of(projection_product(2, v_grad), 3)
-    value_scatter.block(0)
-    value_scatter.block(1)
     loading.wait()
     parts_out = attn_term(2, v_grad)
     for copy in parts_out:
         copy.wait()
     attn_line.start()
+    value_spread.service(0)
+    query_spread.service(2)
+    branch_scatter = scatter_of(branch_product, 3)
+    branch_scatter.block(0)
+    branch_scatter.block(1)
     key_spread.service(1)
-    value_scatter.block(2)
-    value_scatter.block(3)
-    up_spread.service(3)
+    branch_scatter.block(2)
+    branch_scatter.block(3)
+    up_spread.service(1)
+    query_spread.service(3)
+    branch_scatter.turn()
+    branch_scatter.finish(branch_ref)
     attn_line.service(0)
-    value_scatter.turn()
     key_spread.service(2)
-    value_scatter.finish(back_buf)
-    norm_back(3, back_buf)
-    value_spread = stream_spread(3)
-    value_spread.service(0)
+    up_spread.service(2)
+    value_spread.service(1)
     attn_line.service(1)
     key_spread.service(3)
-    value_spread.service(1)
+    query_spread.placed()
+    inner_products(0)
+    inner_products(1)
+    up_spread.service(3)
     attn_line.service(2)
     attn_line.finish(attn_sum)
     attn_swap = swap(1)
     quarter_ref[pl.ds(3 * quarter, quarter), :] = attn_sum[pl.ds(3 * quarter, quarter), :]
     value_spread.service(2)
+    key_spread.placed()
+    inner_products(2)
+    down_spread.placed()
+    up_spread.placed()
     swapped_in(attn_swap)
     value_spread.service(3)
+    value_spread.placed()
+    inner_products(3)
+
+    def share_copy(source_place, target_place):
+        return pltpu.make_async_remote_copy(
+            src_ref=inner_ref.at[source_place],
+            dst_ref=inner_ref.at[source_place],
+            send_sem=share_send.at[target_place],
+            recv_sem=share_recv.at[source_place],
+            device_id=z_place(target_place),
+            device_id_type=DEVICE_MESH,
+        )
+
+    for place in range(4):
+
+        @pl.when(plane == place)
+        def _():
+            others = [p for p in range(4) if p != place]
+            inner_ref[place] = jnp.transpose(inner_columns[...])[:16]
+            for p in others:
+                share_copy(place, p).start()
+            for p in others:
+                share_copy(p, place).wait_recv()
+            for p in others:
+                share_copy(place, p).wait_send()
+
     for spreading in (
         down_spread,
         query_spread,
@@ -2419,6 +2571,12 @@
         value_spread,
     ):
         spreading.finish()
+    for place in range(3):
+
+        @pl.when(plane == place)
+        def _():
+            value_copy(place).wait_send()
+
     for place in range(1, 4):
 
         @pl.when(plane == place)
@@ -2444,7 +2602,9 @@
     gains,
     down_own,
     up_term,
-    kv_before,
+    full3,
+    history,
+    key_before,
     micro_count,
     sequence_length,
 ):
@@ -2471,12 +2631,13 @@
         + [near] * 4
         + [anywhere]
         + [near] * 2
-        + [anywhere, anywhere],
-        out_specs=[anywhere, anywhere, anywhere, near, near, near, anywhere, anywhere],
+        + [anywhere] * 4,
+        out_specs=[anywhere] * 3 + [near, near, near, near, anywhere, anywhere],
         out_shape=[
             shape((12 * rows, features), low_type),
             shape((ff_share, features), low_type),
             shape((4 * quarter, 8 * ff_share), low_type),
+            shape((4, 16, 4 * rows), jnp.float32),
             shape(piece, low_type),
             shape(block, low_type),
             shape((8, features), jnp.float32),
@@ -2506,6 +2667,7 @@
             some(*block),
             pltpu.VMEM(block, jnp.float32),
             some(*piece),
+            pltpu.VMEM((4 * rows, 128), jnp.float32),
             dma((4, 10)),
             dma((4, 10)),
             dma((3, 6)),
@@ -2519,6 +2681,9 @@
             dma((16,)),
             dma((16,)),
             dma((8,)),
+            dma((10,)),
+            dma((4,)),
+            dma((4,)),
         ],
         compiler_params=pltpu.CompilerParams(
             collective_id=6, has_side_effects=True, vmem_limit_bytes=63 * 1024 * 1024
@@ -2546,7 +2711,9 @@
         gains,
         down_own,
         up_term,
-        kv_before,
+        full3,
+        history,
+        key_before,
     )
 
 
@@ -2659,7 +2826,7 @@
         k,
         v,
         out_grad,
-        kv_before,
+        key_before,
         _,
         _,
         _,
@@ -2681,7 +2848,17 @@
         sequence_length,
     )
     lengths_all = packed[:, share + 8, :micro_count].reshape(-1).astype(jnp.int32)
-    full, down_all, up_all, attn_quarter, branch, gain_sums, _, _ = attend_and_back(
+    (
+        full,
+        down_all,
+        up_all,
+        inner_all,
+        attn_quarter,
+        branch,
+        gain_sums,
+        _,
+        _,
+    ) = attend_and_back(
         lengths_all,
         cosine,
         sine_part,
@@ -2699,11 +2876,13 @@
         gains,
         down_own,
         up_term,
-        kv_before,
+        full3,
+        history.reshape(local_slots * all_rows, features),
+        key_before,
         micro_count,
         sequence_length,
     )
-    attn_every = lax.all_gather(attn_quarter, "hist", axis=0, tiled=False)
+    attn_every = lax.all_gather(attn_quarter, "hist", axis=0, tiled=True)
 
     chunk = sequence_length // planes
     inverse_step = pow(micro_count, -1, planes)
@@ -2716,20 +2895,6 @@
         which = lax.div(source * micro_count + i, planes)
         block_out = lax.dynamic_update_index_in_dim(block_out, piece, which, 0)
 
-    flat_history = history.reshape(local_slots, all_rows, features)
-    full_rest = full.reshape(3, all_rows, features)
-    item_grads = [full3.astype(jnp.float32)] + [
-        full_rest[i].astype(jnp.float32) for i in range(3)
-    ]
-    inner = jnp.stack(
-        [
-            jnp.sum(item_grads[item] * flat_history[slot].astype(jnp.float32), axis=-1)
-            for item in range(STREAM_COUNT)
-            for slot in range(local_slots)
-        ],
-        axis=0,
-    )
-    inner_all = line_share(inner)
     mixer_output_wide = (
         packed[:, share : share + mix_rows, :mix_width]
         .reshape(mix_width, mix_width)
@@ -2752,15 +2917,12 @@
     act_grad = precise(dyn_grad, mixer_output_wide.T)
     mix_out_grad = precise(mix_act.T, dyn_grad) * on_root
     latest_grad, gain_zero, mix_in_grad = mix_backward(kept_mix, act_grad, gains[0], mix_in_all)
-    slot_grads = []
-    for slot in range(local_slots):
-        is_latest = (plane * local_slots + slot == newest_output).astype(jnp.float32)
-        slot_grad = latest_grad * is_latest
-        for item in range(STREAM_COUNT):
-            one = item * local_slots + slot
-            slot_grad = slot_grad + factors[:, one : one + 1] * item_grads[item]
-        slot_grads.append(low(slot_grad))
-    history_grad = jnp.stack(slot_grads).reshape(history.shape)
+    latest_here = (plane * local_slots + jnp.arange(local_slots) == newest_output).astype(
+        jnp.float32
+    )
+    history_grad = slot_grads_of(
+        latest_here, factors, full3, full.reshape(3, all_rows, features), latest_grad
+    ).reshape(history.shape)
 
     small_top = jnp.concatenate(
         [
@@ -2778,15 +2940,7 @@
     )
     small = small_sums(low(jnp.concatenate([small_top, small_bottom], axis=1)))
 
-    part = share // planes
-    w_attn_grad = (
-        attn_every[:, : 3 * part]
-        .astype(jnp.float32)
-        .reshape(planes, 3, part, features)
-        .transpose(1, 0, 2, 3)
-        .reshape(3, share, features)
-    )
-    w_out_grad = attn_every[:, 3 * part :].astype(jnp.float32).reshape(share, features)
+    w_attn_grad, w_out_grad = lay_out(attn_every)
     return (
         block_out,
         history_grad,

time: 998 us -> 940 us (0.942)
  other arithmetic: 69 us -> 31.3 us
  local copies, waits for them, and re-layouts: 42.6 us -> 28.6 us
    pallas_call x1, Pallas kernels: 392 us -> 366 us  [forward_and_feed(): pl.pallas_call(functools.partial(forward_kernel, micro_count=micro_count,...]
    convert_element_type x5 -> x1, other arithmetic: 25.9 us -> 2 us  [shards_split(): low = lambda values: values.astype(jnp.bfloat16)]
    slice x4 -> x0, local copies, waits for them, and re-layouts: 15.7 us -> none  [the longest x1 8.61 us: shards_split(): flat_history[slot].astype(jnp.float32)]
    reduce_sum x1 -> x0, other arithmetic: 13.5 us -> none  [shards_split(): jnp.sum(item_grads[item] * flat_history[slot].astype(jnp.float32), axis=-1)]
    pallas_call x1, Pallas kernels: 406 us -> 419 us  [attend_and_back(): pl.pallas_call(functools.partial(backward_kernel, micro_count=micro_count...]
    pallas_call x1 -> x2, Pallas kernels: 12.2 us -> 20.1 us  [the longest x1 16.6 us: slot_grads_of(): pl.pallas_call(slot_grad_kernel, grid=(total // step,), in_specs=[pl.Bloc...]
  transfers between devices with their start and end apart: 4 -> 4, of which waited for: 0 -> 0; matrix products, arithmetic and copies ran while one was open for 10% -> 5% of each run, Pallas kernels for 4% -> 4%
where the time goes in v4:
time: 940 us; the launch traced here: 927 us
  Pallas kernels  827 us (88%)
  other arithmetic  31.3 us (3%)
  local copies, waits for them, and re-layouts  28.6 us (3%)
  between operations  17.2 us (2%)
  matrix products  14.5 us (2%)
    pallas_call x1, Pallas kernels, attend_and_back(): pl.pallas_call(functools.partial(backward_kernel, micro_count=micro_count...  419 us
    pallas_call x1, Pallas kernels, forward_and_feed(): pl.pallas_call(functools.partial(forward_kernel, micro_count=micro_count,...  366 us
    pallas_call x1, Pallas kernels, small_sums(): pl.pallas_call(small_sum_kernel, out_shape=jax.ShapeDtypeStruct(dims, jnp...  22.8 us
  transfers between devices with their start and end apart: 4, of which 0 were waited for; matrix products, arithmetic and copies ran while one was open for 5% of the time, Pallas kernels for 4%

profile of v4, /device:TPU:0, one launch (start us, length us, event | category | flops | bytes accessed | tf_op | source)
XLA Modules:
  0.0 927.1 jit_solution(15205029929159541163)
XLA Ops:
  7.2 1.3 fusion.138
  15.2 0.9 copy.33
  17.4 4.2 multiply_reduce_fusion
  24.2 365.6 %shard_map.187 = (bf16[8,288,128]{2,1,0:T(8,128)(2,1)}, f32[8,2048]{1,0:T(8,128)}, f32[768,128]{1,0:T(8,128)}, f32[768,128]{1,0:T(8,128)}, f32[4,192,2048]{2,1,0...) custom-call(s32[3]{0:T(128)} %length_ref.1, ...), custom_call_target="tpu_custom_call" | custom-call | flops 38654705664 | bytes 600000000 | tf_op jit(solution)/shard_map/pallas_call | solution.py:1687
  391.1 418.9 %shard_map.188 = (bf16[2304,2048]{1,0:T(8,128)(2,1)}, bf16[1024,2048]{1,0:T(8,128)(2,1)}, bf16[256,8192]{1,0:T(8,128)(2,1)}, f32[4,16,768]{2,1,0:T(8,128)}, bf16...) custom-call(s32[24]{0:T(128)} %reshape.157.length_ref, ...), custom_call_target="tpu_custom_call" | custom-call | flops 16106127360 | bytes 1000000000 | tf_op jit(solution)/shard_map/pallas_call | solution.py:2624
  810.2 2.0 fusion.18
  812.2 0.9 fusion.170
  813.1 3.6 collective-permute-start
  816.7 1.2 collective-permute-start.1
  817.9 3.2 collective-permute-start.2
  822.0 1.9 slice.55
  824.0 1.0 fusion.88
  825.4 1.5 convolution_multiply_fusion
  826.9 6.8 fusion.6
  835.6 2.2 fusion.14
  837.8 0.9 maximum_maximum_fusion
  838.7 2.0 copy.39
  840.7 2.6 fusion.21
  844.2 22.8 %shard_map.190 = f32[272,128]{1,0:T(8,128)} custom-call(bf16[8,272,128]{2,1,0:T(8,128)(2,1)} %fusion.22.parts_ref), custom_call_target="tpu_custom_call" | custom-call | bytes 40000000 | tf_op jit(solution)/shard_map/pallas_call | solution.py:1837
  867.0 0.9 slice.60
  867.9 1.3 slice.61
  869.9 5.4 fusion.1.latest_grad_ref
  876.0 6.7 convert_element_type.81
  882.8 4.4 convert_element_type.82
  887.9 2.8 copy-done
  890.7 3.7 copy-done.2
  894.4 16.6 %shard_map.189 = bf16[4,768,2048]{2,1,0:T(8,128)(2,1)} custom-call(f32[4]{0:T(128)S(1)} %compare_convert_fusion.latest_ref, f32[768,128]{1,0:T(8,128)S(1)} %copy-done.4, bf16[768,2048]{1,0:T(8,128)(2,1)S(1)} %copy-done.1, bf16[3,768,2048]{2,1,0:T(8,128)(2,1)S(1)} %bitcast.63, f32[768,2048]{1,0:T(8,128)S(1)} %copy-done), custom_call_target="tpu_custom_call" | custom-call | flops 62914560 | bytes 31457280 | tf_op jit(solution)/shard_map/pallas_call | solution.py:1879
  911.1 1.0 bitcast_dynamic-update-slice_fusion.2
  912.1 1.0 bitcast_dynamic-update-slice_fusion.1
  913.0 1.0 bitcast_dynamic-update-slice_fusion
  914.1 2.4 copy-done.3
  916.5 3.5 shard_map.191
  (77 shorter events, 15.8 us)
Async XLA Ops:
  7.2 15.8 %copy-start.12 = (bf16[8,64]{1,0:T(8,128)(2,1)S(1)}, bf16[8,64]{1,0:T(8,128)(2,1)}, u32[]{:S(2)}) copy-start(bf16[8,64]{1,0:T(8,128)(2,1)} %param.17) | copy-start | bytes 3076
  7.2 906.9 %all-gather.2.cloned.1.call-start = ((), (), s32[]{:S(2)}) async-start(), calls=%async_computation | async-start | bytes 5242880 | tf_op jit(solution)/shard_map/all_gather | solution.py:2885
  13.2 0.5 copy-start.11
  391.1 419.0 %copy-start.13 = (s32[3]{0:T(128)S(1)}, s32[3]{0:T(128)}, u32[]{:S(2)}) copy-start(s32[3]{0:T(128)} %length_ref.1) | copy-start | bytes 40
  391.1 430.0 %copy-start.14 = (s32[16]{0:T(128)S(1)}, s32[16]{0:T(128)}, u32[]{:S(2)}) copy-start(s32[16]{0:T(128)} %param.13) | copy-start | bytes 196
  810.0 13.9 %copy-start.10 = (f32[4,16,768]{2,1,0:T(8,128)S(1)}, f32[4,16,768]{2,1,0:T(8,128)}, u32[]{:S(2)}) copy-start(f32[4,16,768]{2,1,0:T(8,128)} %get-tuple-element.54) | copy-start | bytes 589828
  810.0 16.9 %copy-start.5 = (bf16[1,3,256,2048]{3,2,1,0:T(8,128)(2,1)S(1)}, bf16[1,3,256,2048]{3,2,1,0:T(8,128)(2,1)}, u32[]{:S(2)}) copy-start(bf16[1,3,256,2048]{3,2,1,0:T(8,128)(2,1)} %get-tuple-element.93) | copy-start | bytes 9437188
  813.1 97.9 %collective-permute-start = (bf16[64,2048]{1,0:T(8,128)(2,1)}, bf16[64,2048]{1,0:T(8,128)(2,1)}, u32[]{:S(2)}, u32[]{:S(2)}) collective-permute-start(bf16[64,2048]{1,0:T(8,128)(2,1)} %get-tuple-element.96), channel_id=1, source_target_pairs={{0,0},{1,3},{2,2},{3,1},{4,4},{5,7},{6,6},{7,5},{8,8},{9,11},{10,1... | collective-permute-start | bytes 786440 | tf_op jit(solution)/shard_map/ppermute | solution.py:2893
  816.7 95.4 %collective-permute-start.1 = (bf16[64,2048]{1,0:T(8,128)(2,1)}, bf16[64,2048]{1,0:T(8,128)(2,1)}, u32[]{:S(2)}, u32[]{:S(2)}) collective-permute-start(bf16[64,2048]{1,0:T(8,128)(2,1)} %get-tuple-element.95), channel_id=1, source_target_pairs={{0,1},{1,0},{2,3},{3,2},{4,5},{5,4},{6,7},{7,6},{8,9},{9,8},{10,11... | collective-permute-start | bytes 786440 | tf_op jit(solution)/shard_map/ppermute | solution.py:2893
  817.9 95.1 %collective-permute-start.2 = (bf16[64,2048]{1,0:T(8,128)(2,1)}, bf16[64,2048]{1,0:T(8,128)(2,1)}, u32[]{:S(2)}, u32[]{:S(2)}) collective-permute-start(bf16[64,2048]{1,0:T(8,128)(2,1)} %get-tuple-element.94), channel_id=1, source_target_pairs={{0,2},{1,1},{2,0},{3,3},{4,6},{5,5},{6,4},{7,7},{8,10},{9,9},{10,8... | collective-permute-start | bytes 786440 | tf_op jit(solution)/shard_map/ppermute | solution.py:2893
  840.7 2.6 copy-start.7
  869.9 5.4 copy-start.8
  876.0 6.7 copy-start.6
  882.8 5.1 copy-start.1
  882.8 5.1 copy-start.4
  887.9 2.8 copy-start
  890.7 3.7 copy-start.2
  914.0 6.0 copy-start.9
  914.1 2.5 copy-start.3
Sparse Core Ops, SparseCore 0:
  810.2 92.6 all-gather.1

commit v5 on v4

--- a/solution.py
+++ b/solution.py
@@ -1855,27 +1855,50 @@
 
 
 def slot_grad_kernel(
-    latest_ref, factor_ref, first_ref, rest_ref, latest_grad_ref, out_ref
+    flag_ref,
+    factor_ref,
+    first_ref,
+    rest_ref,
+    latest_ref,
+    pre_grad_ref,
+    mix_in_ref,
+    gain_ref,
+    out_ref,
+    gain_grad_ref,
 ):
+    x = latest_ref[...].astype(jnp.float32)
+    inverse = lax.rsqrt(jnp.mean(x * x, axis=-1, keepdims=True) + epsilon)
+    grad = precise(pre_grad_ref[...], mix_in_ref[...])
+    scaled = grad * gain_ref[pl.ds(0, 1), :]
+    mean = jnp.mean(scaled * x, axis=-1, keepdims=True)
+    latest_grad = inverse * scaled - x * (inverse * inverse * inverse) * mean
+    gain_sum = jnp.sum(grad * x * inverse, axis=0, keepdims=True)
+
+    @pl.when(pl.program_id(0) == 0)
+    def _():
+        gain_grad_ref[...] = jnp.zeros_like(gain_grad_ref)
+
+    gain_grad_ref[pl.ds(0, 1), :] += gain_sum
     grads = [first_ref[...].astype(jnp.float32)] + [
         rest_ref[i].astype(jnp.float32) for i in range(3)
     ]
-    latest_grad = latest_grad_ref[...]
     factors = factor_ref[...]
     for slot in range(4):
-        total = latest_grad * latest_ref[slot]
+        total = latest_grad * flag_ref[slot]
         for item in range(4):
             one = item * 4 + slot
             total = total + factors[:, one : one + 1] * grads[item]
         out_ref[slot] = total.astype(jnp.bfloat16)
 
 
-def slot_grads_of(latest_here, factors, first, rest, latest_grad):
+def slot_grads_of(latest_here, factors, first, rest, latest, pre_grad, mix_in_columns, gains):
     total, features = first.shape
-    step = 32
+    step = 64
+    mix_width = pre_grad.shape[1]
     rows_of = lambda *lead: pl.BlockSpec(
         lead + (step, features), lambda r: (0,) * len(lead) + (r, 0)
     )
+    whole = lambda *dims: pl.BlockSpec(dims, lambda r: (0, 0))
     return pl.pallas_call(
         slot_grad_kernel,
         grid=(total // step,),
@@ -1885,14 +1908,20 @@
             rows_of(),
             rows_of(3),
             rows_of(),
+            pl.BlockSpec((step, mix_width), lambda r: (r, 0)),
+            whole(mix_width, features),
+            whole(8, features),
         ],
-        out_specs=rows_of(4),
-        out_shape=jax.ShapeDtypeStruct((4, total, features), jnp.bfloat16),
-        compiler_params=pltpu.CompilerParams(vmem_limit_bytes=24 * 1024 * 1024),
+        out_specs=[rows_of(4), whole(8, features)],
+        out_shape=[
+            jax.ShapeDtypeStruct((4, total, features), jnp.bfloat16),
+            jax.ShapeDtypeStruct((8, features), jnp.float32),
+        ],
+        compiler_params=pltpu.CompilerParams(vmem_limit_bytes=56 * 1024 * 1024),
         cost_estimate=pl.CostEstimate(
             flops=40 * total * features, bytes_accessed=20 * total * features, transcendentals=0
         ),
-    )(latest_here, factors, first, rest, latest_grad)
+    )(latest_here, factors, first, rest, latest, pre_grad, mix_in_columns, gains)
 
 
 def lay_out_kernel(part_ref, attn_ref, out_ref):
@@ -1920,7 +1949,7 @@
             jax.ShapeDtypeStruct((3, step, features), jnp.float32),
             jax.ShapeDtypeStruct((step, features), jnp.float32),
         ],
-        compiler_params=pltpu.CompilerParams(vmem_limit_bytes=16 * 1024 * 1024),
+        compiler_params=pltpu.CompilerParams(vmem_limit_bytes=56 * 1024 * 1024),
         cost_estimate=pl.CostEstimate(
             flops=0, bytes_accessed=6 * total * features, transcendentals=0
         ),
@@ -2911,24 +2940,31 @@
     ).reshape(all_rows, STREAM_COUNT * slot_count)
     mixer_preactivation = pre[:, :mix_width]
     mix_act = jax.nn.gelu(mixer_preactivation, approximate=False)
-    latest_values = latest_rows.astype(jnp.float32)
-    latest_scaled, latest_inverse = rms_scale(latest_values, gains[0])
-    kept_mix = (latest_values, latest_inverse, low(latest_scaled), mixer_preactivation, mix_act)
     act_grad = precise(dyn_grad, mixer_output_wide.T)
     mix_out_grad = precise(mix_act.T, dyn_grad) * on_root
-    latest_grad, gain_zero, mix_in_grad = mix_backward(kept_mix, act_grad, gains[0], mix_in_all)
+    pre_grad = act_grad * gelu_slope(mixer_preactivation)
+    latest_scaled, _ = rms_scale(latest_rows.astype(jnp.float32), gains[0])
+    mix_in_grad = precise(low(latest_scaled).astype(jnp.float32).T, pre_grad)
     latest_here = (plane * local_slots + jnp.arange(local_slots) == newest_output).astype(
         jnp.float32
     )
-    history_grad = slot_grads_of(
-        latest_here, factors, full3, full.reshape(3, all_rows, features), latest_grad
-    ).reshape(history.shape)
+    history_grad, gain_zero = slot_grads_of(
+        latest_here,
+        factors,
+        full3,
+        full.reshape(3, all_rows, features),
+        latest_rows,
+        pre_grad,
+        mix_in_all.astype(jnp.float32).T,
+        gains,
+    )
+    history_grad = history_grad.reshape(history.shape)
 
     small_top = jnp.concatenate(
         [
             mix_in_grad * on_root,
             jnp.stack(
-                [gain_zero * on_root, gain_sums[1], gain_sums[2], gain_sums[3], gain_sum3[0]]
+                [gain_zero[0] * on_root, gain_sums[1], gain_sums[2], gain_sums[3], gain_sum3[0]]
             ).T,
             jnp.zeros((features, 128 - mix_width - 5), jnp.float32),
         ],

time: 940 us -> 925 us (0.984)
  local copies, waits for them, and re-layouts: 28.6 us -> 14.7 us
    unnamed x33 -> x23, local copies, waits for them, and re-layouts: 11.7 us -> 2.31 us
  transfers between devices with their start and end apart: 4 -> 4, of which waited for: 0 -> 1; matrix products, arithmetic and copies ran while one was open for 5% -> 4% of each run, Pallas kernels for 4% -> 5%
where the time goes in v5:
time: 925 us; the launch traced here: 915 us
  Pallas kernels  833 us (90%)
  other arithmetic  26.7 us (3%)
  between operations  17.2 us (2%)
  local copies, waits for them, and re-layouts  14.7 us (2%)
    pallas_call x1, Pallas kernels, attend_and_back(): pl.pallas_call(functools.partial(backward_kernel, micro_count=micro_count...  419 us
    pallas_call x1, Pallas kernels, forward_and_feed(): pl.pallas_call(functools.partial(forward_kernel, micro_count=micro_count,...  366 us
    pallas_call x1, Pallas kernels, slot_grads_of(): pl.pallas_call(slot_grad_kernel, grid=(total // step,), in_specs=[pl.Bloc...  22.2 us
    pallas_call x1, Pallas kernels, small_sums(): pl.pallas_call(small_sum_kernel, out_shape=jax.ShapeDtypeStruct(dims, jnp...  20.6 us
  transfers between devices with their start and end apart: 4, of which 1 were waited for; matrix products, arithmetic and copies ran while one was open for 4% of the time, Pallas kernels for 5%

profile of v5, /device:TPU:0, one launch (start us, length us, event | category | flops | bytes accessed | tf_op | source)
XLA Modules:
  0.0 915.2 jit_solution(7857559446075227971)
XLA Ops:
  7.2 1.3 fusion.126
  13.9 0.7 pad_maximum_fusion.cos_ref
  14.7 0.9 copy.45
  16.9 4.2 multiply_reduce_fusion
  21.7 0.7 pad_maximum_fusion.1.sin_ref
  23.7 365.7 %shard_map.187 = (bf16[8,288,128]{2,1,0:T(8,128)(2,1)}, f32[8,2048]{1,0:T(8,128)}, f32[768,128]{1,0:T(8,128)}, f32[768,128]{1,0:T(8,128)}, f32[4,192,2048]{2,1,0...) custom-call(s32[3]{0:T(128)} %length_ref.1, ...), custom_call_target="tpu_custom_call" | custom-call | flops 38654705664 | bytes 600000000 | tf_op jit(solution)/shard_map/pallas_call | solution.py:1687
  389.4 0.7 convert_reduce_fusion
  390.7 418.9 %shard_map.188 = (bf16[2304,2048]{1,0:T(8,128)(2,1)}, bf16[1024,2048]{1,0:T(8,128)(2,1)}, bf16[256,8192]{1,0:T(8,128)(2,1)}, f32[4,16,768]{2,1,0:T(8,128)}, bf16...) custom-call(s32[24]{0:T(128)} %reshape.134.length_ref, ...), custom_call_target="tpu_custom_call" | custom-call | flops 16106127360 | bytes 1000000000 | tf_op jit(solution)/shard_map/pallas_call | solution.py:2653
  809.8 1.9 fusion.6
  811.7 0.9 fusion.158
  812.6 1.6 collective-permute-start
  814.2 3.2 collective-permute-start.1
  817.4 3.1 collective-permute-start.2
  820.6 0.8 slice.58
  821.7 1.1 copy.59
  822.8 0.8 slice.87
  823.7 0.8 slice.88
  824.6 1.2 compare_convert_fusion.flag_ref
  826.5 2.2 convolution_multiply_fusion.pre_grad_ref
  828.8 22.2 %shard_map.189 = (bf16[4,768,2048]{2,1,0:T(8,128)(2,1)}, f32[8,2048]{1,0:T(8,128)}) custom-call(f32[4]{0:T(128)} %compare_convert_fusion.flag_ref, f32[768,128]{1,0:T(8,128)} %get-tuple-element.54.factor_ref, bf16[768,2048]{1,0:T(8,128)(2,1)} %get-tuple-element.51.full3_ref.first_ref, bf16[3,768,2048]{2,1,0:T(8,128)(2,1)} %bitcast.66, ...), custom_call_target="tpu_custom_call" | custom-call | flops 62914560 | bytes 31457280 | tf_op jit(solution)/shard_map/pallas_call | solution.py:1902
  851.0 0.9 multiply_convert_fusion.7
  852.0 2.2 fusion.4
  854.6 1.5 fusion.9
  856.1 0.8 fusion.10.parts_ref
  857.0 20.6 %shard_map.190 = f32[272,128]{1,0:T(8,128)} custom-call(bf16[8,272,128]{2,1,0:T(8,128)(2,1)} %fusion.10.parts_ref), custom_call_target="tpu_custom_call" | custom-call | bytes 40000000 | tf_op jit(solution)/shard_map/pallas_call | solution.py:1837
  877.6 0.9 slice.63
  878.5 1.3 slice.64
  880.5 1.0 slice_bitcast_fusion
  882.2 6.8 convert_element_type.85
  889.0 4.4 convert_element_type.86
  893.6 8.6 all-gather.2.cloned.1.call-done.part_ref
  902.3 5.9 shard_map.191
  (64 shorter events, 9.9 us)
Async XLA Ops:
  7.2 15.2 %copy-start.6 = (bf16[8,64]{1,0:T(8,128)(2,1)S(1)}, bf16[8,64]{1,0:T(8,128)(2,1)}, u32[]{:S(2)}) copy-start(bf16[8,64]{1,0:T(8,128)(2,1)} %param.17) | copy-start | bytes 3076
  7.2 895.1 %all-gather.2.cloned.1.call-start = ((), (), s32[]{:S(2)}) async-start(), calls=%async_computation | async-start | bytes 5242880 | tf_op jit(solution)/shard_map/all_gather | solution.py:2914
  390.7 419.0 %copy-start.7 = (s32[3]{0:T(128)S(1)}, s32[3]{0:T(128)}, u32[]{:S(2)}) copy-start(s32[3]{0:T(128)} %length_ref.1) | copy-start | bytes 40
  809.6 10.9 %copy-start.8 = (s32[16]{0:T(128)S(1)}, s32[16]{0:T(128)}, u32[]{:S(2)}) copy-start(s32[16]{0:T(128)} %param.13) | copy-start | bytes 196
  809.6 11.9 %copy-start.3 = (bf16[8,288,128]{2,1,0:T(8,128)(2,1)S(1)}, bf16[8,288,128]{2,1,0:T(8,128)(2,1)}, u32[]{:S(2)}) copy-start(bf16[8,288,128]{2,1,0:T(8,128)(2,1)} %get-tuple-element.39) | copy-start | bytes 1769476
  809.6 11.9 %copy-start.5 = (f32[4,16,768]{2,1,0:T(8,128)S(1)}, f32[4,16,768]{2,1,0:T(8,128)}, u32[]{:S(2)}) copy-start(f32[4,16,768]{2,1,0:T(8,128)} %get-tuple-element.56) | copy-start | bytes 589828
  812.6 80.8 %collective-permute-start = (bf16[64,2048]{1,0:T(8,128)(2,1)}, bf16[64,2048]{1,0:T(8,128)(2,1)S(1)}, u32[]{:S(2)}, u32[]{:S(2)}) collective-permute-start(bf16[64,2048]{1,0:T(8,128)(2,1)} %get-tuple-element.107), channel_id=1, source_target_pairs={{0,0},{1,3},{2,2},{3,1},{4,4},{5,7},{6,6},{7,5},{8,8},{9,11},{10,1... | collective-permute-start | bytes 786440 | tf_op jit(solution)/shard_map/ppermute | solution.py:2922
  814.2 79.3 %collective-permute-start.1 = (bf16[64,2048]{1,0:T(8,128)(2,1)}, bf16[64,2048]{1,0:T(8,128)(2,1)S(1)}, u32[]{:S(2)}, u32[]{:S(2)}) collective-permute-start(bf16[64,2048]{1,0:T(8,128)(2,1)} %get-tuple-element.106), channel_id=1, source_target_pairs={{0,1},{1,0},{2,3},{3,2},{4,5},{5,4},{6,7},{7,6},{8,9},{9,8},{10,11... | collective-permute-start | bytes 786440 | tf_op jit(solution)/shard_map/ppermute | solution.py:2922
  817.4 76.2 %collective-permute-start.2 = (bf16[64,2048]{1,0:T(8,128)(2,1)S(1)}, bf16[64,2048]{1,0:T(8,128)(2,1)S(1)}, u32[]{:S(2)}, u32[]{:S(2)}) collective-permute-start(bf16[64,2048]{1,0:T(8,128)(2,1)S(1)} %get-tuple-element.105), channel_id=1, source_target_pairs={{0,2},{1,1},{2,0},{3,3},{4,6},{5,5},{6,4},{7,7},{8,10},{9,9},{10,8... | collective-permute-start | bytes 786440 | tf_op jit(solution)/shard_map/ppermute | solution.py:2922
  828.8 23.2 %copy-start = (bf16[1,3,256,2048]{3,2,1,0:T(8,128)(2,1)S(1)}, bf16[1,3,256,2048]{3,2,1,0:T(8,128)(2,1)}, u32[]{:S(2)}) copy-start(bf16[1,3,256,2048]{3,2,1,0:T(8,128)(2,1)} %get-tuple-element.104) | copy-start | bytes 9437188
  828.8 23.2 %copy-start.4 = (f32[768,64]{1,0:T(8,128)S(1)}, f32[768,64]{1,0:T(8,128)}, u32[]{:S(2)}) copy-start(f32[768,64]{1,0:T(8,128)} %convolution_multiply_fusion.pre_grad_ref) | copy-start | bytes 589828
  851.0 3.6 copy-start.9
  882.2 6.8 copy-start.1
  893.6 14.6 %copy-start.2 = (bf16[3,64,2048]{2,1,0:T(8,128)(2,1)}, bf16[3,64,2048]{2,1,0:T(8,128)(2,1)S(1)}, u32[]{:S(2)}) copy-start(bf16[3,64,2048]{2,1,0:T(8,128)(2,1)S(1)} %bitcast_dynamic-update-slice_fusion) | copy-start | bytes 2359300
Sparse Core Ops, SparseCore 0:
  809.8 92.4 all-gather.1

commit v6 on v5

--- a/solution.py
+++ b/solution.py
@@ -2049,7 +2049,7 @@
     full_ref,
     down_all_ref,
     up_all_ref,
-    inner_ref,
+    inner_columns,
     quarter_ref,
     branch_ref,
     gain_grad_ref,
@@ -2077,7 +2077,6 @@
     back_buf,
     x_buf,
     stage,
-    inner_columns,
     scatter_send,
     scatter_recv,
     sum_send,
@@ -2092,8 +2091,6 @@
     swap_recv,
     local_sem,
     inner_sem,
-    share_send,
-    share_recv,
     *,
     micro_count,
     sequence_length,
@@ -2567,30 +2564,6 @@
     swapped_in(attn_swap)
     value_spread.service(3)
     value_spread.placed()
-    inner_products(3)
-
-    def share_copy(source_place, target_place):
-        return pltpu.make_async_remote_copy(
-            src_ref=inner_ref.at[source_place],
-            dst_ref=inner_ref.at[source_place],
-            send_sem=share_send.at[target_place],
-            recv_sem=share_recv.at[source_place],
-            device_id=z_place(target_place),
-            device_id_type=DEVICE_MESH,
-        )
-
-    for place in range(4):
-
-        @pl.when(plane == place)
-        def _():
-            others = [p for p in range(4) if p != place]
-            inner_ref[place] = jnp.transpose(inner_columns[...])[:16]
-            for p in others:
-                share_copy(place, p).start()
-            for p in others:
-                share_copy(p, place).wait_recv()
-            for p in others:
-                share_copy(place, p).wait_send()
 
     for spreading in (
         down_spread,
@@ -2666,7 +2639,7 @@
             shape((12 * rows, features), low_type),
             shape((ff_share, features), low_type),
             shape((4 * quarter, 8 * ff_share), low_type),
-            shape((4, 16, 4 * rows), jnp.float32),
+            shape((4 * rows, 128), jnp.float32),
             shape(piece, low_type),
             shape(block, low_type),
             shape((8, features), jnp.float32),
@@ -2696,7 +2669,6 @@
             some(*block),
             pltpu.VMEM(block, jnp.float32),
             some(*piece),
-            pltpu.VMEM((4 * rows, 128), jnp.float32),
             dma((4, 10)),
             dma((4, 10)),
             dma((3, 6)),
@@ -2711,8 +2683,6 @@
             dma((16,)),
             dma((8,)),
             dma((10,)),
-            dma((4,)),
-            dma((4,)),
         ],
         compiler_params=pltpu.CompilerParams(
             collective_id=6, has_side_effects=True, vmem_limit_bytes=63 * 1024 * 1024
@@ -2746,6 +2716,137 @@
     )
 
 
+def last_products_kernel(
+    columns_ref,
+    full_ref,
+    history_ref,
+    inner_ref,
+    inner_columns,
+    big,
+    inner_sem,
+    share_send,
+    share_recv,
+):
+    plane = lax.axis_index("hist")
+    inner_columns[...] = columns_ref[...]
+
+    def barrier_line(plane):
+        barrier = pltpu.get_barrier_semaphore()
+        for place in range(4):
+
+            @pl.when(plane == place)
+            def _():
+                for p in range(4):
+                    if p != place:
+                        pl.semaphore_signal(
+                            barrier, inc=1, device_id=z_place(p), device_id_type=DEVICE_MESH
+                        )
+
+        pl.semaphore_wait(barrier, 3)
+
+    rows = full_ref.shape[0] // 12
+    step_rows = rows // 2
+
+    def inner_loads(item, i):
+        source = full_ref
+        first = (item - 1) * 4 * rows
+        base = (i % 2) * 5 * step_rows
+        copies = [
+            pltpu.make_async_copy(
+                source.at[pl.ds(first + i * step_rows, step_rows)],
+                big.at[pl.ds(base + 4 * step_rows, step_rows)],
+                inner_sem.at[(i % 2) * 5 + 4],
+            )
+        ] + [
+            pltpu.make_async_copy(
+                history_ref.at[pl.ds(slot * 4 * rows + i * step_rows, step_rows)],
+                big.at[pl.ds(base + slot * step_rows, step_rows)],
+                inner_sem.at[(i % 2) * 5 + slot],
+            )
+            for slot in range(4)
+        ]
+        for copy in copies:
+            copy.start()
+        return copies
+
+    def inner_products(item):
+        loads = [inner_loads(item, 0)]
+        for i in range(8):
+            if i + 1 < 8:
+                loads.append(inner_loads(item, i + 1))
+            for copy in loads[i]:
+                copy.wait()
+            base = (i % 2) * 5 * step_rows
+
+            def some_rows(r, carry):
+                grad = big[
+                    pl.ds(pl.multiple_of(base + 4 * step_rows + r * 16, 16), 16), :
+                ].astype(jnp.float32)
+                for slot in range(4):
+                    values = big[
+                        pl.ds(pl.multiple_of(base + slot * step_rows + r * 16, 16), 16), :
+                    ].astype(jnp.float32)
+                    one = item * 4 + slot
+                    inner_columns[
+                        pl.ds(pl.multiple_of(i * step_rows + r * 16, 16), 16), one : one + 1
+                    ] = jnp.sum(grad * values, axis=-1, keepdims=True)
+                return carry
+
+            lax.fori_loop(0, step_rows // 16, some_rows, 0)
+
+    barrier_line(plane)
+    inner_products(3)
+
+    def share_copy(source_place, target_place):
+        return pltpu.make_async_remote_copy(
+            src_ref=inner_ref.at[source_place],
+            dst_ref=inner_ref.at[source_place],
+            send_sem=share_send.at[target_place],
+            recv_sem=share_recv.at[source_place],
+            device_id=z_place(target_place),
+            device_id_type=DEVICE_MESH,
+        )
+
+    for place in range(4):
+
+        @pl.when(plane == place)
+        def _():
+            others = [p for p in range(4) if p != place]
+            inner_ref[place] = jnp.transpose(inner_columns[...])[:16]
+            for p in others:
+                share_copy(place, p).start()
+            for p in others:
+                share_copy(p, place).wait_recv()
+            for p in others:
+                share_copy(place, p).wait_send()
+
+
+def last_products(columns, full, history):
+    rows, features = full.shape[0] // 12, full.shape[1]
+    anywhere = pl.BlockSpec(memory_space=pl.ANY)
+    near = pl.BlockSpec(memory_space=pltpu.VMEM)
+    dma = pltpu.SemaphoreType.DMA
+    return pl.pallas_call(
+        last_products_kernel,
+        in_specs=[near, anywhere, anywhere],
+        out_specs=near,
+        out_shape=jax.ShapeDtypeStruct((4, 16, 4 * rows), jnp.float32),
+        scratch_shapes=[
+            pltpu.VMEM((4 * rows, 128), jnp.float32),
+            pltpu.VMEM((5 * rows, features), jnp.bfloat16),
+            dma((10,)),
+            dma((4,)),
+            dma((4,)),
+        ],
+        compiler_params=pltpu.CompilerParams(
+            collective_id=8, has_side_effects=True, vmem_limit_bytes=56 * 1024 * 1024
+        ),
+        cost_estimate=pl.CostEstimate(
+            flops=0, bytes_accessed=40 * 1000 * 1000, transcendentals=0
+        ),
+    )(columns, full, history)
+
+
 def rotary_table(row_positions, head_dim):
     half_dim = head_dim // 2
     frequency = jnp.exp(
@@ -2816,6 +2917,7 @@
     latest_rows = lax.dynamic_index_in_dim(
         history, newest_output % local_slots, 0, keepdims=False
     ).reshape(all_rows, features)
+    latest_rows = lax.optimization_barrier(latest_rows)
     own_table = lax.dynamic_slice_in_dim(layer_lookup, plane * local_slots, local_slots, 0)
     ordered = jnp.eye(STREAM_COUNT, dtype=jnp.float32)[:, jnp.array(order)]
     select = jnp.einsum("ci,sj->cjis", ordered, own_table).reshape(
@@ -2881,7 +2983,7 @@
         full,
         down_all,
         up_all,
-        inner_all,
+        inner_columns,
         attn_quarter,
         branch,
         gain_sums,
@@ -2924,6 +3026,9 @@
         which = lax.div(source * micro_count + i, planes)
         block_out = lax.dynamic_update_index_in_dim(block_out, piece, which, 0)
 
+    inner_all = last_products(
+        inner_columns, full, history.reshape(local_slots * all_rows, features)
+    )
     mixer_output_wide = (
         packed[:, share : share + mix_rows, :mix_width]
         .reshape(mix_width, mix_width)
@@ -2960,29 +3065,27 @@
     )
     history_grad = history_grad.reshape(history.shape)
 
-    small_top = jnp.concatenate(
+    gain_rows = jnp.stack(
+        [gain_zero[0] * on_root, gain_sums[1], gain_sums[2], gain_sums[3], gain_sum3[0]]
+    )
+    counts = (share * mix_width // 128, 5 * share // 128, mix_rows * mix_width // 128)
+    dense = jnp.concatenate(
         [
-            mix_in_grad * on_root,
-            jnp.stack(
-                [gain_zero[0] * on_root, gain_sums[1], gain_sums[2], gain_sums[3], gain_sum3[0]]
-            ).T,
-            jnp.zeros((features, 128 - mix_width - 5), jnp.float32),
+            (mix_in_grad * on_root).reshape(columns, counts[0], 128),
+            gain_rows.reshape(5, columns, share).transpose(1, 0, 2).reshape(columns, counts[1], 128),
+            mix_out_grad.reshape(columns, counts[2], 128),
         ],
         axis=1,
-    ).reshape(columns, share, 128)
-    small_bottom = jnp.pad(
-        mix_out_grad.reshape(columns, mix_rows, mix_width),
-        ((0, 0), (0, 16 - mix_rows), (0, 128 - mix_width)),
-    )
-    small = small_sums(low(jnp.concatenate([small_top, small_bottom], axis=1)))
-
+    )
+    used = sum(counts)
+    small = small_sums(low(jnp.pad(dense, ((0, 0), (0, -used % 16), (0, 0)))))
     w_attn_grad, w_out_grad = lay_out(attn_every)
     return (
         block_out,
         history_grad,
-        small[:share, mix_width : mix_width + 5].T,
-        small[:share, :mix_width],
-        small[share : share + mix_rows, :mix_width],
+        small[counts[0] : counts[0] + counts[1]].reshape(5, share),
+        small[: counts[0]].reshape(share, mix_width),
+        small[counts[0] + counts[1] : used].reshape(mix_rows, mix_width),
         w_attn_grad,
         w_out_grad,
         up_all.astype(jnp.float32),

time: 925 us -> 921 us (level)
    pallas_call x0 -> x1, Pallas kernels: none -> 27.9 us  [last_products(): pl.pallas_call(last_products_kernel, in_specs=[near, anywhere, anywhere],...]
    pallas_call x1, Pallas kernels: 419 us -> 403 us  [attend_and_back(): pl.pallas_call(functools.partial(backward_kernel, micro_count=micro_count...]
  transfers between devices with their start and end apart: 4 -> 4, of which waited for: 1 -> 0; matrix products, arithmetic and copies ran while one was open for 4% -> 4% of each run, Pallas kernels for 5% -> 7%
where the time goes in v6:
time: 921 us; the launch traced here: 912 us
  Pallas kernels  842 us (91%)
  other arithmetic  21.5 us (2%)
  local copies, waits for them, and re-layouts  17.5 us (2%)
  between operations  17.2 us (2%)
    pallas_call x1, Pallas kernels, attend_and_back(): pl.pallas_call(functools.partial(backward_kernel, micro_count=micro_count...  403 us
    pallas_call x1, Pallas kernels, forward_and_feed(): pl.pallas_call(functools.partial(forward_kernel, micro_count=micro_count,...  366 us
    pallas_call x1, Pallas kernels, last_products(): pl.pallas_call(last_products_kernel, in_specs=[near, anywhere, anywhere],...  27.9 us
    pallas_call x1, Pallas kernels, slot_grads_of(): pl.pallas_call(slot_grad_kernel, grid=(total // step,), in_specs=[pl.Bloc...  22.2 us
  transfers between devices with their start and end apart: 4, of which 0 were waited for; matrix products, arithmetic and copies ran while one was open for 4% of the time, Pallas kernels for 7%

profile of v6, /device:TPU:0, one launch (start us, length us, event | category | flops | bytes accessed | tf_op | source)
XLA Modules:
  0.0 911.7 jit_solution(4527246615546491574)
XLA Ops:
  7.3 1.3 fusion.137
  11.2 4.0 constant_dynamic-slice_fusion
  16.7 0.7 pad_maximum_fusion.cos_ref
  18.2 0.7 pad_maximum_fusion.1.sin_ref
  20.2 365.6 %shard_map.187 = (bf16[8,288,128]{2,1,0:T(8,128)(2,1)}, f32[8,2048]{1,0:T(8,128)}, f32[768,128]{1,0:T(8,128)}, f32[768,128]{1,0:T(8,128)}, f32[4,192,2048]{2,1,0...) custom-call(s32[3]{0:T(128)} %length_ref.1, ...), custom_call_target="tpu_custom_call" | custom-call | flops 38654705664 | bytes 600000000 | tf_op jit(solution)/shard_map/pallas_call | solution.py:1687
  385.8 0.7 convert_reduce_fusion.1
  387.2 403.2 %shard_map.188 = (bf16[2304,2048]{1,0:T(8,128)(2,1)}, bf16[1024,2048]{1,0:T(8,128)(2,1)}, bf16[256,8192]{1,0:T(8,128)(2,1)}, f32[768,128]{1,0:T(8,128)}, bf16[25...) custom-call(s32[24]{0:T(128)} %reshape.150.length_ref, ...), custom_call_target="tpu_custom_call" | custom-call | flops 16106127360 | bytes 1000000000 | tf_op jit(solution)/shard_map/pallas_call | solution.py:2626
  790.5 1.9 fusion.14
  792.4 0.9 fusion.169
  793.3 1.6 collective-permute-start
  794.9 3.0 collective-permute-start.1
  798.0 1.9 collective-permute-start.2
  800.0 0.8 slice.58
  800.9 27.9 %shard_map.189 = f32[4,16,768]{2,1,0:T(8,128)} custom-call(f32[768,128]{1,0:T(8,128)} %get-tuple-element.56.columns_ref, bf16[2304,2048]{1,0:T(8,128)(2,1)} %get-tuple-element.55.full_ref, bf16[3072,2048]{1,0:T(8,128)(2,1)} %bitcast.63), custom_call_target="tpu_custom_call" | custom-call | bytes 40000000 | tf_op jit(solution)/shard_map/pallas_call | solution.py:2829
  828.7 1.0 reshape.140
  829.8 1.1 copy.61
  830.9 1.2 compare_convert_fusion.flag_ref
  832.8 2.2 convolution_multiply_fusion.pre_grad_ref
  835.1 22.2 %shard_map.190 = (bf16[4,768,2048]{2,1,0:T(8,128)(2,1)}, f32[8,2048]{1,0:T(8,128)}) custom-call(f32[4]{0:T(128)} %compare_convert_fusion.flag_ref, f32[768,128]{1,0:T(8,128)} %get-tuple-element.54.factor_ref, bf16[768,2048]{1,0:T(8,128)(2,1)} %get-tuple-element.51.full3_ref.first_ref, bf16[3,768,2048]{2,1,0:T(8,128)(2,1)} %bitcast.64, ...), custom_call_target="tpu_custom_call" | custom-call | flops 62914560 | bytes 31457280 | tf_op jit(solution)/shard_map/pallas_call | solution.py:1902
  857.3 0.9 convert_reduce_fusion
  858.9 1.5 fusion.15
  860.5 2.2 fusion.10
  862.7 0.9 fusion.130
  864.1 0.8 slice.88
  865.1 0.7 fusion.83.parts_ref
  865.9 16.8 %shard_map.191 = f32[144,128]{1,0:T(8,128)} custom-call(bf16[8,144,128]{2,1,0:T(8,128)(2,1)} %fusion.83.parts_ref), custom_call_target="tpu_custom_call" | custom-call | bytes 40000000 | tf_op jit(solution)/shard_map/pallas_call | solution.py:1837
  882.7 0.8 slice.63
  883.5 0.7 slice.62
  885.0 0.7 copy.56
  887.0 6.7 convert_element_type.81
  893.7 4.4 convert_element_type.82
  898.4 6.2 shard_map.192
  (76 shorter events, 8.7 us)
Async XLA Ops:
  7.2 8.2 copy-start.11
  7.2 8.0 copy-start.10
  7.2 10.2 %copy-start.5 = (bf16[256,64]{0,1:T(8,128)(2,1)S(1)}, bf16[256,64]{0,1:T(8,128)(2,1)}, u32[]{:S(2)}) copy-start(bf16[256,64]{0,1:T(8,128)(2,1)} %param.16) | copy-start | bytes 98308
  7.2 10.3 %copy-start.6 = (bf16[5,256]{1,0:T(8,128)(2,1)S(1)}, bf16[5,256]{1,0:T(8,128)(2,1)}, u32[]{:S(2)}) copy-start(bf16[5,256]{1,0:T(8,128)(2,1)} %param.15) | copy-start | bytes 7684
  7.2 10.3 %copy-start.8 = (s32[3]{0:T(128)S(1)}, s32[3]{0:T(128)}, u32[]{:S(2)}) copy-start(s32[3]{0:T(128)} %length_ref.1) | copy-start | bytes 40
  7.2 11.7 %copy-start.7 = (bf16[8,64]{1,0:T(8,128)(2,1)S(1)}, bf16[8,64]{1,0:T(8,128)(2,1)}, u32[]{:S(2)}) copy-start(bf16[8,64]{1,0:T(8,128)(2,1)} %param.17) | copy-start | bytes 3076
  7.2 891.2 %all-gather.2.cloned.1.call-start = ((), (), s32[]{:S(2)}) async-start(), calls=%async_computation | async-start | bytes 5242880 | tf_op jit(solution)/shard_map/all_gather | solution.py:3016
  387.2 403.3 %copy-start.9 = (s32[3]{0:T(128)S(1)}, s32[3]{0:T(128)}, u32[]{:S(2)}) copy-start(s32[3]{0:T(128)} %length_ref.1) | copy-start | bytes 40
  790.4 10.4 %copy-start.3 = (bf16[8,288,128]{2,1,0:T(8,128)(2,1)S(1)}, bf16[8,288,128]{2,1,0:T(8,128)(2,1)}, u32[]{:S(2)}) copy-start(bf16[8,288,128]{2,1,0:T(8,128)(2,1)} %get-tuple-element.39) | copy-start | bytes 1769476
  793.3 104.8 %collective-permute-start = (bf16[64,2048]{1,0:T(8,128)(2,1)}, bf16[64,2048]{1,0:T(8,128)(2,1)S(1)}, u32[]{:S(2)}, u32[]{:S(2)}) collective-permute-start(bf16[64,2048]{1,0:T(8,128)(2,1)} %get-tuple-element.105), channel_id=1, source_target_pairs={{0,0},{1,3},{2,2},{3,1},{4,4},{5,7},{6,6},{7,5},{8,8},{9,11},{10,1... | collective-permute-start | bytes 786440 | tf_op jit(solution)/shard_map/ppermute | solution.py:3024
  794.9 103.4 %collective-permute-start.1 = (bf16[64,2048]{1,0:T(8,128)(2,1)}, bf16[64,2048]{1,0:T(8,128)(2,1)S(1)}, u32[]{:S(2)}, u32[]{:S(2)}) collective-permute-start(bf16[64,2048]{1,0:T(8,128)(2,1)} %get-tuple-element.104), channel_id=1, source_target_pairs={{0,1},{1,0},{2,3},{3,2},{4,5},{5,4},{6,7},{7,6},{8,9},{9,8},{10,11... | collective-permute-start | bytes 786440 | tf_op jit(solution)/shard_map/ppermute | solution.py:3024
  798.0 100.4 %collective-permute-start.2 = (bf16[64,2048]{1,0:T(8,128)(2,1)S(1)}, bf16[64,2048]{1,0:T(8,128)(2,1)S(1)}, u32[]{:S(2)}, u32[]{:S(2)}) collective-permute-start(bf16[64,2048]{1,0:T(8,128)(2,1)S(1)} %get-tuple-element.103), channel_id=1, source_target_pairs={{0,2},{1,1},{2,0},{3,3},{4,6},{5,5},{6,4},{7,7},{8,10},{9,9},{10,8... | collective-permute-start | bytes 786440 | tf_op jit(solution)/shard_map/ppermute | solution.py:3024
  835.1 23.1 %copy-start = (bf16[1,3,256,2048]{3,2,1,0:T(8,128)(2,1)S(1)}, bf16[1,3,256,2048]{3,2,1,0:T(8,128)(2,1)}, u32[]{:S(2)}) copy-start(bf16[1,3,256,2048]{3,2,1,0:T(8,128)(2,1)} %constant_dynamic-slice_fusion) | copy-start | bytes 9437188
  835.1 23.8 %copy-start.12 = (f32[768,128]{1,0:T(8,128)S(1)}, f32[768,128]{1,0:T(8,128)}, u32[]{:S(2)}) copy-start(f32[768,128]{1,0:T(8,128)} %get-tuple-element.57) | copy-start | bytes 1179652
  858.9 1.6 copy-start.4
  887.0 6.7 copy-start.1
  898.4 6.2 copy-start.2
Sparse Core Ops, SparseCore 0:
  790.5 94.1 all-gather.1

commit v7 on v6

--- a/solution.py
+++ b/solution.py
@@ -2049,6 +2049,8 @@
     full_ref,
     down_all_ref,
     up_all_ref,
+    down_wide_ref,
+    up_wide_ref,
     inner_columns,
     quarter_ref,
     branch_ref,
@@ -2091,6 +2093,7 @@
     swap_recv,
     local_sem,
     inner_sem,
+    wide_sem,
     *,
     micro_count,
     sequence_length,
@@ -2312,6 +2315,50 @@
                 return carry
 
             lax.fori_loop(0, step_rows // 16, some_rows, 0)
+
+    def widen(kind):
+        if kind == 0:
+            pieces = [(down_all_ref, down_wide_ref, i * 64, 0) for i in range(ff_share // 64)]
+        else:
+            pieces = [
+                (up_all_ref, up_wide_ref, i * 64, c * features)
+                for i in range(4 * quarter // 64)
+                for c in range(8 * ff_share // features)
+            ]
+        low_at = lambda n: big.at[pl.ds(64 * (n % 3), 64)]
+        wide_at = lambda n: x_buf.at[pl.ds(64 * (n % 3), 64)]
+
+        def load(n):
+            source, _, row, lane = pieces[n]
+            return pltpu.make_async_copy(
+                source.at[pl.ds(row, 64), pl.ds(lane, features)], low_at(n), wide_sem.at[n % 3]
+            )
+
+        def store(n):
+            _, target, row, lane = pieces[n]
+            return pltpu.make_async_copy(
+                wide_at(n), target.at[pl.ds(row, 64), pl.ds(lane, features)], wide_sem.at[3 + n % 3]
+            )
+
+        load(0).start()
+        load(1).start()
+        for n in range(len(pieces)):
+            if n + 2 < len(pieces):
+                load(n + 2).start()
+            load(n).wait()
+            if n >= 3:
+                store(n - 3).wait()
+
+            def some_rows(r, carry):
+                x_buf[pl.ds(pl.multiple_of(64 * (n % 3) + r * 16, 16), 16), :] = big[
+                    pl.ds(pl.multiple_of(64 * (n % 3) + r * 16, 16), 16), :
+                ].astype(jnp.float32)
+                return carry
+
+            lax.fori_loop(0, 4, some_rows, 0)
+            store(n).start()
+        for n in range(len(pieces) - 3, len(pieces)):
+            store(n).wait()
 
     def part_copies(first_row):
         return [
@@ -2551,6 +2598,8 @@
     query_spread.placed()
     inner_products(0)
     inner_products(1)
+    down_spread.placed()
+    widen(0)
     up_spread.service(3)
     attn_line.service(2)
     attn_line.finish(attn_sum)
@@ -2559,9 +2608,9 @@
     value_spread.service(2)
     key_spread.placed()
     inner_products(2)
-    down_spread.placed()
     up_spread.placed()
     swapped_in(attn_swap)
+    widen(1)
     value_spread.service(3)
     value_spread.placed()
 
@@ -2634,11 +2683,13 @@
         + [anywhere]
         + [near] * 2
         + [anywhere] * 4,
-        out_specs=[anywhere] * 3 + [near, near, near, near, anywhere, anywhere],
+        out_specs=[anywhere] * 5 + [near, near, near, near, anywhere, anywhere],
         out_shape=[
             shape((12 * rows, features), low_type),
             shape((ff_share, features), low_type),
             shape((4 * quarter, 8 * ff_share), low_type),
+            shape((ff_share, features), jnp.float32),
+            shape((4 * quarter, 8 * ff_share), jnp.float32),
             shape((4 * rows, 128), jnp.float32),
             shape(piece, low_type),
             shape(block, low_type),
@@ -2683,6 +2734,7 @@
             dma((16,)),
             dma((8,)),
             dma((10,)),
+            dma((6,)),
         ],
         compiler_params=pltpu.CompilerParams(
             collective_id=6, has_side_effects=True, vmem_limit_bytes=63 * 1024 * 1024
@@ -2981,8 +3033,10 @@
     lengths_all = packed[:, share + 8, :micro_count].reshape(-1).astype(jnp.int32)
     (
         full,
-        down_all,
-        up_all,
+        _,
+        _,
+        w_down_grad,
+        w_up_grad,
         inner_columns,
         attn_quarter,
         branch,
@@ -3088,8 +3142,8 @@
         small[counts[0] + counts[1] : used].reshape(mix_rows, mix_width),
         w_attn_grad,
         w_out_grad,
-        up_all.astype(jnp.float32),
-        down_all.astype(jnp.float32),
+        w_up_grad,
+        w_down_grad,
     )
 
 

time: 921 us -> 927 us (level)
  other arithmetic: 21.5 us -> 10.3 us
  local copies, waits for them, and re-layouts: 17.5 us -> 28.7 us
    unnamed x29 -> x33, local copies, waits for them, and re-layouts: 0.89 us -> 12.1 us
    convert_element_type x2 -> x0, other arithmetic: 11.2 us -> none  [the longest x1 6.73 us: shards_split(): up_all.astype(jnp.float32)]
  transfers between devices with their start and end apart: 4 -> 4, of which waited for: 0 -> 0; matrix products, arithmetic and copies ran while one was open for 4% -> 3% of each run, Pallas kernels for 7% -> 7%
where the time goes in v7:
time: 927 us; the launch traced here: 917 us
  Pallas kernels  849 us (92%)
  local copies, waits for them, and re-layouts  28.7 us (3%)
  between operations  17.3 us (2%)
  other arithmetic  10.3 us (1%)
    pallas_call x1, Pallas kernels, attend_and_back(): pl.pallas_call(functools.partial(backward_kernel, micro_count=micro_count...  408 us
    pallas_call x1, Pallas kernels, forward_and_feed(): pl.pallas_call(functools.partial(forward_kernel, micro_count=micro_count,...  366 us
    pallas_call x1, Pallas kernels, last_products(): pl.pallas_call(last_products_kernel, in_specs=[near, anywhere, anywhere],...  28.1 us
    pallas_call x1, Pallas kernels, slot_grads_of(): pl.pallas_call(slot_grad_kernel, grid=(total // step,), in_specs=[pl.Bloc...  22.2 us
  transfers between devices with their start and end apart: 4, of which 0 were waited for; matrix products, arithmetic and copies ran while one was open for 3% of the time, Pallas kernels for 7%

profile of v7, /device:TPU:0, one launch (start us, length us, event | category | flops | bytes accessed | tf_op | source)
XLA Modules:
  0.0 917.3 jit_solution(12812826647838709012)
XLA Ops:
  7.3 1.3 fusion.137
  11.2 4.0 constant_dynamic-slice_fusion
  16.7 0.7 pad_maximum_fusion.cos_ref
  18.2 0.7 pad_maximum_fusion.1.sin_ref
  20.2 365.6 %shard_map.187 = (bf16[8,288,128]{2,1,0:T(8,128)(2,1)}, f32[8,2048]{1,0:T(8,128)}, f32[768,128]{1,0:T(8,128)}, f32[768,128]{1,0:T(8,128)}, f32[4,192,2048]{2,1,0...) custom-call(s32[3]{0:T(128)} %length_ref.1, ...), custom_call_target="tpu_custom_call" | custom-call | flops 38654705664 | bytes 600000000 | tf_op jit(solution)/shard_map/pallas_call | solution.py:1687
  385.8 0.7 convert_reduce_fusion.1
  387.2 408.0 %shard_map.188 = (bf16[2304,2048]{1,0:T(8,128)(2,1)}, bf16[1024,2048]{1,0:T(8,128)(2,1)}, bf16[256,8192]{1,0:T(8,128)(2,1)}, f32[1024,2048]{1,0:T(8,128)}, f32[2...) custom-call(s32[24]{0:T(128)} %reshape.150.length_ref, ...), custom_call_target="tpu_custom_call" | custom-call | flops 16106127360 | bytes 1000000000 | tf_op jit(solution)/shard_map/pallas_call | solution.py:2675
  795.3 1.9 fusion.14
  797.2 0.9 fusion.169
  798.1 1.6 collective-permute-start
  799.7 1.5 collective-permute-start.1
  801.3 1.9 collective-permute-start.2
  803.3 0.8 slice.58
  804.1 28.1 %shard_map.189 = f32[4,16,768]{2,1,0:T(8,128)} custom-call(f32[768,128]{1,0:T(8,128)} %get-tuple-element.56.columns_ref, bf16[2304,2048]{1,0:T(8,128)(2,1)} %get-tuple-element.55.full_ref, bf16[3072,2048]{1,0:T(8,128)(2,1)} %bitcast.63), custom_call_target="tpu_custom_call" | custom-call | bytes 40000000 | tf_op jit(solution)/shard_map/pallas_call | solution.py:2881
  832.2 1.0 reshape.140
  833.3 1.1 copy.61
  834.4 1.2 compare_convert_fusion.flag_ref
  836.3 2.2 convolution_multiply_fusion.pre_grad_ref
  838.6 22.2 %shard_map.190 = (bf16[4,768,2048]{2,1,0:T(8,128)(2,1)}, f32[8,2048]{1,0:T(8,128)}) custom-call(f32[4]{0:T(128)} %compare_convert_fusion.flag_ref, f32[768,128]{1,0:T(8,128)} %get-tuple-element.54.factor_ref, bf16[768,2048]{1,0:T(8,128)(2,1)} %get-tuple-element.51.full3_ref.first_ref, bf16[3,768,2048]{2,1,0:T(8,128)(2,1)} %bitcast.64, ...), custom_call_target="tpu_custom_call" | custom-call | flops 62914560 | bytes 31457280 | tf_op jit(solution)/shard_map/pallas_call | solution.py:1902
  860.8 0.9 convert_reduce_fusion
  862.4 1.5 fusion.15
  864.0 2.2 fusion.10
  866.2 0.9 fusion.130
  867.6 0.8 slice.88
  868.6 0.7 fusion.83.parts_ref
  869.4 18.1 %shard_map.191 = f32[144,128]{1,0:T(8,128)} custom-call(bf16[8,144,128]{2,1,0:T(8,128)(2,1)} %fusion.83.parts_ref), custom_call_target="tpu_custom_call" | custom-call | bytes 40000000 | tf_op jit(solution)/shard_map/pallas_call | solution.py:1837
  887.5 0.8 slice.63
  888.4 0.7 slice.62
  889.8 0.7 copy.56
  892.1 7.0 shard_map.192
  899.0 7.8 copy.74
  906.9 3.4 copy.75
  (79 shorter events, 8.7 us)
Async XLA Ops:
  7.2 8.2 copy-start.10
  7.2 8.0 copy-start.9
  7.2 10.2 %copy-start.4 = (bf16[256,64]{0,1:T(8,128)(2,1)S(1)}, bf16[256,64]{0,1:T(8,128)(2,1)}, u32[]{:S(2)}) copy-start(bf16[256,64]{0,1:T(8,128)(2,1)} %param.16) | copy-start | bytes 98308
  7.2 10.3 %copy-start.5 = (bf16[5,256]{1,0:T(8,128)(2,1)S(1)}, bf16[5,256]{1,0:T(8,128)(2,1)}, u32[]{:S(2)}) copy-start(bf16[5,256]{1,0:T(8,128)(2,1)} %param.15) | copy-start | bytes 7684
  7.2 10.3 %copy-start.7 = (s32[3]{0:T(128)S(1)}, s32[3]{0:T(128)}, u32[]{:S(2)}) copy-start(s32[3]{0:T(128)} %length_ref.1) | copy-start | bytes 40
  7.2 11.7 %copy-start.6 = (bf16[8,64]{1,0:T(8,128)(2,1)S(1)}, bf16[8,64]{1,0:T(8,128)(2,1)}, u32[]{:S(2)}) copy-start(bf16[8,64]{1,0:T(8,128)(2,1)} %param.17) | copy-start | bytes 3076
  7.2 884.8 %all-gather.2.cloned.1.call-start = ((), (), s32[]{:S(2)}) async-start(), calls=%async_computation | async-start | bytes 5242880 | tf_op jit(solution)/shard_map/all_gather | solution.py:3070
  387.2 408.1 %copy-start.8 = (s32[3]{0:T(128)S(1)}, s32[3]{0:T(128)}, u32[]{:S(2)}) copy-start(s32[3]{0:T(128)} %length_ref.1) | copy-start | bytes 40
  795.2 8.9 copy-start.2
  798.1 93.7 %collective-permute-start = (bf16[64,2048]{1,0:T(8,128)(2,1)}, bf16[64,2048]{1,0:T(8,128)(2,1)S(1)}, u32[]{:S(2)}, u32[]{:S(2)}) collective-permute-start(bf16[64,2048]{1,0:T(8,128)(2,1)} %get-tuple-element.105), channel_id=1, source_target_pairs={{0,0},{1,3},{2,2},{3,1},{4,4},{5,7},{6,6},{7,5},{8,8},{9,11},{10,1... | collective-permute-start | bytes 786440 | tf_op jit(solution)/shard_map/ppermute | solution.py:3078
  799.7 92.2 %collective-permute-start.1 = (bf16[64,2048]{1,0:T(8,128)(2,1)}, bf16[64,2048]{1,0:T(8,128)(2,1)S(1)}, u32[]{:S(2)}, u32[]{:S(2)}) collective-permute-start(bf16[64,2048]{1,0:T(8,128)(2,1)} %get-tuple-element.104), channel_id=1, source_target_pairs={{0,1},{1,0},{2,3},{3,2},{4,5},{5,4},{6,7},{7,6},{8,9},{9,8},{10,11... | collective-permute-start | bytes 786440 | tf_op jit(solution)/shard_map/ppermute | solution.py:3078
  801.3 90.7 %collective-permute-start.2 = (bf16[64,2048]{1,0:T(8,128)(2,1)S(1)}, bf16[64,2048]{1,0:T(8,128)(2,1)S(1)}, u32[]{:S(2)}, u32[]{:S(2)}) collective-permute-start(bf16[64,2048]{1,0:T(8,128)(2,1)S(1)} %get-tuple-element.103), channel_id=1, source_target_pairs={{0,2},{1,1},{2,0},{3,3},{4,6},{5,5},{6,4},{7,7},{8,10},{9,9},{10,8... | collective-permute-start | bytes 786440 | tf_op jit(solution)/shard_map/ppermute | solution.py:3078
  838.6 23.1 %copy-start = (bf16[1,3,256,2048]{3,2,1,0:T(8,128)(2,1)S(1)}, bf16[1,3,256,2048]{3,2,1,0:T(8,128)(2,1)}, u32[]{:S(2)}) copy-start(bf16[1,3,256,2048]{3,2,1,0:T(8,128)(2,1)} %constant_dynamic-slice_fusion) | copy-start | bytes 9437188
  838.6 23.8 %copy-start.11 = (f32[768,128]{1,0:T(8,128)S(1)}, f32[768,128]{1,0:T(8,128)}, u32[]{:S(2)}) copy-start(f32[768,128]{1,0:T(8,128)} %get-tuple-element.57) | copy-start | bytes 1179652
  862.4 1.6 copy-start.3
  892.0 14.8 %copy-start.1 = (bf16[3,64,2048]{2,1,0:T(8,128)(2,1)}, bf16[3,64,2048]{2,1,0:T(8,128)(2,1)S(1)}, u32[]{:S(2)}) copy-start(bf16[3,64,2048]{2,1,0:T(8,128)(2,1)S(1)} %bitcast_dynamic-update-slice_fusion) | copy-start | bytes 2359300
  892.1 14.8 %slice-start = ((s8[8388608]{0:T(1024)(128)(4,1)}), s8[4194304]{0:T(1024)(128)(4,1)S(1)}, s32[]{:S(2)}) async-start(s8[8388608]{0:T(1024)(128)(4,1)} %bitcast.69), calls=%async_computation.1 | async-start | bytes 8388608
  899.0 7.8 slice-start.1
Sparse Core Ops, SparseCore 0:
  795.4 93.0 all-gather.1
